TPU v7x, 512 devices: a whole 4x8x8 slice. The times are simulated.
512 devices in a mesh: replica: 32 (over y, x_hi, core), shard: 16 (over x_lo, z).
Axes of the slice: x: 4 (x_hi: 2, x_lo: 2; x = x_hi * 2 + x_lo), y: 8, z: 8, core: 2. Of those that a mesh axis runs over, the one named last changes fastest.
Arguments:
- image: bfloat16 [512, 14, 14, 768], P(('replica', 'shard')), may hold values from -6 to 6
- upstream: bfloat16 [512, 14, 14, 768], P(('replica', 'shard')), may hold values from -0.75 to 0.75
- group_ids: int32 [512], P(('replica', 'shard')), may hold values from 0 to 3
- group_weights: float32 [4], replicated, may hold values from 0.2 to 5
- conv_kernel: bfloat16 [7, 7, 768], replicated, may hold values from -0.875 to 0.875
- norm_gain: float32 [768], replicated, may hold values from 0.1 to 1.9
- first_weight: bfloat16 [768, 3072], P(None, 'shard'), may hold values from -0.21875 to 0.21875
- first_bias: float32 [3072], P('shard'), may hold values from -3 to 3
- second_weight: bfloat16 [3072, 768], P('shard'), may hold values from -0.109375 to 0.109375
- layer_scale: float32 [768], replicated, may hold values from 0.3 to 3
Outputs:
- grad_input: bfloat16 [512, 14, 14, 768], P(('replica', 'shard'))
- grad_first: float32 [768, 3072], P(None, 'shard')
- grad_first_bias: float32 [3072], P('shard')
- grad_second: float32 [3072, 768], P('shard')
- grad_kernel: float32 [7, 7, 768], replicated
- grad_gain: float32 [768], replicated
- grad_scale: float32 [768], replicated
All inputs are finite; a program needn't handle non-finite values.
Results may differ from a plain program's by a relative error of at most 0.009.
Values may be sent and summed in bfloat16 or wider, within the bound.
No kernel may reach another device: no remote copies, remote signals or barrier semaphores. Data moves between devices by JAX's collectives and lax.ppermute only.
A program may use at most 128 MiB of HBM per device.

v0:
```python
import jax
import jax.numpy as jnp
from jax import lax
from jax.sharding import PartitionSpec as P


def depthwise(image_map, kernel):
    rows_map, cols_map = (image_map.shape[0], image_map.shape[1])
    padded = jnp.pad(image_map, ((3, 3), (3, 3), (0, 0)))
    output = jnp.zeros(image_map.shape, jnp.float32)
    for row_shift in range(7):
        for col_shift in range(7):
            output = (
                output
                + padded[row_shift : row_shift + rows_map, col_shift : col_shift + cols_map]
                * kernel[row_shift, col_shift]
            )
    return output


def depthwise_back(signal, image_map, kernel):
    rows_map, cols_map = (image_map.shape[0], image_map.shape[1])
    padded_grad = jnp.pad(signal, ((3, 3), (3, 3), (0, 0)))
    padded_map = jnp.pad(image_map, ((3, 3), (3, 3), (0, 0)))
    input_grad = jnp.zeros(image_map.shape, jnp.float32)
    kernel_rows = []
    for row_shift in range(7):
        for col_shift in range(7):
            input_grad = (
                input_grad
                + padded_grad[
                    6 - row_shift : 6 - row_shift + rows_map,
                    6 - col_shift : 6 - col_shift + cols_map,
                ]
                * kernel[row_shift, col_shift]
            )
            kernel_rows.append(
                jnp.sum(
                    signal
                    * padded_map[
                        row_shift : row_shift + rows_map, col_shift : col_shift + cols_map
                    ],
                    axis=(0, 1),
                )
            )
    kernel_grad = jnp.stack(kernel_rows).reshape(7, 7, image_map.shape[2])
    return (input_grad, kernel_grad)


def standardize(convolved):
    centred = convolved - jnp.mean(convolved, axis=-1, keepdims=True)
    inv_std = lax.rsqrt(jnp.mean(centred * centred, axis=-1, keepdims=True) + 1e-06)
    return (centred * inv_std, inv_std)


def gelu_value(value):
    return 0.5 * value * (1.0 + lax.erf(value * 0.7071067811865476))


def gelu_slope(value):
    return (
        0.5 * (1.0 + lax.erf(value * 0.7071067811865476))
        + value * jnp.exp(-0.5 * value * value) * 0.3989422804014327
    )


def contract_rows(left_side, right_side):
    return lax.dot_general(
        left_side, right_side, (((0,), (0,)), ((), ())), preferred_element_type=jnp.float32
    )


def contract_cols(left_side, right_side):
    return lax.dot_general(
        left_side, right_side, (((1,), (1,)), ((), ())), preferred_element_type=jnp.float32
    )


def per_device(
    image,
    upstream,
    group_ids,
    group_weights,
    conv_kernel,
    norm_gain,
    first_weight,
    first_bias,
    second_weight,
    layer_scale,
):
    rows_map, cols_map, channels = (image.shape[1], image.shape[2], image.shape[3])
    pixels = rows_map * cols_map
    shards = lax.axis_size("shard")
    images_all = lax.axis_size("replica") * shards
    kernel = conv_kernel.astype(jnp.float32)
    field_map = image[0].astype(jnp.float32)
    labels = jnp.arange(group_weights.shape[0], dtype=jnp.int32)
    own_weight = jnp.sum(jnp.where(labels == group_ids[0], group_weights, 0.0))
    scaled = (own_weight * upstream[0].reshape(pixels, channels).astype(jnp.float32)).astype(
        jnp.bfloat16
    )
    weight_sum = lax.psum(own_weight, ("replica", "shard"))
    grad_gathered = lax.all_gather(scaled, "shard", axis=0, tiled=True)
    convolved = depthwise(field_map, kernel).reshape(pixels, channels)
    centred, inv_std = standardize(convolved)
    normed = (centred * norm_gain).astype(jnp.bfloat16)
    normed_gathered = lax.all_gather(normed, "shard", axis=0, tiled=True)
    preact = jnp.dot(normed_gathered, first_weight, preferred_element_type=jnp.float32) + first_bias
    activation = gelu_value(preact).astype(jnp.bfloat16)
    branch_grad = (grad_gathered.astype(jnp.float32) * layer_scale).astype(jnp.bfloat16)
    branch = jnp.dot(activation, second_weight, preferred_element_type=jnp.float32)
    scale_part = jnp.sum(grad_gathered.astype(jnp.float32) * branch, axis=0)
    second_sum = contract_rows(activation, branch_grad)
    hidden_grad = contract_cols(branch_grad, second_weight)
    preact_grad = (hidden_grad * gelu_slope(preact)).astype(jnp.bfloat16)
    bias_sum = jnp.sum(preact_grad.astype(jnp.float32), axis=0)
    first_sum = contract_rows(normed_gathered, preact_grad)
    first_sum, bias_sum, second_sum = lax.psum((first_sum, bias_sum, second_sum), "replica")
    own_hidden = lax.all_to_all(preact_grad, "shard", split_axis=0, concat_axis=1, tiled=True)
    normed_grad = contract_cols(
        own_hidden, lax.all_gather(first_weight, "shard", axis=1, tiled=True)
    )
    gain_part = jnp.sum(normed_grad * centred, axis=0)
    gained = normed_grad * norm_gain
    conv_grad = inv_std * (
        gained
        - jnp.mean(gained, axis=-1, keepdims=True)
        - centred * jnp.mean(gained * centred, axis=-1, keepdims=True)
    )
    map_grad, kernel_part = depthwise_back(
        conv_grad.reshape(rows_map, cols_map, channels), field_map, kernel
    )
    members = (kernel_part, gain_part, scale_part) + ()
    summed = lax.psum(members, ("replica", "shard"))
    kernel_sum, gain_sum, scale_sum = (summed[0], summed[1], summed[2])
    factor = images_all / weight_sum
    grad_input = (
        factor * (scaled.astype(jnp.float32).reshape(rows_map, cols_map, channels) + map_grad)
    ).astype(jnp.bfloat16)
    return (
        grad_input.reshape(1, rows_map, cols_map, channels),
        factor * first_sum,
        factor * bias_sum,
        factor * second_sum,
        factor * kernel_sum,
        factor * gain_sum,
        factor * scale_sum,
    )


def solution(mesh):
    placed = (
        P(("replica", "shard"), None, None, None),
        P(("replica", "shard"), None, None, None),
        P(("replica", "shard")),
        P(),
        P(),
        P(),
        P(None, "shard"),
        P("shard"),
        P("shard", None),
        P(),
    )
    return jax.shard_map(
        per_device,
        mesh=mesh,
        in_specs=placed,
        out_specs=(
            P(("replica", "shard"), None, None, None),
            P(None, "shard"),
            P("shard"),
            P("shard", None),
            P(),
            P(),
            P(),
        ),
        check_vma=False,
    )
```

profile of v0, /device:TPU:1, one launch (start us, length us, event | category | flops | bytes accessed | tf_op | source)
XLA Modules:
  0.0 845.1 jit_solution(10145403940507758785)
XLA Ops:
  7.2 0.0 copy-start
  7.2 0.0 all-gather.10.cloned.1.call-start
  7.2 0.9 convert_element_type.68
  8.2 0.2 slice_reduce_fusion.48
  8.3 0.2 slice_reduce_fusion.47
  8.5 0.0 copy-start.7
  8.5 0.0 copy-start.9
  8.6 0.0 copy-start.51
  8.6 0.1 slice_reduce_fusion.46
  8.8 1.0 convert_bitcast_fusion
  9.9 0.0 copy-start.59
  9.9 0.0 copy-start.4
  9.9 5.5 fusion.108
  15.4 0.0 copy-done.9
  15.6 0.1 reshape.89
  15.7 0.2 multiply_reduce_fusion.49
  16.0 0.1 div.20
  16.0 0.0 copy-start.54
  16.1 0.1 rsqrt.12
  16.2 0.9 fusion.106
  17.1 0.0 all-gather.10.cloned.1.call-update
  17.1 0.0 all-gather.8.cloned.1.call-start
  17.8 0.7 fusion.107
  18.5 0.7 multiply_convert_fusion.4
  19.2 0.8 reshape.96
  20.0 0.0 all-gather.8.cloned.1.call-update
  20.1 0.0 all-gather.6.cloned.1.call-start
  20.1 0.7 all-gather.6.cloned.1.call-update
  20.8 76.8 %all-gather.10.cloned.1.call-done = bf16[16,196,768]{2,1,0:T(8,128)(2,1)} async-done(((bf16[1,196,768]{2,1,0:T(8,128)(2,1)}), bf16[16,196,768]{2,1,0:T(8,128)(2,1)}) %all-gather.10.cloned.1.call-update) | async-done | bytes 4816912 | tf_op jit(solution)/shard_map/all_gather | solution.py:107
  97.6 7.2 reshape.99
  104.8 73.6 %all-gather.8.cloned.1.call-done = bf16[16,196,768]{2,1,0:T(8,128)(2,1)} async-done(((bf16[1,196,768]{2,1,0:T(8,128)(2,1)}), bf16[16,196,768]{2,1,0:T(8,128)(2,1)}) %all-gather.8.cloned.1.call-update) | async-done | bytes 4816912 | tf_op jit(solution)/shard_map/all_gather | solution.py:103
  178.3 7.9 reshape.100
  186.2 4.2 convolution_add_fusion
  190.5 7.5 convert_reduce_fusion
  198.0 6.7 all_to_all.14
  204.7 3.1 copy.18
  207.8 4.4 all-to-all-start
  212.2 0.2 all-reduce.9.cloned.1.call-start
  212.4 1.9 reshape.95
  214.3 4.8 fusion.109
  219.1 6.0 fusion.5
  225.1 0.0 all-reduce.9.cloned.1.call-update
  225.1 0.0 all-reduce.7.cloned.1.call-start
  225.2 72.9 %psum.51 = f32[192]{0:T(256)} all-reduce(f32[192]{0:T(256)} %get-tuple-element.117), channel_id=1, replica_groups=mesh['replica'=32,'shard'=16] {'replica'}, use_global_device_ids=true, to_apply=%region_8.9 | all-reduce | flops 192 | bytes 1536 | tf_op jit(solution)/shard_map/psum | solution.py:118
  298.1 5.4 multiply_reduce_fusion
  303.6 4.4 multiply_reduce_fusion.50
  308.0 0.3 multiply_reduce_fusion.51
  308.3 0.1 reshape.90
  308.4 0.0 copy-start.10
  308.6 2.0 multiply_reduce_fusion.19
  310.6 1.7 multiply_reduce_fusion.1
  312.4 102.1 %all-reduce.2 = (f32[]{:T(128)}, f32[768]{0:T(1024)S(1)}, f32[768]{0:T(1024)S(1)}) all-reduce(f32[]{:T(128)} %fusion.107, f32[768]{0:T(1024)S(1)} %get-tuple-element.55, f32[768]{0:T(1024)S(1)} %copy-done.53), channel_id=1, replica_groups=mesh['replica'=32,'shard'=16] {'replica','shard'}, use_global_device_ids=true, to_apply=%region_1.2 | all-reduce | flops 1537 | bytes 12296 | tf_op jit(solution)/shard_map/psum | solution.py:102
  414.8 1.2 multiply_reduce_fusion.37
  416.2 0.3 stack.199
  416.5 0.7 reshape.92
  418.1 6.3 fusion.105
  424.4 0.0 all-reduce.7.cloned.1.call-update
  424.4 140.7 %all-reduce.9.cloned.1.call-done = (f32[768,192]{0,1:T(8,128)}, f32[192,768]{1,0:T(8,128)}) async-done(((f32[768,192]{0,1:T(8,128)}, f32[192,768]{1,0:T(8,128)}), (f32[768,192]{0,1:T(8,128)}, f32[192,768]{1,0:T(8,128)})) %all-reduce.9.cloned.1.call-update) | async-done | bytes 1179664 | tf_op jit(solution)/shard_map/psum | solution.py:118
  565.1 1.9 broadcast_multiply_fusion
  567.0 1.9 broadcast_multiply_fusion.1
  568.9 0.6 broadcast_multiply_fusion.4
  569.5 0.6 broadcast_multiply_fusion.6
  570.1 266.9 %all-reduce.7.cloned.1.call-done = f32[7,7,768]{2,1,0:T(8,128)} async-done(((f32[7,7,768]{2,1,0:T(8,128)}), f32[7,7,768]{2,1,0:T(8,128)}) %all-reduce.7.cloned.1.call-update) | async-done | bytes 150544 | tf_op jit(solution)/shard_map/psum | solution.py:134
  837.0 1.6 broadcast_multiply_fusion.2
  (165 shorter events, 0.5 us)
Async XLA Ops:
  7.2 183.3 %copy-start = (bf16[192,768]{1,0:T(8,128)(2,1)S(1)}, bf16[192,768]{1,0:T(8,128)(2,1)}, u32[]{:S(2)}) copy-start(bf16[192,768]{1,0:T(8,128)(2,1)} %param.18) | copy-start | bytes 884740
  7.2 90.4 %all-gather.10.cloned.1.call-start = ((), (), s32[]{:S(2)}) async-start(), calls=%async_computation.4 | async-start | bytes 5222400 | tf_op jit(solution)/shard_map/all_gather | solution.py:107
  8.5 6.9 copy-start.7
  8.5 6.9 copy-start.9
  8.5 6.9 copy-start.11
  8.5 6.9 copy-start.13
  8.5 6.9 copy-start.15
  8.6 6.9 copy-start.17
  8.6 6.9 copy-start.19
  8.6 6.9 copy-start.21
  8.6 6.9 copy-start.23
  8.6 6.9 copy-start.25
  8.6 6.9 copy-start.27
  8.6 7.5 copy-start.51
  8.7 6.8 copy-start.29
  8.7 6.8 copy-start.31
  8.8 6.8 copy-start.33
  8.8 6.8 copy-start.35
  8.8 6.8 copy-start.37
  8.8 6.8 copy-start.39
  8.8 6.8 copy-start.41
  8.8 6.8 copy-start.43
  8.8 6.8 copy-start.45
  8.8 6.8 copy-start.47
  8.8 6.8 copy-start.49
  9.9 7.9 copy-start.59
  9.9 8.6 %copy-start.4 = (bf16[1,14,14,768]{3,2,1,0:T(8,128)(2,1)S(1)}, bf16[1,14,14,768]{3,2,1,0:T(8,128)(2,1)}, u32[]{:S(2)}) copy-start(bf16[1,14,14,768]{3,2,1,0:T(8,128)(2,1)} %param.11) | copy-start | bytes 903172
  15.7 89.0 %copy-start.1 = (f32[196,768]{1,0:T(8,128)}, f32[196,768]{1,0:T(8,128)S(1)}, u32[]{:S(2)}) copy-start(f32[196,768]{1,0:T(8,128)S(1)} %reshape.89) | copy-start | bytes 1806340
  16.2 88.6 %copy-start.56 = (f32[196]{0:T(256)}, f32[196]{0:T(256)S(1)}, u32[]{:S(2)}) copy-start(f32[196]{0:T(256)S(1)} %rsqrt.12) | copy-start | bytes 2356
  17.1 161.3 %all-gather.8.cloned.1.call-start = ((), (), s32[]{:S(2)}) async-start(), calls=%async_computation.3 | async-start | bytes 5222400 | tf_op jit(solution)/shard_map/all_gather | solution.py:103
  20.1 283.5 %all-gather.6.cloned.1.call-start = ((), (), s32[]{:S(2)}) async-start(), calls=%async_computation.1 | async-start | bytes 5013504 | tf_op jit(solution)/shard_map/all_gather | solution.py:121
  186.2 4.2 copy-start.6
  207.8 95.8 %all-to-all-start = ((bf16[16,196,192]{1,2,0:T(8,128)(2,1)}), bf16[16,196,192]{1,2,0:T(8,128)(2,1)}, u32[]{:S(2)}, u32[]{:S(2)}) async-start(bf16[16,196,192]{1,2,0:T(8,128)(2,1)} %copy.18), calls=%async_computation | async-start | bytes 3145728 | tf_op jit(solution)/shard_map/all_to_all | solution.py:119
  212.2 352.9 %all-reduce.9.cloned.1.call-start = ((), (), s32[]{:S(2)}) async-start(), calls=%async_computation.5 | async-start | bytes 2359296 | tf_op jit(solution)/shard_map/psum | solution.py:118
  225.1 611.8 %all-reduce.7.cloned.1.call-start = ((), (), s32[]{:S(2)}) async-start(), calls=%async_computation.2 | async-start | bytes 344064 | tf_op jit(solution)/shard_map/psum | solution.py:134
  298.1 5.4 copy-start.52
  303.5 4.5 copy-start.2
  303.5 4.5 copy-start.3
  303.5 4.5 copy-start.55
  303.5 4.5 copy-start.57
  308.4 109.5 %copy-start.5 = (bf16[1,14,14,768]{3,2,1,0:T(8,128)(2,1)S(1)}, bf16[1,14,14,768]{3,2,1,0:T(8,128)(2,1)}, u32[]{:S(2)}) copy-start(bf16[1,14,14,768]{3,2,1,0:T(8,128)(2,1)} %param.11) | copy-start | bytes 903172
  308.4 109.5 %copy-start.8 = (f32[768]{0:T(1024)S(1)}, f32[768]{0:T(1024)}, u32[]{:S(2)}) copy-start(f32[768]{0:T(1024)} %copy-done.7) | copy-start | bytes 9220
  308.4 109.5 %copy-start.10 = (f32[768]{0:T(1024)S(1)}, f32[768]{0:T(1024)}, u32[]{:S(2)}) copy-start(f32[768]{0:T(1024)} %copy-done.9) | copy-start | bytes 9220
  308.4 109.5 %copy-start.12 = (f32[768]{0:T(1024)S(1)}, f32[768]{0:T(1024)}, u32[]{:S(2)}) copy-start(f32[768]{0:T(1024)} %copy-done.11) | copy-start | bytes 9220
  308.4 109.5 %copy-start.14 = (f32[768]{0:T(1024)S(1)}, f32[768]{0:T(1024)}, u32[]{:S(2)}) copy-start(f32[768]{0:T(1024)} %copy-done.13) | copy-start | bytes 9220
  308.4 109.5 %copy-start.16 = (f32[768]{0:T(1024)S(1)}, f32[768]{0:T(1024)}, u32[]{:S(2)}) copy-start(f32[768]{0:T(1024)} %copy-done.15) | copy-start | bytes 9220
  308.5 109.5 %copy-start.18 = (f32[768]{0:T(1024)S(1)}, f32[768]{0:T(1024)}, u32[]{:S(2)}) copy-start(f32[768]{0:T(1024)} %copy-done.17) | copy-start | bytes 9220
  308.5 109.5 %copy-start.20 = (f32[768]{0:T(1024)S(1)}, f32[768]{0:T(1024)}, u32[]{:S(2)}) copy-start(f32[768]{0:T(1024)} %copy-done.19) | copy-start | bytes 9220
  308.5 109.5 %copy-start.22 = (f32[768]{0:T(1024)S(1)}, f32[768]{0:T(1024)}, u32[]{:S(2)}) copy-start(f32[768]{0:T(1024)} %copy-done.21) | copy-start | bytes 9220
  308.5 109.5 %copy-start.24 = (f32[768]{0:T(1024)S(1)}, f32[768]{0:T(1024)}, u32[]{:S(2)}) copy-start(f32[768]{0:T(1024)} %copy-done.23) | copy-start | bytes 9220
  308.5 109.5 %copy-start.26 = (f32[768]{0:T(1024)S(1)}, f32[768]{0:T(1024)}, u32[]{:S(2)}) copy-start(f32[768]{0:T(1024)} %copy-done.25) | copy-start | bytes 9220
  308.5 109.5 %copy-start.28 = (f32[768]{0:T(1024)S(1)}, f32[768]{0:T(1024)}, u32[]{:S(2)}) copy-start(f32[768]{0:T(1024)} %copy-done.27) | copy-start | bytes 9220
  308.5 109.5 %copy-start.30 = (f32[768]{0:T(1024)S(1)}, f32[768]{0:T(1024)}, u32[]{:S(2)}) copy-start(f32[768]{0:T(1024)} %copy-done.29) | copy-start | bytes 9220
  308.5 109.5 %copy-start.32 = (f32[768]{0:T(1024)S(1)}, f32[768]{0:T(1024)}, u32[]{:S(2)}) copy-start(f32[768]{0:T(1024)} %copy-done.31) | copy-start | bytes 9220
  308.5 109.5 %copy-start.34 = (f32[768]{0:T(1024)S(1)}, f32[768]{0:T(1024)}, u32[]{:S(2)}) copy-start(f32[768]{0:T(1024)} %copy-done.33) | copy-start | bytes 9220
  308.5 109.5 %copy-start.36 = (f32[768]{0:T(1024)S(1)}, f32[768]{0:T(1024)}, u32[]{:S(2)}) copy-start(f32[768]{0:T(1024)} %copy-done.35) | copy-start | bytes 9220
  308.6 109.5 %copy-start.38 = (f32[768]{0:T(1024)S(1)}, f32[768]{0:T(1024)}, u32[]{:S(2)}) copy-start(f32[768]{0:T(1024)} %copy-done.37) | copy-start | bytes 9220
  308.6 109.5 %copy-start.40 = (f32[768]{0:T(1024)S(1)}, f32[768]{0:T(1024)}, u32[]{:S(2)}) copy-start(f32[768]{0:T(1024)} %copy-done.39) | copy-start | bytes 9220
  308.6 109.5 %copy-start.42 = (f32[768]{0:T(1024)S(1)}, f32[768]{0:T(1024)}, u32[]{:S(2)}) copy-start(f32[768]{0:T(1024)} %copy-done.41) | copy-start | bytes 9220
  308.6 109.5 %copy-start.44 = (f32[768]{0:T(1024)S(1)}, f32[768]{0:T(1024)}, u32[]{:S(2)}) copy-start(f32[768]{0:T(1024)} %copy-done.43) | copy-start | bytes 9220
  308.6 109.5 %copy-start.46 = (f32[768]{0:T(1024)S(1)}, f32[768]{0:T(1024)}, u32[]{:S(2)}) copy-start(f32[768]{0:T(1024)} %copy-done.45) | copy-start | bytes 9220
  308.6 109.5 %copy-start.48 = (f32[768]{0:T(1024)S(1)}, f32[768]{0:T(1024)}, u32[]{:S(2)}) copy-start(f32[768]{0:T(1024)} %copy-done.47) | copy-start | bytes 9220
  308.6 109.5 %copy-start.50 = (f32[768]{0:T(1024)S(1)}, f32[768]{0:T(1024)}, u32[]{:S(2)}) copy-start(f32[768]{0:T(1024)} %copy-done.49) | copy-start | bytes 9220
  416.1 153.5 %copy-start.58 = (f32[192]{0:T(256)S(1)}, f32[192]{0:T(256)}, u32[]{:S(2)}) copy-start(f32[192]{0:T(256)} %psum.51) | copy-start | bytes 2308
  (2 other events, 5.8 us)
Sparse Core Ops, SparseCore 0:
  17.2 80.3 all-gather.9
  100.3 78.0 all-gather.7
  180.4 107.5 all-gather.5
  291.5 273.5 all-reduce.8
  571.3 265.6 all-reduce.6
where the time goes:
time: 846 us; the launch traced here: 845 us
  waiting for transfers between devices  559 us (66%)
  blocking collectives  175 us (21%)
  matrix products  32.3 us (4%)
  local copies, waits for them, and re-layouts  29.8 us (4%)
  other arithmetic  28 us (3%)
  between operations  16.5 us (2%)
    psum x1, waiting for transfers between devices, per_device(): summed = lax.psum(members, ('replica', 'shard'))  267 us
    psum x1, waiting for transfers between devices, per_device(): lax.psum((first_sum, bias_sum, second_sum), 'replica')  141 us
    psum x1, blocking collectives, per_device(): weight_sum = lax.psum(own_weight, ('replica', 'shard'))  102 us
    all_gather x1, waiting for transfers between devices, per_device(): normed_gathered = lax.all_gather(normed, 'shard', axis=0, tiled=True)  76.8 us
    all_gather x1, waiting for transfers between devices, per_device(): grad_gathered = lax.all_gather(scaled, 'shard', axis=0, tiled=True)  73.6 us
    psum x1, blocking collectives, per_device(): lax.psum((first_sum, bias_sum, second_sum), 'replica')  72.9 us
  transfers between devices with their start and end apart: 6, of which 4 were waited for; matrix products, arithmetic and copies ran while one was open for 9% of the time, Pallas kernels for 0%

commit v1 on v0

v1 whole, which is shorter than its diff:
```python
import jax
import jax.numpy as jnp
import numpy as np
from jax import lax
from jax.experimental import pallas as pl
from jax.experimental.pallas import tpu as pltpu
from jax.sharding import Mesh, PartitionSpec as P

F32 = jnp.float32
BF16 = jnp.bfloat16
ROWS = 14
COLS = 14
WIDE = 16
PIX = ROWS * WIDE
CH = 768
LANES = 128
BLOCKS = CH // LANES
OWN = 48
HID = 384
PACK = 112
REPLICA = ("y", "xh", "core")
SHARD = ("xl", "z")
RING = ("xh", "xl")
TEAM = ("xh", "core", "xl")
INTERPRET = False


def params(limit_mib, **more):
    return pltpu.CompilerParams(vmem_limit_bytes=limit_mib * 1024 * 1024, **more)


def nt(left, right):
    return lax.dot_general(left, right, (((1,), (1,)), ((), ())), preferred_element_type=F32)


def tn(left, right):
    return lax.dot_general(left, right, (((0,), (0,)), ((), ())), preferred_element_type=F32)


def whole():
    return pl.BlockSpec(memory_space=pltpu.VMEM)


def scalars():
    return pl.BlockSpec(memory_space=pltpu.SMEM)


def pack_kernel(place_ref, first_ref, bias_ref, second_ref, out_ref):
    block = place_ref[0]
    column = place_ref[1]
    row = lax.broadcasted_iota(jnp.int32, (OWN, 192), 0)
    lane = lax.broadcasted_iota(jnp.int32, (OWN, 192), 1)
    pick = (lane == row + block * OWN).astype(BF16)
    out_ref[0:OWN, :] = nt(pick, first_ref[...]).astype(BF16)
    out_ref[OWN : 2 * OWN, :] = jnp.dot(pick, second_ref[...], preferred_element_type=F32).astype(BF16)
    unit = lax.broadcasted_iota(jnp.int32, (192, HID), 0) - block * OWN
    spot = lax.broadcasted_iota(jnp.int32, (192, HID), 1) - column * OWN
    put = ((unit == spot) & (unit >= 0) & (unit < OWN)).astype(BF16)
    bias = jnp.broadcast_to(bias_ref[...], (16, 192))
    high = bias.astype(BF16)
    low = (bias - high.astype(F32)).astype(BF16)
    out_ref[2 * OWN : PACK, 0:HID] = jnp.dot(high, put, preferred_element_type=F32).astype(BF16)
    out_ref[2 * OWN : PACK, HID:CH] = jnp.dot(low, put, preferred_element_type=F32).astype(BF16)


def pack_weights(place, first_weight, first_bias, second_weight):
    return pl.pallas_call(
        pack_kernel,
        out_shape=jax.ShapeDtypeStruct((PACK, CH), BF16),
        in_specs=[scalars(), whole(), whole(), whole()],
        out_specs=whole(),
        compiler_params=params(16),
        interpret=INTERPRET,
        name="pack",
    )(place, first_weight, first_bias.reshape(1, 192), second_weight)


def taps_sum(padded_ref, kernel, flip):
    halves = []
    for half in range(2):
        total = jnp.zeros((7, WIDE, LANES), F32)
        for b in range(7):
            moved = padded_ref[half * 7 : half * 7 + 13, b : b + WIDE, :]
            for a in range(7):
                tap = (6 - a) * 7 + (6 - b) if flip else a * 7 + b
                total = total + moved[a : a + 7] * kernel[tap : tap + 1, :].reshape(1, 1, LANES)
        halves.append(total)
    return halves


def column_mask():
    return (lax.broadcasted_iota(jnp.int32, (ROWS, WIDE, LANES), 1) < COLS).astype(F32)


def forward_kernel(image_ref, kernel_ref, gain_ref, normed_ref, centred_ref, inv_ref, padded, conv):
    j = pl.program_id(0)

    @pl.when(j == 0)
    def _():
        padded[...] = jnp.zeros_like(padded)

    padded[3:17, 3:17, :] = image_ref[...].astype(F32)
    halves = taps_sum(padded, kernel_ref[...].astype(F32), False)
    conv[j, 0:7] = halves[0]
    conv[j, 7:14] = halves[1]

    @pl.when(j == BLOCKS - 1)
    def _():
        mask = column_mask()
        total = conv[0]
        for i in range(1, BLOCKS):
            total = total + conv[i]
        mean = jnp.sum(total, axis=-1, keepdims=True) * (1.0 / CH)
        square = jnp.zeros((ROWS, WIDE, LANES), F32)
        for i in range(BLOCKS):
            part = conv[i] - mean
            square = square + part * part
        inv = lax.rsqrt(jnp.sum(square, axis=-1, keepdims=True) * (1.0 / CH) + 1e-06)
        inv_ref[...] = jnp.broadcast_to(inv, (ROWS, WIDE, LANES))
        for i in range(BLOCKS):
            part = (conv[i] - mean) * inv * mask
            centred_ref[i] = part
            lanes = slice(i * LANES, (i + 1) * LANES)
            gain = gain_ref[:, lanes].reshape(1, 1, LANES)
            normed_ref[:, lanes] = (part * gain).reshape(PIX, LANES).astype(BF16)


def forward(image, kernel, gain):
    return pl.pallas_call(
        forward_kernel,
        grid=(BLOCKS,),
        out_shape=(
            jax.ShapeDtypeStruct((PIX, CH), BF16),
            jax.ShapeDtypeStruct((BLOCKS, ROWS, WIDE, LANES), F32),
            jax.ShapeDtypeStruct((ROWS, WIDE, LANES), F32),
        ),
        in_specs=[
            pl.BlockSpec((ROWS, COLS, LANES), lambda j: (0, 0, j)),
            pl.BlockSpec((49, LANES), lambda j: (0, j)),
            pl.BlockSpec((1, CH), lambda j: (0, 0)),
        ],
        out_specs=(
            pl.BlockSpec((PIX, CH), lambda j: (0, 0)),
            pl.BlockSpec((BLOCKS, ROWS, WIDE, LANES), lambda j: (0, 0, 0, 0)),
            pl.BlockSpec((ROWS, WIDE, LANES), lambda j: (0, 0, 0)),
        ),
        scratch_shapes=[
            pltpu.VMEM((20, 24, LANES), F32),
            pltpu.VMEM((BLOCKS, ROWS, WIDE, LANES), F32),
        ],
        compiler_params=params(24),
        interpret=INTERPRET,
        name="conv_norm",
    )(image, kernel, gain)


def hidden_kernel(*refs):
    normed = refs[0:8]
    scaled = refs[8:16]
    pack_ref, layer_ref = refs[16:18]
    mine_ref, other_ref, act_ref, grad_ref = refs[18:22]
    first = pack_ref[:, 0:OWN, :].reshape(HID, CH)
    second = pack_ref[:, OWN : 2 * OWN, :].reshape(HID, CH)
    bias = jnp.sum(pack_ref[:, 2 * OWN : PACK, :].astype(F32), axis=0)[0:1, :]
    bias = bias[:, 0:HID] + bias[:, HID:CH]
    layer = layer_ref[...]
    for i in range(8):
        preact = nt(normed[i][...], first) + bias
        cumulative = 0.5 * (1.0 + lax.erf(preact * 0.7071067811865476))
        slope = cumulative + preact * jnp.exp(-0.5 * preact * preact) * 0.3989422804014327
        act_ref[i] = (preact * cumulative).astype(BF16)
        branch_grad = (scaled[i][...].astype(F32) * layer).astype(BF16)
        preact_grad = (nt(branch_grad, second) * slope).astype(BF16)
        grad_ref[i] = preact_grad
        part = jnp.dot(preact_grad, first, preferred_element_type=F32).astype(BF16)
        if i % 2 == 0:
            mine_ref[i // 2] = part
        else:
            other_ref[i // 2] = part


def hidden(normed, scaled, pack, layer):
    return pl.pallas_call(
        hidden_kernel,
        out_shape=(
            jax.ShapeDtypeStruct((4, PIX, CH), BF16),
            jax.ShapeDtypeStruct((4, PIX, CH), BF16),
            jax.ShapeDtypeStruct((8, PIX, HID), BF16),
            jax.ShapeDtypeStruct((8, PIX, HID), BF16),
        ),
        in_specs=[whole()] * 18,
        out_specs=(whole(),) * 4,
        compiler_params=params(48),
        interpret=INTERPRET,
        name="hidden",
    )(*normed, *scaled, pack, layer)


def weights_kernel(*refs):
    normed = refs[0:8]
    scaled = refs[8:16]
    act_ref, grad_ref, pack_ref, layer_ref = refs[16:20]
    out_ref, scale_ref = refs[20:22]
    product = tn(act_ref[0], scaled[0][...])
    for i in range(1, 8):
        product = product + tn(act_ref[i], scaled[i][...])
    second = pack_ref[:, OWN : 2 * OWN, :].reshape(HID, CH).astype(F32)
    scale_ref[...] = jnp.sum((second * product).reshape(HID // 8, 8, CH), axis=0)
    spread(out_ref, (product * layer_ref[...]).astype(BF16), 0)
    product = tn(grad_ref[0], normed[0][...])
    for i in range(1, 8):
        product = product + tn(grad_ref[i], normed[i][...])
    spread(out_ref, product.astype(BF16), 18)
    ones = jnp.ones((16, PIX), BF16)
    bias = jnp.dot(ones, grad_ref[0], preferred_element_type=F32)
    for i in range(1, 8):
        bias = bias + jnp.dot(ones, grad_ref[i], preferred_element_type=F32)
    row = lax.broadcasted_iota(jnp.int32, (16, LANES), 0)
    block = jnp.zeros((16, LANES), F32)
    for k in range(3):
        block = jnp.where(row == k, bias[:, k * LANES : (k + 1) * LANES], block)
    block = block.astype(BF16)
    empty = jnp.zeros((16, LANES), BF16)
    for z in range(8):
        for s in range(36, 40):
            out_ref[(s // 5) * 8 + z, (s % 5) * 16 : (s % 5) * 16 + 16, :] = block if s == 36 else empty


def spread(out_ref, matrix, start):
    for z in range(8):
        for j in range(BLOCKS):
            for part in range(3):
                s = start + j * 3 + part
                row = z * OWN + part * 16
                out_ref[(s // 5) * 8 + z, (s % 5) * 16 : (s % 5) * 16 + 16, :] = matrix[
                    row : row + 16, j * LANES : (j + 1) * LANES
                ]


def weight_grads(normed, scaled, act, grad, pack, layer):
    return pl.pallas_call(
        weights_kernel,
        out_shape=(
            jax.ShapeDtypeStruct((64, 80, LANES), BF16),
            jax.ShapeDtypeStruct((8, CH), F32),
        ),
        in_specs=[whole()] * 20,
        out_specs=(whole(),) * 2,
        compiler_params=params(48),
        interpret=INTERPRET,
        name="weight_grads",
    )(*normed, *scaled, act, grad, pack, layer)


def pair_kernel(mine_ref, got_ref, *out_refs):
    for r in range(1, 4):
        out_refs[r - 1][...] = (mine_ref[r].astype(F32) + got_ref[r].astype(F32)).astype(BF16)


def pair_sums(mine, got):
    return pl.pallas_call(
        pair_kernel,
        out_shape=(jax.ShapeDtypeStruct((PIX, CH), BF16),) * 3,
        in_specs=[whole()] * 2,
        out_specs=(whole(),) * 3,
        compiler_params=params(24),
        interpret=INTERPRET,
        name="pair_sums",
    )(mine, got)


def backward_kernel(
    mine_ref, got_ref, one_ref, two_ref, three_ref, centred_ref, inv_ref, gain_ref, scale_ref, image_ref,
    sums_ref, conv_ref, padded, conv, parts, gains,
):
    j = pl.program_id(0)

    @pl.when(j == 0)
    def _():
        padded[...] = jnp.zeros_like(padded)
        first = jnp.zeros((ROWS, WIDE, LANES), F32)
        second = jnp.zeros((ROWS, WIDE, LANES), F32)
        for i in range(BLOCKS):
            lanes = slice(i * LANES, (i + 1) * LANES)
            grad = (
                mine_ref[0, :, lanes].astype(F32)
                + got_ref[0, :, lanes].astype(F32)
                + one_ref[:, lanes].astype(F32)
                + two_ref[:, lanes].astype(F32)
                + three_ref[:, lanes].astype(F32)
            ).reshape(ROWS, WIDE, LANES)
            centred = centred_ref[i]
            product = grad * centred
            gains[i] = jnp.sum(jnp.sum(product, axis=0).reshape(2, 8, LANES), axis=0)
            gain = gain_ref[:, lanes].reshape(1, 1, LANES)
            gained = grad * gain
            conv[i] = gained
            first = first + gained
            second = second + product * gain
        mean = jnp.sum(first, axis=-1, keepdims=True) * (1.0 / CH)
        slant = jnp.sum(second, axis=-1, keepdims=True) * (1.0 / CH)
        inv = inv_ref[...] * column_mask()
        for i in range(BLOCKS):
            conv[i] = inv * (conv[i] - mean - centred_ref[i] * slant)

    padded[3:17, 3:17, :] = image_ref[...].astype(F32)
    conv_ref[0] = conv[j]
    for half in range(2):
        signal = conv[j, half * 7 : half * 7 + 7]
        for b in range(7):
            moved = padded[half * 7 : half * 7 + 13, b : b + WIDE, :]
            for a in range(7):
                product = jnp.sum(signal * moved[a : a + 7], axis=0)
                product = product[0:8] + product[8:16]
                if half == 0:
                    parts[a * 7 + b] = product
                else:
                    parts[a * 7 + b] += product
    sums_ref[0] = jnp.zeros((64, LANES), F32)
    sums_ref[0, 0:49, :] = jnp.sum(parts[...], axis=1)
    sums_ref[0, 49:50, :] = jnp.sum(gains[j], axis=0, keepdims=True)
    sums_ref[0, 50:51, :] = jnp.sum(scale_ref[...], axis=0, keepdims=True)


def backward(mine, got, one, two, three, centred, inv, gain, scale, image):
    def fixed(*shape):
        return pl.BlockSpec(shape, lambda j: (0,) * len(shape))

    return pl.pallas_call(
        backward_kernel,
        grid=(BLOCKS,),
        out_shape=(
            jax.ShapeDtypeStruct((BLOCKS, 64, LANES), F32),
            jax.ShapeDtypeStruct((BLOCKS, ROWS, WIDE, LANES), F32),
        ),
        in_specs=[
            fixed(1, PIX, CH),
            fixed(1, PIX, CH),
            fixed(PIX, CH),
            fixed(PIX, CH),
            fixed(PIX, CH),
            fixed(BLOCKS, ROWS, WIDE, LANES),
            fixed(ROWS, WIDE, LANES),
            fixed(1, CH),
            pl.BlockSpec((8, LANES), lambda j: (0, j)),
            pl.BlockSpec((ROWS, COLS, LANES), lambda j: (0, 0, j)),
        ],
        out_specs=(
            pl.BlockSpec((1, 64, LANES), lambda j: (j, 0, 0)),
            pl.BlockSpec((1, ROWS, WIDE, LANES), lambda j: (j, 0, 0, 0)),
        ),
        scratch_shapes=[
            pltpu.VMEM((20, 24, LANES), F32),
            pltpu.VMEM((BLOCKS, ROWS, WIDE, LANES), F32),
            pltpu.VMEM((49, 8, LANES), F32),
            pltpu.VMEM((BLOCKS, 8, LANES), F32),
        ],
        compiler_params=params(32),
        interpret=INTERPRET,
        name="norm_back",
    )(mine, got, one, two, three, centred, inv, gain, scale, image)


def input_kernel(factor_ref, conv_ref, kernel_ref, scaled_ref, out_ref, padded):
    @pl.when(pl.program_id(0) == 0)
    def _():
        padded[...] = jnp.zeros_like(padded)

    padded[3:17, 3 : 3 + WIDE, :] = conv_ref[0]
    halves = taps_sum(padded, kernel_ref[...].astype(F32), True)
    factor = factor_ref[0]
    for half in range(2):
        rows = slice(half * 7 * WIDE, (half + 1) * 7 * WIDE)
        scaled = scaled_ref[rows, :].astype(F32).reshape(7, WIDE, LANES)
        result = (factor * (scaled + halves[half])).astype(BF16)
        out_ref[0, half * 7 : half * 7 + 7] = result[:, 0:COLS, :]


def input_grad(factor, conv, kernel, scaled):
    return pl.pallas_call(
        input_kernel,
        grid=(BLOCKS,),
        out_shape=jax.ShapeDtypeStruct((1, ROWS, COLS, CH), BF16),
        in_specs=[
            scalars(),
            pl.BlockSpec((1, ROWS, WIDE, LANES), lambda j: (j, 0, 0, 0)),
            pl.BlockSpec((49, LANES), lambda j: (0, j)),
            pl.BlockSpec((PIX, LANES), lambda j: (0, j)),
        ],
        out_specs=pl.BlockSpec((1, ROWS, COLS, LANES), lambda j: (0, 0, 0, j)),
        scratch_shapes=[pltpu.VMEM((20, 24, LANES), F32)],
        compiler_params=params(24),
        interpret=INTERPRET,
        name="input_grad",
    )(factor, conv, kernel, scaled)


def unpack_kernel(factor_ref, core_ref, mine_ref, other_ref, first_ref, second_ref):
    factor = factor_ref[0]
    even = core_ref[0] == 0

    def column(kind, j):
        pieces = []
        for xh in range(2):
            own, got = [], []
            for part in range(3):
                s = kind * 18 + j * 3 + part
                rows = slice((s % 5) * 16, (s % 5) * 16 + 16)
                own.append(mine_ref[(s // 5) * 2 + xh, rows, :].astype(F32))
                got.append(other_ref[(s // 5) * 2 + xh, rows, :].astype(F32))
            own, got = jnp.concatenate(own), jnp.concatenate(got)
            pieces += [jnp.where(even, own, got), jnp.where(even, got, own)]
        return jnp.concatenate(pieces) * factor

    for j in range(BLOCKS):
        lanes = slice(j * LANES, (j + 1) * LANES)
        second_ref[:, lanes] = column(0, j)
        first_ref[lanes, :] = column(1, j).T


def unpack(factor, core, mine, other):
    return pl.pallas_call(
        unpack_kernel,
        out_shape=(
            jax.ShapeDtypeStruct((CH, 192), F32),
            jax.ShapeDtypeStruct((192, CH), F32),
        ),
        in_specs=[scalars(), scalars(), whole(), whole()],
        out_specs=(whole(),) * 2,
        compiler_params=params(16),
        interpret=INTERPRET,
        name="unpack",
    )(factor, core, mine, other)


def to_all(value, axes):
    count = lax.axis_size(axes)
    return lax.all_to_all(jnp.broadcast_to(value, (count, *value.shape)), axes, 0, 0, tiled=True)


def swap_core(value):
    return lax.ppermute(value, "core", [(0, 1), (1, 0)])


def ring(value, shift):
    return lax.ppermute(value, RING, [(i, (i + shift) % 4) for i in range(4)])


def share(value):
    mine = [value] + [ring(value, r) for r in range(1, 4)]
    result = []
    for item in mine:
        result += [item, swap_core(item)]
    return result


def per_device(
    image, upstream, group_ids, group_weights, conv_kernel, norm_gain, first_weight, first_bias, second_weight, layer_scale
):
    core = lax.axis_index("core")
    block = lax.axis_index("xh") * 2 + core
    column = lax.axis_index("z")
    place = jnp.stack([block, column]).astype(jnp.int32)
    packed = pack_weights(place, first_weight, first_bias, second_weight)
    packed = lax.all_gather(packed, "z", axis=0, tiled=True).reshape(8, PACK, CH)

    labels = jnp.arange(group_weights.shape[0], dtype=jnp.int32)
    own_weight = jnp.sum(jnp.where(labels == group_ids[0], group_weights, 0.0))
    scaled = (own_weight * upstream[0].astype(F32)).astype(BF16)
    scaled = jnp.pad(scaled, ((0, 0), (0, WIDE - COLS), (0, 0))).reshape(PIX, CH)
    scaled_all = share(scaled)

    kernel = conv_kernel.reshape(49, CH)
    gain = norm_gain.reshape(1, CH)
    layer = layer_scale.reshape(1, CH)
    normed, centred, inv = forward(image[0], kernel, gain)
    normed_all = share(normed)

    weight_sum = jnp.sum(to_all(jnp.full((8, LANES), own_weight, F32), SHARD), axis=0)
    weight_sum = jnp.sum(to_all(weight_sum, REPLICA), axis=0)
    images = lax.axis_size(REPLICA) * lax.axis_size(SHARD)
    factor = (images / weight_sum[0:1, 0]).astype(F32)

    mine, other, act, preact_grad = hidden(normed_all, scaled_all, packed, layer)
    got = swap_core(other)
    sums = pair_sums(mine, got)
    returned = [ring(sums[r - 1], 4 - r) for r in range(1, 4)]

    grads, scale = weight_grads(normed_all, scaled_all, act, preact_grad, packed, layer)
    grads = lax.all_to_all(grads, ("y", "z"), 0, 0, tiled=True)
    grads = jnp.sum(grads.astype(F32), axis=0).astype(BF16)
    grads = to_all(grads, ("y", "xh"))
    grads_other = swap_core(grads)
    grad_first, grad_second = unpack(factor, core.reshape(1).astype(jnp.int32), grads, grads_other)

    def bias_of(gathered):
        both = gathered[14:16, 16:32, :][:, 0:3, :].reshape(2, HID).astype(F32)
        return lax.dynamic_slice(both, (0, column * OWN), (2, OWN))

    bias_mine, bias_other = bias_of(grads), bias_of(grads_other)
    bias = jnp.stack([jnp.where(core == 0, bias_mine, bias_other), jnp.where(core == 0, bias_other, bias_mine)], axis=1)
    grad_bias = factor * bias.reshape(4 * OWN)

    small, conv_grad = backward(mine, got, *returned, centred, inv, gain, scale, image[0])
    small = lax.all_to_all(small.reshape(8, OWN, LANES), TEAM, 0, 0, tiled=True)
    small = jnp.sum(small, axis=0)
    small = jnp.sum(to_all(small, "y"), axis=0)
    small = jnp.sum(to_all(small, "z"), axis=0)
    small = to_all(small, TEAM).reshape(BLOCKS, 64, LANES) * factor
    small = small.transpose(1, 0, 2).reshape(64, CH)
    grad_image = input_grad(factor, conv_grad, kernel, scaled)
    return (
        grad_image,
        grad_first,
        grad_bias,
        grad_second,
        small[0:49].reshape(7, 7, CH),
        small[49],
        small[50],
    )


def solution(mesh):
    fine = Mesh(mesh.devices.reshape(8, 2, 2, 2, 8), ("y", "xh", "core", "xl", "z"))
    images = P((*REPLICA, *SHARD), None, None, None)
    return jax.shard_map(
        per_device,
        mesh=fine,
        in_specs=(
            images,
            images,
            P((*REPLICA, *SHARD)),
            P(),
            P(),
            P(),
            P(None, SHARD),
            P(SHARD),
            P(SHARD, None),
            P(),
        ),
        out_specs=(images, P(None, SHARD), P(SHARD), P(SHARD, None), P(), P(), P()),
        check_vma=False,
    )
```

time: 846 us -> 283 us (0.33)
  waiting for transfers between devices: 559 us -> 87.8 us
  blocking collectives: 175 us -> 22.7 us
  starting transfers between devices: 4.79 us -> 100 us
  matrix products: 32.3 us -> 0 us
  Pallas kernels: 0 us -> 27.2 us
  other arithmetic: 28 us -> 1.8 us
    psum x2 -> x0, waiting for transfers between devices: 408 us -> none  [the longest x1 267 us: per_device(): summed = lax.psum(members, ('replica', 'shard'))]
    psum x2 -> x0, blocking collectives: 175 us -> none  [the longest x1 102 us: per_device(): weight_sum = lax.psum(own_weight, ('replica', 'shard'))]
    all_gather x3 -> x1, waiting for transfers between devices: 150 us -> 0.01 us  [per_device(): lax.all_gather(packed, 'z', axis=0, tiled=True).reshape(8, PACK, CH)]
    all_to_all x1 -> x6, waiting for transfers between devices: 0.01 us -> 73.8 us  [the longest x5 40.8 us: to_all(): lax.all_to_all(jnp.broadcast_to(value, (count, *value.shape)), axes, 0, 0...]
    ppermute x0 -> x19, starting transfers between devices: none -> 59.6 us  [the longest x9 31.2 us: ring(): return lax.ppermute(value, RING, [(i, (i + shift) % 4) for i in range(4)])]
    all_to_all x1 -> x6, starting transfers between devices: 4.4 us -> 40.4 us  [the longest x5 35.8 us: to_all(): lax.all_to_all(jnp.broadcast_to(value, (count, *value.shape)), axes, 0, 0...]
    dot_general x6 -> x0, matrix products: 32.3 us -> none  [the longest x2 11.9 us: contract_cols(): lax.dot_general(left_side, right_side, (((1,), (1,)), ((), ())), preferre...]
    pallas_call x0 -> x8, Pallas kernels: none -> 27.2 us  [the longest x1 8.39 us: hidden(): pl.pallas_call(hidden_kernel, out_shape=(jax.ShapeDtypeStruct((4, PIX, CH...]
  transfers between devices with their start and end apart: 6 -> 26, of which waited for: 4 -> 11; matrix products, arithmetic and copies ran while one was open for 9% -> 2% of each run, Pallas kernels for 0% -> 5%
where the time goes in v1:
time: 283 us; the launch traced here: 281 us
  starting transfers between devices  100 us (35%)
  waiting for transfers between devices  87.8 us (31%)
  Pallas kernels  27.2 us (10%)
  local copies, waits for them, and re-layouts  25.5 us (9%)
  blocking collectives  22.7 us (8%)
  between operations  15.9 us (6%)
    all_to_all x5, waiting for transfers between devices, to_all(): lax.all_to_all(jnp.broadcast_to(value, (count, *value.shape)), axes, 0, 0...  40.8 us
    all_to_all x5, starting transfers between devices, to_all(): lax.all_to_all(jnp.broadcast_to(value, (count, *value.shape)), axes, 0, 0...  35.8 us
    all_to_all x1, waiting for transfers between devices, per_device(): grads = lax.all_to_all(grads, ('y', 'z'), 0, 0, tiled=True)  33.1 us
    ppermute x9, starting transfers between devices, ring(): return lax.ppermute(value, RING, [(i, (i + shift) % 4) for i in range(4)])  31.2 us
    ppermute x10, starting transfers between devices, swap_core(): return lax.ppermute(value, 'core', [(0, 1), (1, 0)])  28.3 us
    unnamed x62, local copies, waits for them, and re-layouts  17.9 us
    all_to_all x1, blocking collectives, to_all(): lax.all_to_all(jnp.broadcast_to(value, (count, *value.shape)), axes, 0, 0...  13.4 us
    ppermute x9, waiting for transfers between devices, ring(): return lax.ppermute(value, RING, [(i, (i + shift) % 4) for i in range(4)])  10.4 us
  transfers between devices with their start and end apart: 26, of which 11 were waited for; matrix products, arithmetic and copies ran while one was open for 2% of the time, Pallas kernels for 5%

profile of v1, /device:TPU:1, one launch (start us, length us, event | category | flops | bytes accessed | tf_op | source)
XLA Modules:
  0.0 281.0 jit_solution(7208252889762739938)
XLA Ops:
  7.3 1.2 copy.23.first_ref
  8.5 1.0 copy-done.21
  10.2 1.5 pack.1
  11.7 0.9 reshape.68.kernel_ref
  12.7 2.8 %conv_norm.1 = (bf16[224,768]{1,0:T(8,128)(2,1)S(1)}, f32[6,14,16,128]{3,2,1,0:T(8,128)S(1)}, f32[14,16,128]{2,1,0:T(8,128)S(1)}) custom-call(bf16[14,14,768]{2,1,0:T(8,128)(2,1)S(1)} %bitcast.40, bf16[49,768]{1,0:T(8,128)(2,1)S(1)} %reshape.68.kernel_ref, f32[1,768]{1,0:T(1,128)S(1)} %reshape.69.gain_ref), custom_call_target="tpu_custom_call" | custom-call | tf_op jit(solution)/shard_map/conv_norm/pallas_call | solution.py:129
  16.2 3.9 %collective-permute-start.1 = (bf16[224,768]{1,0:T(8,128)(2,1)S(1)}, bf16[224,768]{1,0:T(8,128)(2,1)S(1)}, u32[]{:S(2)}, u32[]{:S(2)}) collective-permute-start(bf16[224,768]{1,0:T(8,128)(2,1)S(1)} %get-tuple-element.23.refs_0_), channel_id=1, source_target_pairs={{0,8},{8,32},{32,40},{40,0},{1,9},{9,33},{33,41},{41,1},{2,10},{10... | collective-permute-start | bytes 1032200 | tf_op jit(solution)/shard_map/ppermute | solution.py:446
  20.1 4.4 %collective-permute-start.3 = (bf16[224,768]{1,0:T(8,128)(2,1)S(1)}, bf16[224,768]{1,0:T(8,128)(2,1)S(1)}, u32[]{:S(2)}, u32[]{:S(2)}) collective-permute-start(bf16[224,768]{1,0:T(8,128)(2,1)S(1)} %get-tuple-element.23.refs_0_), channel_id=1, source_target_pairs={{0,32},{8,40},{32,0},{40,8},{1,33},{9,41},{33,1},{41,9},{2,34},{10... | collective-permute-start | bytes 1032200 | tf_op jit(solution)/shard_map/ppermute | solution.py:446
  24.5 3.1 %collective-permute-start.5 = (bf16[224,768]{1,0:T(8,128)(2,1)S(1)}, bf16[224,768]{1,0:T(8,128)(2,1)S(1)}, u32[]{:S(2)}, u32[]{:S(2)}) collective-permute-start(bf16[224,768]{1,0:T(8,128)(2,1)S(1)} %get-tuple-element.23.refs_0_), channel_id=1, source_target_pairs={{0,40},{8,0},{32,8},{40,32},{1,41},{9,1},{33,9},{41,33},{2,42},{10... | collective-permute-start | bytes 1032200 | tf_op jit(solution)/shard_map/ppermute | solution.py:446
  27.6 6.4 %collective-permute-start = (bf16[224,768]{1,0:T(8,128)(2,1)S(1)}, bf16[224,768]{1,0:T(8,128)(2,1)S(1)}, u32[]{:S(2)}, u32[]{:S(2)}) collective-permute-start(bf16[224,768]{1,0:T(8,128)(2,1)S(1)} %get-tuple-element.23.refs_0_), channel_id=1, source_target_pairs={{0,16},{16,0},{1,17},{17,1},{2,18},{18,2},{3,19},{19,3},{4,20},{20... | collective-permute-start | bytes 1032200 | tf_op jit(solution)/shard_map/ppermute | solution.py:442
  36.0 4.5 %collective-permute-start.10 = (bf16[224,768]{1,0:T(8,128)(2,1)S(1)}, bf16[224,768]{1,0:T(8,128)(2,1)S(1)}, u32[]{:S(2)}, u32[]{:S(2)}) collective-permute-start(bf16[224,768]{1,0:T(8,128)(2,1)S(1)} %bitcast.33), channel_id=1, source_target_pairs={{0,32},{8,40},{32,0},{40,8},{1,33},{9,41},{33,1},{41,9},{2,34},{10... | collective-permute-start | bytes 1032200 | tf_op jit(solution)/shard_map/ppermute | solution.py:446
  40.6 2.2 collective-permute-start.12
  42.8 3.0 %collective-permute-start.8 = (bf16[224,768]{1,0:T(8,128)(2,1)S(1)}, bf16[224,768]{1,0:T(8,128)(2,1)S(1)}, u32[]{:S(2)}, u32[]{:S(2)}) collective-permute-start(bf16[224,768]{1,0:T(8,128)(2,1)S(1)} %bitcast.35), channel_id=1, source_target_pairs={{0,8},{8,32},{32,40},{40,0},{1,9},{9,33},{33,41},{41,1},{2,10},{10... | collective-permute-start | bytes 1032200 | tf_op jit(solution)/shard_map/ppermute | solution.py:446
  45.9 2.8 collective-permute-start.7
  48.6 1.9 collective-permute-start.2
  50.6 2.4 collective-permute-start.4
  53.0 1.8 collective-permute-done.12.refs_14_
  54.8 2.6 collective-permute-start.6
  57.4 1.9 collective-permute-start.11
  59.3 0.7 copy-done.3
  60.1 2.4 collective-permute-start.13
  62.5 0.7 copy-done.5
  63.2 1.9 collective-permute-start.9
  65.2 0.7 copy-done.7
  65.9 0.7 copy-done.9
  66.6 0.7 copy-done.11
  67.4 0.7 copy-done.13
  68.1 0.7 copy-done.15
  68.9 1.0 copy-done.4
  69.8 1.0 copy-done.6
  70.8 1.0 copy-done.8
  71.8 1.0 copy-done.10
  72.8 1.0 copy-done.12
  73.8 1.0 copy-done.14
  74.7 1.0 copy-done.16
  75.7 8.4 %hidden.1 = (bf16[4,224,768]{2,1,0:T(8,128)(2,1)}, bf16[4,224,768]{2,1,0:T(8,128)(2,1)}, bf16[8,224,384]{2,1,0:T(8,128)(2,1)}, bf16[8,224,384]{2,1,0:T(8,128)(2,1)}) custom-call(bf16[224,768]{1,0:T(8,128)(2,1)S(1)} %get-tuple-element.23.refs_0_, bf16[224,768]{1,0:T(8,128)(2,1)S(1)} %collective-permute-done.refs_1_, ...), custom_call_target="tpu_custom_call" | custom-call | tf_op jit(solution)/shard_map/hidden/pallas_call | solution.py:183
  84.1 2.4 collective-permute-start.14
  86.5 2.9 %collective-permute-done.14.got_ref = bf16[4,224,768]{2,1,0:T(8,128)(2,1)S(1)} collective-permute-done((bf16[4,224,768]{2,1,0:T(8,128)(2,1)}, bf16[4,224,768]{2,1,0:T(8,128)(2,1)S(1)}, u32[]{:S(2)}, u32[]{:S(2)}) %collective-permute-start.14) | collective-permute-done | bytes 1376288 | tf_op jit(solution)/shard_map/ppermute | solution.py:442
  89.5 1.3 copy-done
  91.0 4.3 %collective-permute-start.15 = (bf16[224,768]{1,0:T(8,128)(2,1)S(1)}, bf16[224,768]{1,0:T(8,128)(2,1)S(1)}, u32[]{:S(2)}, u32[]{:S(2)}) collective-permute-start(bf16[224,768]{1,0:T(8,128)(2,1)S(1)} %get-tuple-element.26), channel_id=1, source_target_pairs={{0,40},{8,0},{32,8},{40,32},{1,41},{9,1},{33,9},{41,33},{2,42},{10... | collective-permute-start | bytes 1032200 | tf_op jit(solution)/shard_map/ppermute | solution.py:446
  95.3 3.7 %collective-permute-start.16 = (bf16[224,768]{1,0:T(8,128)(2,1)S(1)}, bf16[224,768]{1,0:T(8,128)(2,1)S(1)}, u32[]{:S(2)}, u32[]{:S(2)}) collective-permute-start(bf16[224,768]{1,0:T(8,128)(2,1)S(1)} %get-tuple-element.27), channel_id=1, source_target_pairs={{0,32},{8,40},{32,0},{40,8},{1,33},{9,41},{33,1},{41,9},{2,34},{10... | collective-permute-start | bytes 1032200 | tf_op jit(solution)/shard_map/ppermute | solution.py:446
  99.0 2.1 collective-permute-start.17
  101.2 6.3 %weight_grads.1 = (bf16[64,80,128]{2,1,0:T(8,128)(2,1)}, f32[8,768]{1,0:T(8,128)S(1)}) custom-call(bf16[224,768]{1,0:T(8,128)(2,1)S(1)} %get-tuple-element.23.refs_0_, bf16[224,768]{1,0:T(8,128)(2,1)S(1)} %collective-permute-done.refs_1_, bf16[224,768]{1,0:T(8,128)(2,1)S(1)} %collective-permute-done.1.refs_2_, bf16[224,768]{1,0:T(8,128)(2,1)S(1)} %copy-done.6, ...), custom_call_target="tpu_custom_call" | custom-call | tf_op jit(solution)/shard_map/weight_grads/pallas_call | solution.py:241
  107.7 8.3 %collective-permute-done.17.three_ref = bf16[224,768]{1,0:T(8,128)(2,1)S(1)} collective-permute-done((bf16[224,768]{1,0:T(8,128)(2,1)S(1)}, bf16[224,768]{1,0:T(8,128)(2,1)S(1)}, u32[]{:S(2)}, u32[]{:S(2)}) %collective-permute-start.17) | collective-permute-done | bytes 344096 | tf_op jit(solution)/shard_map/ppermute | solution.py:446
  116.1 3.2 %norm_back.1 = (f32[6,64,128]{2,1,0:T(8,128)S(1)}, f32[6,14,16,128]{3,2,1,0:T(8,128)S(1)}) custom-call(bf16[4,224,768]{2,1,0:T(8,128)(2,1)S(1)} %copy-done.1, bf16[4,224,768]{2,1,0:T(8,128)(2,1)S(1)} %collective-permute-done.14.got_ref, bf16[224,768]{1,0:T(8,128)(2,1)S(1)} %collective-permute-done.15.one_ref, ...), custom_call_target="tpu_custom_call" | custom-call | tf_op jit(solution)/shard_map/norm_back/pallas_call | solution.py:329
  119.3 9.3 %all_to_all.40 = f32[8,48,128]{2,1,0:T(8,128)S(1)} all-to-all(f32[8,48,128]{2,1,0:T(8,128)S(1)} %bitcast.42), channel_id=1, replica_groups=mesh['y'=8,'xh'=2,'core'=2,'xl'=2,'z'=8] {'xh','core','xl'}, dimensions={0} | all-to-all | bytes 393216 | tf_op jit(solution)/shard_map/all_to_all | solution.py:505
  128.6 1.3 broadcast_in_dim_broadcast_in_dim.3
  129.9 9.7 %all-to-all-start = ((f32[16,8,128]{2,1,0:T(8,128)}), f32[16,8,128]{2,1,0:T(8,128)S(1)}, u32[]{:S(2)}, u32[]{:S(2)}) async-start(f32[16,8,128]{2,1,0:T(8,128)} %broadcast_in_dim_broadcast_in_dim.3), calls=%async_computation | async-start | bytes 131072 | tf_op jit(solution)/shard_map/all_to_all | solution.py:438
  139.6 7.4 %all-to-all-done = f32[16,8,128]{2,1,0:T(8,128)S(1)} async-done(((f32[16,8,128]{2,1,0:T(8,128)}), f32[16,8,128]{2,1,0:T(8,128)S(1)}, u32[]{:S(2)}, u32[]{:S(2)}) %all-to-all-start) | async-done | bytes 65568 | tf_op jit(solution)/shard_map/all_to_all | solution.py:438
  147.6 6.8 %all-to-all-start.5 = ((f32[8,48,128]{2,1,0:T(8,128)}), f32[8,48,128]{2,1,0:T(8,128)S(1)}, u32[]{:S(2)}, u32[]{:S(2)}) async-start(f32[8,48,128]{2,1,0:T(8,128)} %broadcast_in_dim.23), calls=%async_computation.5 | async-start | bytes 393216 | tf_op jit(solution)/shard_map/all_to_all | solution.py:438
  154.5 8.7 %all-to-all-done.5 = f32[8,48,128]{2,1,0:T(8,128)S(1)} async-done(((f32[8,48,128]{2,1,0:T(8,128)}), f32[8,48,128]{2,1,0:T(8,128)S(1)}, u32[]{:S(2)}, u32[]{:S(2)}) %all-to-all-start.5) | async-done | bytes 196640 | tf_op jit(solution)/shard_map/all_to_all | solution.py:438
  163.8 7.4 %all-to-all-start.1 = ((f32[32,8,128]{2,1,0:T(8,128)}), f32[32,8,128]{2,1,0:T(8,128)S(1)}, u32[]{:S(2)}, u32[]{:S(2)}) async-start(f32[32,8,128]{2,1,0:T(8,128)} %broadcast_in_dim.21), calls=%async_computation.1 | async-start | bytes 262144 | tf_op jit(solution)/shard_map/all_to_all | solution.py:438
  171.3 10.9 %all-to-all-done.1 = f32[32,8,128]{2,1,0:T(8,128)S(1)} async-done(((f32[32,8,128]{2,1,0:T(8,128)}), f32[32,8,128]{2,1,0:T(8,128)S(1)}, u32[]{:S(2)}, u32[]{:S(2)}) %all-to-all-start.1) | async-done | bytes 131104 | tf_op jit(solution)/shard_map/all_to_all | solution.py:438
  182.3 13.4 %all_to_all.41 = f32[8,48,128]{2,1,0:T(8,128)S(1)} all-to-all(f32[8,48,128]{2,1,0:T(8,128)S(1)} %broadcast_in_dim.24), channel_id=1, replica_groups=mesh['y'=8,'xh'=2,'core'=2,'xl'=2,'z'=8] {'z'}, dimensions={0} | all-to-all | bytes 393216 | tf_op jit(solution)/shard_map/all_to_all | solution.py:438
  195.6 4.7 %all-to-all-start.2 = ((bf16[64,80,128]{2,1,0:T(8,128)(2,1)}), bf16[64,80,128]{2,1,0:T(8,128)(2,1)S(1)}, u32[]{:S(2)}, u32[]{:S(2)}) async-start(bf16[64,80,128]{2,1,0:T(8,128)(2,1)} %get-tuple-element.35), calls=%async_computation.2 | async-start | bytes 2621440 | tf_op jit(solution)/shard_map/all_to_all | solution.py:490
  200.3 33.1 %all-to-all-done.2 = bf16[64,80,128]{2,1,0:T(8,128)(2,1)S(1)} async-done(((bf16[64,80,128]{2,1,0:T(8,128)(2,1)}), bf16[64,80,128]{2,1,0:T(8,128)(2,1)S(1)}, u32[]{:S(2)}, u32[]{:S(2)}) %all-to-all-start.2) | async-done | bytes 1310752 | tf_op jit(solution)/shard_map/all_to_all | solution.py:490
  234.1 6.3 %all-to-all-start.7 = ((f32[8,48,128]{2,1,0:T(8,128)}), f32[8,48,128]{2,1,0:T(8,128)S(1)}, u32[]{:S(2)}, u32[]{:S(2)}) async-start(f32[8,48,128]{2,1,0:T(8,128)} %broadcast_in_dim.25), calls=%async_computation.7 | async-start | bytes 393216 | tf_op jit(solution)/shard_map/all_to_all | solution.py:438
  240.7 5.5 %all-to-all-done.7 = f32[8,48,128]{2,1,0:T(8,128)S(1)} async-done(((f32[8,48,128]{2,1,0:T(8,128)}), f32[8,48,128]{2,1,0:T(8,128)S(1)}, u32[]{:S(2)}, u32[]{:S(2)}) %all-to-all-start.7) | async-done | bytes 196640 | tf_op jit(solution)/shard_map/all_to_all | solution.py:438
  246.2 0.8 broadcast_in_dim.22
  246.9 5.5 %all-to-all-start.3 = ((bf16[16,80,128]{2,1,0:T(8,128)(2,1)}), bf16[16,80,128]{2,1,0:T(8,128)(2,1)S(1)}, u32[]{:S(2)}, u32[]{:S(2)}) async-start(bf16[16,80,128]{2,1,0:T(8,128)(2,1)} %broadcast_in_dim.22), calls=%async_computation.3 | async-start | bytes 655360 | tf_op jit(solution)/shard_map/all_to_all | solution.py:438
  253.7 3.6 %input_grad.1 = bf16[1,14,14,768]{3,2,1,0:T(8,128)(2,1)} custom-call(f32[1]{0:T(128)} %bitcast.1.factor_ref, f32[6,14,16,128]{3,2,1,0:T(8,128)S(1)} %get-tuple-element.34.conv_ref, bf16[49,768]{1,0:T(8,128)(2,1)S(1)} %copy-done.18, bf16[224,768]{1,0:T(8,128)(2,1)S(1)} %bitcast.39), custom_call_target="tpu_custom_call" | custom-call | tf_op jit(solution)/shard_map/input_grad/pallas_call | solution.py:380
  258.1 8.2 %all-to-all-done.3.mine_ref = bf16[16,80,128]{2,1,0:T(8,128)(2,1)S(1)} async-done(((bf16[16,80,128]{2,1,0:T(8,128)(2,1)}), bf16[16,80,128]{2,1,0:T(8,128)(2,1)S(1)}, u32[]{:S(2)}, u32[]{:S(2)}) %all-to-all-start.3) | async-done | bytes 327712 | tf_op jit(solution)/shard_map/all_to_all | solution.py:438
  266.4 3.7 %collective-permute-start.18 = (bf16[16,80,128]{2,1,0:T(8,128)(2,1)S(1)}, bf16[16,80,128]{2,1,0:T(8,128)(2,1)S(1)}, u32[]{:S(2)}, u32[]{:S(2)}) collective-permute-start(bf16[16,80,128]{2,1,0:T(8,128)(2,1)S(1)} %all-to-all-done.3.mine_ref), channel_id=1, source_target_pairs={{0,16},{16,0},{1,17},{17,1},{2,18},{18,2},{3,19},{19,3},{4,20},{20... | collective-permute-start | bytes 983048 | tf_op jit(solution)/shard_map/ppermute | solution.py:442
  272.0 1.1 unpack.1
  273.1 1.1 copy.26
  (92 shorter events, 9.0 us)
Async XLA Ops:
  7.2 5.5 %copy-start.26 = (f32[768]{0:T(1024)S(1)}, f32[768]{0:T(1024)}, u32[]{:S(2)}) copy-start(f32[768]{0:T(1024)} %param.15) | copy-start | bytes 9220
  7.2 5.5 %copy-start.2 = (bf16[1,14,14,768]{3,2,1,0:T(8,128)(2,1)S(1)}, bf16[1,14,14,768]{3,2,1,0:T(8,128)(2,1)}, u32[]{:S(2)}) copy-start(bf16[1,14,14,768]{3,2,1,0:T(8,128)(2,1)} %param.10) | copy-start | bytes 903172
  7.2 27.4 %copy-start.28 = (f32[4]{0:T(128)S(1)}, f32[4]{0:T(128)}, u32[]{:S(2)}) copy-start(f32[4]{0:T(128)} %param.13) | copy-start | bytes 52
  7.2 28.0 %copy-start.25 = (bf16[1,14,14,768]{3,2,1,0:T(8,128)(2,1)S(1)}, bf16[1,14,14,768]{3,2,1,0:T(8,128)(2,1)}, u32[]{:S(2)}) copy-start(bf16[1,14,14,768]{3,2,1,0:T(8,128)(2,1)} %param.11) | copy-start | bytes 903172
  7.2 61.7 %all-gather.2.cloned.1.call-start = ((), (), s32[]{:S(2)}) async-start(), calls=%async_computation.8 | async-start | bytes 1548288 | tf_op jit(solution)/shard_map/all_gather | solution.py:465
  8.5 1.0 copy-start.21
  9.5 0.7 copy-start.24
  10.2 55.0 %copy-start.27 = (f32[768]{0:T(1024)S(1)}, f32[768]{0:T(1024)}, u32[]{:S(2)}) copy-start(f32[768]{0:T(1024)} %param.19) | copy-start | bytes 9220
  12.7 22.6 %copy-start.17 = (bf16[49,768]{1,0:T(8,128)(2,1)}, bf16[49,768]{1,0:T(8,128)(2,1)S(1)}, u32[]{:S(2)}) copy-start(bf16[49,768]{1,0:T(8,128)(2,1)S(1)} %reshape.68.kernel_ref) | copy-start | bytes 225796
  15.5 0.7 copy-start.22
  16.2 51.2 %copy-start.19 = (f32[6,14,16,128]{3,2,1,0:T(8,128)}, f32[6,14,16,128]{3,2,1,0:T(8,128)S(1)}, u32[]{:S(2)}) copy-start(f32[6,14,16,128]{3,2,1,0:T(8,128)S(1)} %get-tuple-element.29.centred_ref) | copy-start | bytes 2064388
  16.2 24.3 %collective-permute-start.1 = (bf16[224,768]{1,0:T(8,128)(2,1)S(1)}, bf16[224,768]{1,0:T(8,128)(2,1)S(1)}, u32[]{:S(2)}, u32[]{:S(2)}) collective-permute-start(bf16[224,768]{1,0:T(8,128)(2,1)S(1)} %get-tuple-element.23.refs_0_), channel_id=1, source_target_pairs={{0,8},{8,32},{32,40},{40,0},{1,9},{9,33},{33,41},{41,1},{2,10},{10... | collective-permute-start | bytes 1032200 | tf_op jit(solution)/shard_map/ppermute | solution.py:446
  20.1 22.7 %collective-permute-start.3 = (bf16[224,768]{1,0:T(8,128)(2,1)S(1)}, bf16[224,768]{1,0:T(8,128)(2,1)S(1)}, u32[]{:S(2)}, u32[]{:S(2)}) collective-permute-start(bf16[224,768]{1,0:T(8,128)(2,1)S(1)} %get-tuple-element.23.refs_0_), channel_id=1, source_target_pairs={{0,32},{8,40},{32,0},{40,8},{1,33},{9,41},{33,1},{41,9},{2,34},{10... | collective-permute-start | bytes 1032200 | tf_op jit(solution)/shard_map/ppermute | solution.py:446
  24.5 21.4 %collective-permute-start.5 = (bf16[224,768]{1,0:T(8,128)(2,1)S(1)}, bf16[224,768]{1,0:T(8,128)(2,1)S(1)}, u32[]{:S(2)}, u32[]{:S(2)}) collective-permute-start(bf16[224,768]{1,0:T(8,128)(2,1)S(1)} %get-tuple-element.23.refs_0_), channel_id=1, source_target_pairs={{0,40},{8,0},{32,8},{40,32},{1,41},{9,1},{33,9},{41,33},{2,42},{10... | collective-permute-start | bytes 1032200 | tf_op jit(solution)/shard_map/ppermute | solution.py:446
  27.6 21.1 %collective-permute-start = (bf16[224,768]{1,0:T(8,128)(2,1)S(1)}, bf16[224,768]{1,0:T(8,128)(2,1)S(1)}, u32[]{:S(2)}, u32[]{:S(2)}) collective-permute-start(bf16[224,768]{1,0:T(8,128)(2,1)S(1)} %get-tuple-element.23.refs_0_), channel_id=1, source_target_pairs={{0,16},{16,0},{1,17},{17,1},{2,18},{18,2},{3,19},{19,3},{4,20},{20... | collective-permute-start | bytes 1032200 | tf_op jit(solution)/shard_map/ppermute | solution.py:442
  36.0 14.6 %collective-permute-start.10 = (bf16[224,768]{1,0:T(8,128)(2,1)S(1)}, bf16[224,768]{1,0:T(8,128)(2,1)S(1)}, u32[]{:S(2)}, u32[]{:S(2)}) collective-permute-start(bf16[224,768]{1,0:T(8,128)(2,1)S(1)} %bitcast.33), channel_id=1, source_target_pairs={{0,32},{8,40},{32,0},{40,8},{1,33},{9,41},{33,1},{41,9},{2,34},{10... | collective-permute-start | bytes 1032200 | tf_op jit(solution)/shard_map/ppermute | solution.py:446
  40.6 14.2 %collective-permute-start.12 = (bf16[224,768]{1,0:T(8,128)(2,1)S(1)}, bf16[224,768]{1,0:T(8,128)(2,1)S(1)}, u32[]{:S(2)}, u32[]{:S(2)}) collective-permute-start(bf16[224,768]{1,0:T(8,128)(2,1)S(1)} %bitcast.34), channel_id=1, source_target_pairs={{0,40},{8,0},{32,8},{40,32},{1,41},{9,1},{33,9},{41,33},{2,42},{10... | collective-permute-start | bytes 1032200 | tf_op jit(solution)/shard_map/ppermute | solution.py:446
  42.8 14.6 %collective-permute-start.8 = (bf16[224,768]{1,0:T(8,128)(2,1)S(1)}, bf16[224,768]{1,0:T(8,128)(2,1)S(1)}, u32[]{:S(2)}, u32[]{:S(2)}) collective-permute-start(bf16[224,768]{1,0:T(8,128)(2,1)S(1)} %bitcast.35), channel_id=1, source_target_pairs={{0,8},{8,32},{32,40},{40,0},{1,9},{9,33},{33,41},{41,1},{2,10},{10... | collective-permute-start | bytes 1032200 | tf_op jit(solution)/shard_map/ppermute | solution.py:446
  45.9 13.4 %collective-permute-start.7 = (bf16[224,768]{1,0:T(8,128)(2,1)S(1)}, bf16[224,768]{1,0:T(8,128)(2,1)S(1)}, u32[]{:S(2)}, u32[]{:S(2)}) collective-permute-start(bf16[224,768]{1,0:T(8,128)(2,1)S(1)} %bitcast.36), channel_id=1, source_target_pairs={{0,16},{16,0},{1,17},{17,1},{2,18},{18,2},{3,19},{19,3},{4,20},{20... | collective-permute-start | bytes 1032200 | tf_op jit(solution)/shard_map/ppermute | solution.py:442
  48.6 13.8 %collective-permute-start.2 = (bf16[224,768]{1,0:T(8,128)(2,1)S(1)}, bf16[224,768]{1,0:T(8,128)(2,1)S(1)}, u32[]{:S(2)}, u32[]{:S(2)}) collective-permute-start(bf16[224,768]{1,0:T(8,128)(2,1)S(1)} %collective-permute-done.1.refs_2_), channel_id=1, source_target_pairs={{0,16},{16,0},{1,17},{17,1},{2,18},{18,2},{3,19},{19,3},{4,20},{20... | collective-permute-start | bytes 1032200 | tf_op jit(solution)/shard_map/ppermute | solution.py:442
  50.6 14.6 %collective-permute-start.4 = (bf16[224,768]{1,0:T(8,128)(2,1)S(1)}, bf16[224,768]{1,0:T(8,128)(2,1)S(1)}, u32[]{:S(2)}, u32[]{:S(2)}) collective-permute-start(bf16[224,768]{1,0:T(8,128)(2,1)S(1)} %collective-permute-done.3.refs_4_), channel_id=1, source_target_pairs={{0,16},{16,0},{1,17},{17,1},{2,18},{18,2},{3,19},{19,3},{4,20},{20... | collective-permute-start | bytes 1032200 | tf_op jit(solution)/shard_map/ppermute | solution.py:442
  54.8 11.1 %collective-permute-start.6 = (bf16[224,768]{1,0:T(8,128)(2,1)S(1)}, bf16[224,768]{1,0:T(8,128)(2,1)S(1)}, u32[]{:S(2)}, u32[]{:S(2)}) collective-permute-start(bf16[224,768]{1,0:T(8,128)(2,1)S(1)} %collective-permute-done.5.refs_6_), channel_id=1, source_target_pairs={{0,16},{16,0},{1,17},{17,1},{2,18},{18,2},{3,19},{19,3},{4,20},{20... | collective-permute-start | bytes 1032200 | tf_op jit(solution)/shard_map/ppermute | solution.py:442
  57.4 9.3 %collective-permute-start.11 = (bf16[224,768]{1,0:T(8,128)(2,1)S(1)}, bf16[224,768]{1,0:T(8,128)(2,1)S(1)}, u32[]{:S(2)}, u32[]{:S(2)}) collective-permute-start(bf16[224,768]{1,0:T(8,128)(2,1)S(1)} %collective-permute-done.10.refs_12_), channel_id=1, source_target_pairs={{0,16},{16,0},{1,17},{17,1},{2,18},{18,2},{3,19},{19,3},{4,20},{20... | collective-permute-start | bytes 1032200 | tf_op jit(solution)/shard_map/ppermute | solution.py:442
  59.3 0.8 copy-start.3
  60.1 7.3 %collective-permute-start.13 = (bf16[224,768]{1,0:T(8,128)(2,1)S(1)}, bf16[224,768]{1,0:T(8,128)(2,1)S(1)}, u32[]{:S(2)}, u32[]{:S(2)}) collective-permute-start(bf16[224,768]{1,0:T(8,128)(2,1)S(1)} %collective-permute-done.12.refs_14_), channel_id=1, source_target_pairs={{0,16},{16,0},{1,17},{17,1},{2,18},{18,2},{3,19},{19,3},{4,20},{20... | collective-permute-start | bytes 1032200 | tf_op jit(solution)/shard_map/ppermute | solution.py:442
  62.5 0.7 copy-start.5
  63.2 4.9 %collective-permute-start.9 = (bf16[224,768]{1,0:T(8,128)(2,1)S(1)}, bf16[224,768]{1,0:T(8,128)(2,1)S(1)}, u32[]{:S(2)}, u32[]{:S(2)}) collective-permute-start(bf16[224,768]{1,0:T(8,128)(2,1)S(1)} %collective-permute-done.8.refs_10_), channel_id=1, source_target_pairs={{0,16},{16,0},{1,17},{17,1},{2,18},{18,2},{3,19},{19,3},{4,20},{20... | collective-permute-start | bytes 1032200 | tf_op jit(solution)/shard_map/ppermute | solution.py:442
  65.2 0.7 copy-start.7
  65.9 0.7 copy-start.9
  66.6 0.7 copy-start.11
  67.4 0.7 copy-start.13
  68.1 0.7 copy-start.15
  68.9 1.0 copy-start.4
  69.8 1.0 copy-start.6
  70.8 1.0 copy-start.8
  71.8 1.0 copy-start.10
  72.8 1.0 copy-start.12
  73.8 1.0 copy-start.14
  74.7 1.0 copy-start.16
  84.1 5.3 %collective-permute-start.14 = (bf16[4,224,768]{2,1,0:T(8,128)(2,1)}, bf16[4,224,768]{2,1,0:T(8,128)(2,1)S(1)}, u32[]{:S(2)}, u32[]{:S(2)}) collective-permute-start(bf16[4,224,768]{2,1,0:T(8,128)(2,1)} %get-tuple-element.25), channel_id=1, source_target_pairs={{0,16},{16,0},{1,17},{17,1},{2,18},{18,2},{3,19},{19,3},{4,20},{20... | collective-permute-start | bytes 4128776 | tf_op jit(solution)/shard_map/ppermute | solution.py:442
  89.5 1.3 copy-start
  91.0 16.5 %collective-permute-start.15 = (bf16[224,768]{1,0:T(8,128)(2,1)S(1)}, bf16[224,768]{1,0:T(8,128)(2,1)S(1)}, u32[]{:S(2)}, u32[]{:S(2)}) collective-permute-start(bf16[224,768]{1,0:T(8,128)(2,1)S(1)} %get-tuple-element.26), channel_id=1, source_target_pairs={{0,40},{8,0},{32,8},{40,32},{1,41},{9,1},{33,9},{41,33},{2,42},{10... | collective-permute-start | bytes 1032200 | tf_op jit(solution)/shard_map/ppermute | solution.py:446
  95.3 12.4 %collective-permute-start.16 = (bf16[224,768]{1,0:T(8,128)(2,1)S(1)}, bf16[224,768]{1,0:T(8,128)(2,1)S(1)}, u32[]{:S(2)}, u32[]{:S(2)}) collective-permute-start(bf16[224,768]{1,0:T(8,128)(2,1)S(1)} %get-tuple-element.27), channel_id=1, source_target_pairs={{0,32},{8,40},{32,0},{40,8},{1,33},{9,41},{33,1},{41,9},{2,34},{10... | collective-permute-start | bytes 1032200 | tf_op jit(solution)/shard_map/ppermute | solution.py:446
  99.0 17.1 %collective-permute-start.17 = (bf16[224,768]{1,0:T(8,128)(2,1)S(1)}, bf16[224,768]{1,0:T(8,128)(2,1)S(1)}, u32[]{:S(2)}, u32[]{:S(2)}) collective-permute-start(bf16[224,768]{1,0:T(8,128)(2,1)S(1)} %get-tuple-element.28), channel_id=1, source_target_pairs={{0,8},{8,32},{32,40},{40,0},{1,9},{9,33},{33,41},{41,1},{2,10},{10... | collective-permute-start | bytes 1032200 | tf_op jit(solution)/shard_map/ppermute | solution.py:446
  101.1 14.9 %copy-start.1 = (bf16[4,224,768]{2,1,0:T(8,128)(2,1)S(1)}, bf16[4,224,768]{2,1,0:T(8,128)(2,1)}, u32[]{:S(2)}) copy-start(bf16[4,224,768]{2,1,0:T(8,128)(2,1)} %get-tuple-element.24.mine_ref) | copy-start | bytes 4128772
  101.1 14.9 %copy-start.20 = (f32[6,14,16,128]{3,2,1,0:T(8,128)S(1)}, f32[6,14,16,128]{3,2,1,0:T(8,128)}, u32[]{:S(2)}) copy-start(f32[6,14,16,128]{3,2,1,0:T(8,128)} %copy-done.19) | copy-start | bytes 2064388
  101.1 14.9 %copy-start.23 = (f32[14,16,128]{2,1,0:T(8,128)S(1)}, f32[14,16,128]{2,1,0:T(8,128)}, u32[]{:S(2)}) copy-start(f32[14,16,128]{2,1,0:T(8,128)} %copy-done.22) | copy-start | bytes 344068
  129.9 17.1 %all-to-all-start = ((f32[16,8,128]{2,1,0:T(8,128)}), f32[16,8,128]{2,1,0:T(8,128)S(1)}, u32[]{:S(2)}, u32[]{:S(2)}) async-start(f32[16,8,128]{2,1,0:T(8,128)} %broadcast_in_dim_broadcast_in_dim.3), calls=%async_computation | async-start | bytes 131072 | tf_op jit(solution)/shard_map/all_to_all | solution.py:438
  147.6 15.6 %all-to-all-start.5 = ((f32[8,48,128]{2,1,0:T(8,128)}), f32[8,48,128]{2,1,0:T(8,128)S(1)}, u32[]{:S(2)}, u32[]{:S(2)}) async-start(f32[8,48,128]{2,1,0:T(8,128)} %broadcast_in_dim.23), calls=%async_computation.5 | async-start | bytes 393216 | tf_op jit(solution)/shard_map/all_to_all | solution.py:438
  163.8 18.4 %all-to-all-start.1 = ((f32[32,8,128]{2,1,0:T(8,128)}), f32[32,8,128]{2,1,0:T(8,128)S(1)}, u32[]{:S(2)}, u32[]{:S(2)}) async-start(f32[32,8,128]{2,1,0:T(8,128)} %broadcast_in_dim.21), calls=%async_computation.1 | async-start | bytes 262144 | tf_op jit(solution)/shard_map/all_to_all | solution.py:438
  195.6 37.8 %all-to-all-start.2 = ((bf16[64,80,128]{2,1,0:T(8,128)(2,1)}), bf16[64,80,128]{2,1,0:T(8,128)(2,1)S(1)}, u32[]{:S(2)}, u32[]{:S(2)}) async-start(bf16[64,80,128]{2,1,0:T(8,128)(2,1)} %get-tuple-element.35), calls=%async_computation.2 | async-start | bytes 2621440 | tf_op jit(solution)/shard_map/all_to_all | solution.py:490
  234.1 19.6 %copy-start.18 = (bf16[49,768]{1,0:T(8,128)(2,1)S(1)}, bf16[49,768]{1,0:T(8,128)(2,1)}, u32[]{:S(2)}) copy-start(bf16[49,768]{1,0:T(8,128)(2,1)} %copy-done.17) | copy-start | bytes 225796
  234.1 12.0 %all-to-all-start.7 = ((f32[8,48,128]{2,1,0:T(8,128)}), f32[8,48,128]{2,1,0:T(8,128)S(1)}, u32[]{:S(2)}, u32[]{:S(2)}) async-start(f32[8,48,128]{2,1,0:T(8,128)} %broadcast_in_dim.25), calls=%async_computation.7 | async-start | bytes 393216 | tf_op jit(solution)/shard_map/all_to_all | solution.py:438
  246.9 19.4 %all-to-all-start.3 = ((bf16[16,80,128]{2,1,0:T(8,128)(2,1)}), bf16[16,80,128]{2,1,0:T(8,128)(2,1)S(1)}, u32[]{:S(2)}, u32[]{:S(2)}) async-start(bf16[16,80,128]{2,1,0:T(8,128)(2,1)} %broadcast_in_dim.22), calls=%async_computation.3 | async-start | bytes 655360 | tf_op jit(solution)/shard_map/all_to_all | solution.py:438
  266.4 4.9 %collective-permute-start.18 = (bf16[16,80,128]{2,1,0:T(8,128)(2,1)S(1)}, bf16[16,80,128]{2,1,0:T(8,128)(2,1)S(1)}, u32[]{:S(2)}, u32[]{:S(2)}) collective-permute-start(bf16[16,80,128]{2,1,0:T(8,128)(2,1)S(1)} %all-to-all-done.3.mine_ref), channel_id=1, source_target_pairs={{0,16},{16,0},{1,17},{17,1},{2,18},{18,2},{3,19},{19,3},{4,20},{20... | collective-permute-start | bytes 983048 | tf_op jit(solution)/shard_map/ppermute | solution.py:442
Sparse Core Ops, SparseCore 0:
  11.9 43.9 all-gather.1

commit v2 on v1

v2 whole, which is shorter than its diff:
```python
import jax
import jax.numpy as jnp
import numpy as np
from jax import lax
from jax.experimental import pallas as pl
from jax.experimental.pallas import tpu as pltpu
from jax.sharding import Mesh, PartitionSpec as P

F32 = jnp.float32
BF16 = jnp.bfloat16
ROWS = 14
COLS = 14
WIDE = 16
PIX = ROWS * WIDE
CH = 768
LANES = 128
BLOCKS = CH // LANES
OWN = 48
HALF = 384
PACK = 64
REPLICA = ("y", "xh", "core")
SHARD = ("xl", "z")
RING = ("xh", "xl")
TEAM = ("core", "xl", "xh")
INTERPRET = False


def params(limit_mib, **more):
    return pltpu.CompilerParams(vmem_limit_bytes=limit_mib * 1024 * 1024, **more)


def nt(left, right):
    return lax.dot_general(left, right, (((1,), (1,)), ((), ())), preferred_element_type=F32)


def tn(left, right):
    return lax.dot_general(left, right, (((0,), (0,)), ((), ())), preferred_element_type=F32)


def whole():
    return pl.BlockSpec(memory_space=pltpu.VMEM)


def scalars():
    return pl.BlockSpec(memory_space=pltpu.SMEM)


def pack_kernel(place_ref, first_ref, bias_ref, second_ref, one_ref, two_ref):
    block = place_ref[0]
    column = place_ref[1]
    row = lax.broadcasted_iota(jnp.int32, (2 * OWN, 192), 0)
    lane = lax.broadcasted_iota(jnp.int32, (2 * OWN, 192), 1)
    partner = block + 1 - 2 * lax.rem(block, 2)
    wanted = jnp.where(row < OWN, row + block * OWN, row - OWN + partner * OWN)
    pick = (lane == wanted).astype(BF16)
    one_ref[0:OWN, :] = nt(pick[0:OWN], first_ref[...]).astype(BF16)
    two_ref[...] = jnp.dot(pick, second_ref[...], preferred_element_type=F32).astype(BF16)
    unit = lax.broadcasted_iota(jnp.int32, (192, HALF), 0) - block * OWN
    spot = lax.broadcasted_iota(jnp.int32, (192, HALF), 1) - column * OWN
    put = ((unit == spot) & (unit >= 0) & (unit < OWN)).astype(BF16)
    bias = jnp.broadcast_to(bias_ref[...], (16, 192))
    high = bias.astype(BF16)
    low = (bias - high.astype(F32)).astype(BF16)
    one_ref[OWN:PACK, 0:HALF] = jnp.dot(high, put, preferred_element_type=F32).astype(BF16)
    one_ref[OWN:PACK, HALF:CH] = jnp.dot(low, put, preferred_element_type=F32).astype(BF16)


def pack_weights(place, first_weight, first_bias, second_weight):
    return pl.pallas_call(
        pack_kernel,
        out_shape=(jax.ShapeDtypeStruct((PACK, CH), BF16), jax.ShapeDtypeStruct((2 * OWN, CH), BF16)),
        in_specs=[scalars(), whole(), whole(), whole()],
        out_specs=(whole(), whole()),
        compiler_params=params(8),
        interpret=INTERPRET,
        name="pack",
    )(place, first_weight, first_bias.reshape(1, 192), second_weight)


def taps_sum(padded_ref, kernel, flip):
    halves = []
    for half in range(2):
        total = jnp.zeros((7, WIDE, LANES), F32)
        for b in range(7):
            moved = padded_ref[half * 7 : half * 7 + 13, b : b + WIDE, :]
            for a in range(7):
                tap = (6 - a) * 7 + (6 - b) if flip else a * 7 + b
                total = total + moved[a : a + 7] * kernel[tap : tap + 1, :].reshape(1, 1, LANES)
        halves.append(total)
    return halves


def column_mask():
    return (lax.broadcasted_iota(jnp.int32, (ROWS, WIDE, LANES), 1) < COLS).astype(F32)


def forward_kernel(image_ref, kernel_ref, gain_ref, normed_ref, centred_ref, inv_ref, padded, conv):
    j = pl.program_id(0)

    @pl.when(j == 0)
    def _():
        padded[...] = jnp.zeros_like(padded)

    padded[3:17, 3:17, :] = image_ref[...].astype(F32)
    halves = taps_sum(padded, kernel_ref[...].astype(F32), False)
    conv[j, 0:7] = halves[0]
    conv[j, 7:14] = halves[1]

    @pl.when(j == BLOCKS - 1)
    def _():
        mask = column_mask()
        total = conv[0]
        for i in range(1, BLOCKS):
            total = total + conv[i]
        mean = jnp.sum(total, axis=-1, keepdims=True) * (1.0 / CH)
        square = jnp.zeros((ROWS, WIDE, LANES), F32)
        for i in range(BLOCKS):
            part = conv[i] - mean
            square = square + part * part
        inv = lax.rsqrt(jnp.sum(square, axis=-1, keepdims=True) * (1.0 / CH) + 1e-06)
        inv_ref[...] = jnp.broadcast_to(inv, (ROWS, WIDE, LANES))
        for i in range(BLOCKS):
            part = (conv[i] - mean) * inv * mask
            centred_ref[i] = part
            lanes = slice(i * LANES, (i + 1) * LANES)
            gain = gain_ref[:, lanes].reshape(1, 1, LANES)
            normed_ref[:, lanes] = (part * gain).reshape(PIX, LANES).astype(BF16)


def forward(image, kernel, gain):
    return pl.pallas_call(
        forward_kernel,
        grid=(BLOCKS,),
        out_shape=(
            jax.ShapeDtypeStruct((PIX, CH), BF16),
            jax.ShapeDtypeStruct((BLOCKS, ROWS, WIDE, LANES), F32),
            jax.ShapeDtypeStruct((ROWS, WIDE, LANES), F32),
        ),
        in_specs=[
            pl.BlockSpec((ROWS, COLS, LANES), lambda j: (0, 0, j)),
            pl.BlockSpec((49, LANES), lambda j: (0, j)),
            pl.BlockSpec((1, CH), lambda j: (0, 0)),
        ],
        out_specs=(
            pl.BlockSpec((PIX, CH), lambda j: (0, 0)),
            pl.BlockSpec((BLOCKS, ROWS, WIDE, LANES), lambda j: (0, 0, 0, 0)),
            pl.BlockSpec((ROWS, WIDE, LANES), lambda j: (0, 0, 0)),
        ),
        scratch_shapes=[
            pltpu.VMEM((20, 24, LANES), F32),
            pltpu.VMEM((BLOCKS, ROWS, WIDE, LANES), F32),
        ],
        compiler_params=params(24),
        interpret=INTERPRET,
        name="conv_norm",
    )(image, kernel, gain)


def first_of(mine_ref, other_ref):
    return jnp.concatenate(
        [ref[:, 0:OWN, :].reshape(HALF, CH) for ref in (mine_ref, other_ref)], axis=0
    )


def second_of(two_ref):
    return jnp.concatenate(
        [two_ref[:, k * OWN : (k + 1) * OWN, :].reshape(HALF, CH) for k in range(2)], axis=0
    )


def activation_kernel(*refs):
    normed = refs[0:4]
    mine_ref, other_ref, act_ref, slope_ref = refs[4:8]
    first = first_of(mine_ref, other_ref)
    biases = []
    for ref in (mine_ref, other_ref):
        bias = jnp.sum(ref[:, OWN:PACK, :].astype(F32), axis=0)[0:1, :]
        biases.append(bias[:, 0:HALF] + bias[:, HALF:CH])
    bias = jnp.concatenate(biases, axis=1)
    for i in range(4):
        preact = nt(normed[i][...], first) + bias
        cumulative = 0.5 * (1.0 + lax.erf(preact * 0.7071067811865476))
        slope_ref[i] = cumulative + preact * jnp.exp(-0.5 * preact * preact) * 0.3989422804014327
        act_ref[i] = (preact * cumulative).astype(BF16)


def activations(normed, mine, other):
    return pl.pallas_call(
        activation_kernel,
        out_shape=(
            jax.ShapeDtypeStruct((4, PIX, CH), BF16),
            jax.ShapeDtypeStruct((4, PIX, CH), F32),
        ),
        in_specs=[whole()] * 6,
        out_specs=(whole(),) * 2,
        compiler_params=params(16),
        interpret=INTERPRET,
        name="activations",
    )(*normed, mine, other)


def hidden_kernel(*refs):
    scaled = refs[0:4]
    mine_ref, other_ref, two_ref, layer_ref, slope_ref = refs[4:9]
    grad_ref = refs[9]
    parts = refs[10:14]
    first = first_of(mine_ref, other_ref)
    second = second_of(two_ref)
    layer = layer_ref[...]
    for i in (2, 1, 3, 0):
        branch_grad = (scaled[i][...].astype(F32) * layer).astype(BF16)
        preact_grad = (nt(branch_grad, second) * slope_ref[i]).astype(BF16)
        grad_ref[i] = preact_grad
        parts[i][...] = jnp.dot(preact_grad, first, preferred_element_type=F32).astype(BF16)


def hidden(scaled, mine, other, two, layer, slope):
    return pl.pallas_call(
        hidden_kernel,
        out_shape=(jax.ShapeDtypeStruct((4, PIX, CH), BF16),)
        + (jax.ShapeDtypeStruct((PIX, CH), BF16),) * 4,
        in_specs=[whole()] * 9,
        out_specs=(whole(),) * 5,
        compiler_params=params(16),
        interpret=INTERPRET,
        name="hidden",
    )(*scaled, mine, other, two, layer, slope)


def weights_kernel(*refs):
    normed = refs[0:4]
    scaled = refs[4:8]
    act_ref, grad_ref, two_ref, layer_ref = refs[8:12]
    outs = refs[12:14]
    scale_ref = refs[14]
    product = tn(
        act_ref[...].reshape(4 * PIX, CH), jnp.concatenate([ref[...] for ref in scaled], axis=0)
    )
    weighted = second_of(two_ref).astype(F32) * product
    scale_ref[...] = jnp.sum(weighted.reshape(CH // 8, 8, CH), axis=0)
    product = (product * layer_ref[...]).astype(BF16)
    for half in range(2):
        spread(outs[half], product[half * HALF : (half + 1) * HALF], 0)
    product = tn(
        grad_ref[...].reshape(4 * PIX, CH), jnp.concatenate([ref[...] for ref in normed], axis=0)
    ).astype(BF16)
    for half in range(2):
        spread(outs[half], product[half * HALF : (half + 1) * HALF], 18)
    ones = jnp.ones((16, 4 * PIX), BF16)
    bias = jnp.dot(ones, grad_ref[...].reshape(4 * PIX, CH), preferred_element_type=F32)
    row = lax.broadcasted_iota(jnp.int32, (16, LANES), 0)
    empty = jnp.zeros((16, LANES), BF16)
    for half in range(2):
        block = jnp.zeros((16, LANES), F32)
        for k in range(3):
            start = half * HALF + k * LANES
            block = jnp.where(row == k, bias[:, start : start + LANES], block)
        block = block.astype(BF16)
        for z in range(8):
            for s in range(36, 40):
                outs[half][(s // 5) * 8 + z, (s % 5) * 16 : (s % 5) * 16 + 16, :] = block if s == 36 else empty


def spread(out_ref, matrix, start):
    for z in range(8):
        for j in range(BLOCKS):
            for part in range(3):
                s = start + j * 3 + part
                row = z * OWN + part * 16
                out_ref[(s // 5) * 8 + z, (s % 5) * 16 : (s % 5) * 16 + 16, :] = matrix[
                    row : row + 16, j * LANES : (j + 1) * LANES
                ]


def weight_grads(normed, scaled, act, grad, two, layer):
    return pl.pallas_call(
        weights_kernel,
        out_shape=(
            jax.ShapeDtypeStruct((64, 80, LANES), BF16),
            jax.ShapeDtypeStruct((64, 80, LANES), BF16),
            jax.ShapeDtypeStruct((8, CH), F32),
        ),
        in_specs=[whole()] * 12,
        out_specs=(whole(),) * 3,
        compiler_params=params(24),
        interpret=INTERPRET,
        name="weight_grads",
    )(*normed, *scaled, act, grad, two, layer)


def backward_kernel(
    weight_ref, zero_ref, one_ref, two_ref, three_ref, centred_ref, inv_ref, gain_ref, scale_ref, image_ref,
    sums_ref, conv_ref, padded, conv, parts, gains,
):
    j = pl.program_id(0)

    @pl.when(j == 0)
    def _():
        padded[...] = jnp.zeros_like(padded)
        first = jnp.zeros((ROWS, WIDE, LANES), F32)
        second = jnp.zeros((ROWS, WIDE, LANES), F32)
        for i in range(BLOCKS):
            lanes = slice(i * LANES, (i + 1) * LANES)
            grad = (
                zero_ref[:, lanes].astype(F32)
                + one_ref[:, lanes].astype(F32)
                + two_ref[:, lanes].astype(F32)
                + three_ref[:, lanes].astype(F32)
            ).reshape(ROWS, WIDE, LANES)
            centred = centred_ref[i]
            product = grad * centred
            gains[i] = jnp.sum(jnp.sum(product, axis=0).reshape(2, 8, LANES), axis=0)
            gain = gain_ref[:, lanes].reshape(1, 1, LANES)
            gained = grad * gain
            conv[i] = gained
            first = first + gained
            second = second + product * gain
        mean = jnp.sum(first, axis=-1, keepdims=True) * (1.0 / CH)
        slant = jnp.sum(second, axis=-1, keepdims=True) * (1.0 / CH)
        inv = inv_ref[...] * column_mask()
        for i in range(BLOCKS):
            conv[i] = inv * (conv[i] - mean - centred_ref[i] * slant)

    padded[3:17, 3:17, :] = image_ref[...].astype(F32)
    conv_ref[0] = conv[j]
    for half in range(2):
        signal = conv[j, half * 7 : half * 7 + 7]
        for b in range(7):
            moved = padded[half * 7 : half * 7 + 13, b : b + WIDE, :]
            for a in range(7):
                product = jnp.sum(signal * moved[a : a + 7], axis=0)
                product = product[0:8] + product[8:16]
                if half == 0:
                    parts[a * 7 + b] = product
                else:
                    parts[a * 7 + b] += product
    sums_ref[0] = jnp.zeros((64, LANES), F32)
    sums_ref[0, 0:49, :] = jnp.sum(parts[...], axis=1)
    sums_ref[0, 49:50, :] = jnp.sum(gains[j], axis=0, keepdims=True)
    sums_ref[0, 50:51, :] = jnp.sum(scale_ref[...], axis=0, keepdims=True)
    sums_ref[0, 51:52, :] = jnp.full((1, LANES), weight_ref[0], F32)


def backward(weight, zero, one, two, three, centred, inv, gain, scale, image):
    def fixed(*shape):
        return pl.BlockSpec(shape, lambda j: (0,) * len(shape))

    return pl.pallas_call(
        backward_kernel,
        grid=(BLOCKS,),
        out_shape=(
            jax.ShapeDtypeStruct((BLOCKS, 64, LANES), F32),
            jax.ShapeDtypeStruct((BLOCKS, ROWS, WIDE, LANES), F32),
        ),
        in_specs=[
            scalars(),
            fixed(PIX, CH),
            fixed(PIX, CH),
            fixed(PIX, CH),
            fixed(PIX, CH),
            fixed(BLOCKS, ROWS, WIDE, LANES),
            fixed(ROWS, WIDE, LANES),
            fixed(1, CH),
            pl.BlockSpec((8, LANES), lambda j: (0, j)),
            pl.BlockSpec((ROWS, COLS, LANES), lambda j: (0, 0, j)),
        ],
        out_specs=(
            pl.BlockSpec((1, 64, LANES), lambda j: (j, 0, 0)),
            pl.BlockSpec((1, ROWS, WIDE, LANES), lambda j: (j, 0, 0, 0)),
        ),
        scratch_shapes=[
            pltpu.VMEM((20, 24, LANES), F32),
            pltpu.VMEM((BLOCKS, ROWS, WIDE, LANES), F32),
            pltpu.VMEM((49, 8, LANES), F32),
            pltpu.VMEM((BLOCKS, 8, LANES), F32),
        ],
        compiler_params=params(32),
        interpret=INTERPRET,
        name="norm_back",
    )(weight, zero, one, two, three, centred, inv, gain, scale, image)


def input_kernel(conv_ref, kernel_ref, scaled_ref, out_ref, padded):
    @pl.when(pl.program_id(0) == 0)
    def _():
        padded[...] = jnp.zeros_like(padded)

    padded[3:17, 3 : 3 + WIDE, :] = conv_ref[0]
    halves = taps_sum(padded, kernel_ref[...].astype(F32), True)
    for half in range(2):
        rows = slice(half * 7 * WIDE, (half + 1) * 7 * WIDE)
        scaled = scaled_ref[rows, :].astype(F32).reshape(7, WIDE, LANES)
        out_ref[0, half * 7 : half * 7 + 7] = (scaled + halves[half])[:, 0:COLS, :]


def input_grad(conv, kernel, scaled):
    return pl.pallas_call(
        input_kernel,
        grid=(BLOCKS,),
        out_shape=jax.ShapeDtypeStruct((1, ROWS, COLS, CH), F32),
        in_specs=[
            pl.BlockSpec((1, ROWS, WIDE, LANES), lambda j: (j, 0, 0, 0)),
            pl.BlockSpec((49, LANES), lambda j: (0, j)),
            pl.BlockSpec((PIX, LANES), lambda j: (0, j)),
        ],
        out_specs=pl.BlockSpec((1, ROWS, COLS, LANES), lambda j: (0, 0, 0, j)),
        scratch_shapes=[pltpu.VMEM((20, 24, LANES), F32)],
        compiler_params=params(24),
        interpret=INTERPRET,
        name="input_grad",
    )(conv, kernel, scaled)


def unpack_kernel(factor_ref, core_ref, mine_ref, other_ref, first_ref, second_ref):
    factor = factor_ref[0]
    even = core_ref[0] == 0

    def column(kind, j):
        pieces = []
        for xh in range(2):
            own, got = [], []
            for part in range(3):
                s = kind * 18 + j * 3 + part
                rows = slice((s % 5) * 16, (s % 5) * 16 + 16)
                own.append(mine_ref[xh, s // 5, rows, :].astype(F32))
                got.append(other_ref[xh, s // 5, rows, :].astype(F32))
            own, got = jnp.concatenate(own), jnp.concatenate(got)
            pieces += [jnp.where(even, own, got), jnp.where(even, got, own)]
        return jnp.concatenate(pieces) * factor

    for j in range(BLOCKS):
        lanes = slice(j * LANES, (j + 1) * LANES)
        second_ref[:, lanes] = column(0, j)
        first_ref[lanes, :] = column(1, j).T


def unpack(factor, core, mine, other):
    return pl.pallas_call(
        unpack_kernel,
        out_shape=(
            jax.ShapeDtypeStruct((CH, 192), F32),
            jax.ShapeDtypeStruct((192, CH), F32),
        ),
        in_specs=[scalars(), scalars(), whole(), whole()],
        out_specs=(whole(),) * 2,
        compiler_params=params(16),
        interpret=INTERPRET,
        name="unpack",
    )(factor, core, mine, other)


def to_all(value, axes):
    count = lax.axis_size(axes)
    return lax.all_to_all(jnp.broadcast_to(value, (count, *value.shape)), axes, 0, 0, tiled=True)


def swap_core(value):
    return lax.ppermute(value, "core", [(0, 1), (1, 0)])


def ring(value, shift):
    return lax.ppermute(value, RING, [(i, (i + shift) % 4) for i in range(4)])


def ring_share(value):
    return [value] + [ring(value, r) for r in range(1, 4)]


def halve(value, axis):
    at = lax.axis_index(axis)
    keep = lax.dynamic_index_in_dim(value, at, 0, keepdims=False)
    send = lax.dynamic_index_in_dim(value, 1 - at, 0, keepdims=False)
    return keep + lax.ppermute(send, axis, [(0, 1), (1, 0)])


def per_device(
    image, upstream, group_ids, group_weights, conv_kernel, norm_gain, first_weight, first_bias, second_weight, layer_scale
):
    core = lax.axis_index("core")
    half = lax.axis_index("xh")
    column = lax.axis_index("z")
    place = jnp.stack([half * 2 + core, column]).astype(jnp.int32)
    one, two = pack_weights(place, first_weight, first_bias, second_weight)
    two = lax.all_gather(two, "z", axis=0, tiled=True).reshape(8, 2 * OWN, CH)
    one = to_all(one, "z")
    one_other = swap_core(one)

    kernel = conv_kernel.reshape(49, CH)
    gain = norm_gain.reshape(1, CH)
    layer = layer_scale.reshape(1, CH)
    normed, centred, inv = forward(image[0], kernel, gain)
    normed_all = ring_share(normed)

    labels = jnp.arange(group_weights.shape[0], dtype=jnp.int32)
    own_weight = jnp.sum(jnp.where(labels == group_ids[0], group_weights, 0.0))
    scaled = (own_weight * upstream[0].astype(F32)).astype(BF16)
    scaled = jnp.pad(scaled, ((0, 0), (0, WIDE - COLS), (0, 0))).reshape(PIX, CH)
    scaled_all = ring_share(scaled)

    act, slope = activations(normed_all, one, one_other)
    preact_grad, *parts = hidden(scaled_all, one, one_other, two, layer, slope)
    grads, other, scale = weight_grads(normed_all, scaled_all, act, preact_grad, two, layer)
    parts[1], parts[2], parts[3], other = lax.optimization_barrier((parts[1], parts[2], parts[3], other))
    got = swap_core(other)
    grads = (grads.astype(F32) + got.astype(F32)).astype(BF16)
    grads = lax.all_to_all(grads, ("y", "z"), 0, 0, tiled=True)
    grads = jnp.sum(grads.astype(F32), axis=0)

    returned = [ring(parts[r], 4 - r) for r in range(1, 4)]
    small, conv_grad = backward(own_weight.reshape(1), parts[0], *returned, centred, inv, gain, scale, image[0])
    small = small.reshape(2, 2, 2, OWN, LANES)
    small = halve(small, "core")
    small = halve(small, "xl")
    small = halve(small, "xh")
    small, grads = lax.optimization_barrier((small, grads))
    small = jnp.sum(to_all(small, "z"), axis=0)
    high = small.astype(BF16)
    low = (small - high.astype(F32)).astype(BF16)
    both = to_all(jnp.concatenate([grads.astype(BF16), high, low], axis=0), "y")
    small = jnp.sum(both[:, 80:128, :].astype(F32) + both[:, 128:176, :].astype(F32), axis=0)
    small = to_all(small, TEAM).reshape(BLOCKS, 64, LANES)
    small = small.transpose(1, 0, 2).reshape(64, CH)

    mine = both[:, 0:80, :]
    across = lax.ppermute(mine, "xh", [(0, 1), (1, 0)])
    mine = jnp.where(half == 0, jnp.stack([mine, across]), jnp.stack([across, mine]))
    other = swap_core(mine)

    images = lax.axis_size(REPLICA) * lax.axis_size(SHARD)
    factor = images / small[51, 0]
    grad_first, grad_second = unpack(factor.reshape(1), core.reshape(1).astype(jnp.int32), mine, other)

    def bias_of(gathered):
        rows = gathered[:, 7, 16:19, :].reshape(2, HALF).astype(F32)
        return lax.dynamic_slice(rows, (0, column * OWN), (2, OWN))

    bias_mine, bias_other = bias_of(mine), bias_of(other)
    bias = jnp.stack([jnp.where(core == 0, bias_mine, bias_other), jnp.where(core == 0, bias_other, bias_mine)], axis=1)
    grad_image = (factor * input_grad(conv_grad, kernel, scaled)).astype(BF16)
    small = factor * small
    return (
        grad_image,
        grad_first,
        factor * bias.reshape(4 * OWN),
        grad_second,
        small[0:49].reshape(7, 7, CH),
        small[49],
        small[50],
    )


def solution(mesh):
    fine = Mesh(mesh.devices.reshape(8, 2, 2, 2, 8), ("y", "xh", "core", "xl", "z"))
    images = P((*REPLICA, *SHARD), None, None, None)
    return jax.shard_map(
        per_device,
        mesh=fine,
        in_specs=(
            images,
            images,
            P((*REPLICA, *SHARD)),
            P(),
            P(),
            P(),
            P(None, SHARD),
            P(SHARD),
            P(SHARD, None),
            P(),
        ),
        out_specs=(images, P(None, SHARD), P(SHARD), P(SHARD, None), P(), P(), P()),
        check_vma=False,
    )
```

time: 283 us -> 235 us (0.83)
  starting transfers between devices: 100 us -> 73.9 us
  waiting for transfers between devices: 87.8 us -> 63.6 us
  blocking collectives: 22.7 us -> 31.5 us
  Pallas kernels: 27.2 us -> 20.2 us
  other arithmetic: 1.8 us -> 5.39 us
    all_to_all x1, waiting for transfers between devices: 33.1 us -> 0.01 us  [per_device(): grads = lax.all_to_all(grads, ('y', 'z'), 0, 0, tiled=True)]
    ppermute x10 -> x3, starting transfers between devices: 28.3 us -> 7.41 us  [swap_core(): return lax.ppermute(value, 'core', [(0, 1), (1, 0)])]
    all_to_all x1 -> x2, blocking collectives: 13.4 us -> 31.5 us  [to_all(): lax.all_to_all(jnp.broadcast_to(value, (count, *value.shape)), axes, 0, 0...]
    ppermute x9, waiting for transfers between devices: 10.4 us -> 27.3 us  [ring(): return lax.ppermute(value, RING, [(i, (i + shift) % 4) for i in range(4)])]
    all_to_all x5 -> x2, starting transfers between devices: 35.8 us -> 19.9 us  [to_all(): lax.all_to_all(jnp.broadcast_to(value, (count, *value.shape)), axes, 0, 0...]
    all_to_all x5 -> x2, waiting for transfers between devices: 40.8 us -> 26.6 us  [to_all(): lax.all_to_all(jnp.broadcast_to(value, (count, *value.shape)), axes, 0, 0...]
    ppermute x0 -> x4, starting transfers between devices: none -> 11.2 us  [the longest x3 7.8 us: halve(): return keep + lax.ppermute(send, axis, [(0, 1), (1, 0)])]
    all_to_all x1 -> x0, blocking collectives: 9.3 us -> none  [per_device(): small = lax.all_to_all(small.reshape(8, OWN, LANES), TEAM, 0, 0, tiled=True)]
  transfers between devices with their start and end apart: 26 -> 20, of which waited for: 11 -> 13; matrix products, arithmetic and copies ran while one was open for 2% -> 2% of each run, Pallas kernels for 5% -> 5%
where the time goes in v2:
time: 235 us; the launch traced here: 234 us
  starting transfers between devices  73.9 us (31%)
  waiting for transfers between devices  63.6 us (27%)
  blocking collectives  31.5 us (13%)
  local copies, waits for them, and re-layouts  23.1 us (10%)
  Pallas kernels  20.2 us (9%)
  between operations  15.9 us (7%)
  other arithmetic  5.39 us (2%)
    all_to_all x2, blocking collectives, to_all(): lax.all_to_all(jnp.broadcast_to(value, (count, *value.shape)), axes, 0, 0...  31.5 us
    ppermute x9, waiting for transfers between devices, ring(): return lax.ppermute(value, RING, [(i, (i + shift) % 4) for i in range(4)])  27.3 us
    ppermute x9, starting transfers between devices, ring(): return lax.ppermute(value, RING, [(i, (i + shift) % 4) for i in range(4)])  27 us
    all_to_all x2, waiting for transfers between devices, to_all(): lax.all_to_all(jnp.broadcast_to(value, (count, *value.shape)), axes, 0, 0...  26.6 us
    all_to_all x2, starting transfers between devices, to_all(): lax.all_to_all(jnp.broadcast_to(value, (count, *value.shape)), axes, 0, 0...  19.9 us
    unnamed x70, local copies, waits for them, and re-layouts  18.7 us
    all_to_all x1, starting transfers between devices, per_device(): grads = lax.all_to_all(grads, ('y', 'z'), 0, 0, tiled=True)  8.29 us
    ppermute x3, starting transfers between devices, halve(): return keep + lax.ppermute(send, axis, [(0, 1), (1, 0)])  7.8 us
  transfers between devices with their start and end apart: 20, of which 13 were waited for; matrix products, arithmetic and copies ran while one was open for 2% of the time, Pallas kernels for 5%

profile of v2, /device:TPU:1, one launch (start us, length us, event | category | flops | bytes accessed | tf_op | source)
XLA Modules:
  0.0 233.5 jit_solution(1117086338336707159)
XLA Ops:
  7.2 1.1 copy.23.first_ref
  8.4 1.0 copy-done.24
  10.0 1.5 pack.1
  11.5 0.9 broadcast_in_dim.17
  12.5 11.0 %all-to-all-start = ((bf16[8,64,768]{2,1,0:T(8,128)(2,1)}), bf16[8,64,768]{2,1,0:T(8,128)(2,1)S(1)}, u32[]{:S(2)}, u32[]{:S(2)}) async-start(bf16[8,64,768]{2,1,0:T(8,128)(2,1)} %broadcast_in_dim.17), calls=%async_computation | async-start | bytes 1572864 | tf_op jit(solution)/shard_map/all_to_all | solution.py:454
  24.2 22.8 %all-to-all-done.refs_4_ = bf16[8,64,768]{2,1,0:T(8,128)(2,1)S(1)} async-done(((bf16[8,64,768]{2,1,0:T(8,128)(2,1)}), bf16[8,64,768]{2,1,0:T(8,128)(2,1)S(1)}, u32[]{:S(2)}, u32[]{:S(2)}) %all-to-all-start) | async-done | bytes 786464 | tf_op jit(solution)/shard_map/all_to_all | solution.py:454
  47.1 2.4 %collective-permute-start.3 = (bf16[8,64,768]{2,1,0:T(8,128)(2,1)S(1)}, bf16[8,64,768]{2,1,0:T(8,128)(2,1)S(1)}, u32[]{:S(2)}, u32[]{:S(2)}) collective-permute-start(bf16[8,64,768]{2,1,0:T(8,128)(2,1)S(1)} %all-to-all-done.refs_4_), channel_id=1, source_target_pairs={{0,16},{16,0},{1,17},{17,1},{2,18},{18,2},{3,19},{19,3},{4,20},{20... | collective-permute-start | bytes 2359304 | tf_op jit(solution)/shard_map/ppermute | solution.py:458
  49.6 2.8 %conv_norm.1 = (bf16[224,768]{1,0:T(8,128)(2,1)S(1)}, f32[6,14,16,128]{3,2,1,0:T(8,128)S(1)}, f32[14,16,128]{2,1,0:T(8,128)S(1)}) custom-call(bf16[14,14,768]{2,1,0:T(8,128)(2,1)S(1)} %bitcast.63, bf16[49,768]{1,0:T(8,128)(2,1)S(1)} %reshape.72.kernel_ref, f32[1,768]{1,0:T(1,128)S(1)} %reshape.73.gain_ref), custom_call_target="tpu_custom_call" | custom-call | tf_op jit(solution)/shard_map/conv_norm/pallas_call | solution.py:131
  52.4 0.9 copy-done.18
  53.2 3.1 %collective-permute-start.4 = (bf16[224,768]{1,0:T(8,128)(2,1)S(1)}, bf16[224,768]{1,0:T(8,128)(2,1)S(1)}, u32[]{:S(2)}, u32[]{:S(2)}) collective-permute-start(bf16[224,768]{1,0:T(8,128)(2,1)S(1)} %get-tuple-element.34.refs_0_), channel_id=1, source_target_pairs={{0,8},{8,32},{32,40},{40,0},{1,9},{9,33},{33,41},{41,1},{2,10},{10... | collective-permute-start | bytes 1032200 | tf_op jit(solution)/shard_map/ppermute | solution.py:462
  56.4 4.4 %collective-permute-start.5 = (bf16[224,768]{1,0:T(8,128)(2,1)S(1)}, bf16[224,768]{1,0:T(8,128)(2,1)S(1)}, u32[]{:S(2)}, u32[]{:S(2)}) collective-permute-start(bf16[224,768]{1,0:T(8,128)(2,1)S(1)} %get-tuple-element.34.refs_0_), channel_id=1, source_target_pairs={{0,32},{8,40},{32,0},{40,8},{1,33},{9,41},{33,1},{41,9},{2,34},{10... | collective-permute-start | bytes 1032200 | tf_op jit(solution)/shard_map/ppermute | solution.py:462
  60.7 3.1 %collective-permute-start.6 = (bf16[224,768]{1,0:T(8,128)(2,1)S(1)}, bf16[224,768]{1,0:T(8,128)(2,1)S(1)}, u32[]{:S(2)}, u32[]{:S(2)}) collective-permute-start(bf16[224,768]{1,0:T(8,128)(2,1)S(1)} %get-tuple-element.34.refs_0_), channel_id=1, source_target_pairs={{0,40},{8,0},{32,8},{40,32},{1,41},{9,1},{33,9},{41,33},{2,42},{10... | collective-permute-start | bytes 1032200 | tf_op jit(solution)/shard_map/ppermute | solution.py:462
  65.1 0.7 fusion
  65.8 2.2 collective-permute-start
  68.0 2.8 %collective-permute-start.1 = (bf16[224,768]{1,0:T(8,128)(2,1)S(1)}, bf16[224,768]{1,0:T(8,128)(2,1)S(1)}, u32[]{:S(2)}, u32[]{:S(2)}) collective-permute-start(bf16[224,768]{1,0:T(8,128)(2,1)S(1)} %bitcast.56), channel_id=1, source_target_pairs={{0,32},{8,40},{32,0},{40,8},{1,33},{9,41},{33,1},{41,9},{2,34},{10... | collective-permute-start | bytes 1032200 | tf_op jit(solution)/shard_map/ppermute | solution.py:462
  70.8 3.6 %collective-permute-done.5.refs_2_ = bf16[224,768]{1,0:T(8,128)(2,1)S(1)} collective-permute-done((bf16[224,768]{1,0:T(8,128)(2,1)S(1)}, bf16[224,768]{1,0:T(8,128)(2,1)S(1)}, u32[]{:S(2)}, u32[]{:S(2)}) %collective-permute-start.5) | collective-permute-done | bytes 344096 | tf_op jit(solution)/shard_map/ppermute | solution.py:462
  74.4 1.9 collective-permute-start.2
  76.4 1.9 activations.1
  78.3 1.5 copy-done.2
  79.8 1.1 copy-done.5
  80.9 1.4 collective-permute-done.refs_1_.refs_5_
  82.3 0.7 copy-done.9
  83.0 6.1 %collective-permute-done.1.refs_2_.refs_6_ = bf16[224,768]{1,0:T(8,128)(2,1)S(1)} collective-permute-done((bf16[224,768]{1,0:T(8,128)(2,1)S(1)}, bf16[224,768]{1,0:T(8,128)(2,1)S(1)}, u32[]{:S(2)}, u32[]{:S(2)}) %collective-permute-start.1) | collective-permute-done | bytes 344096 | tf_op jit(solution)/shard_map/ppermute | solution.py:462
  89.2 0.7 copy-done.12
  90.4 0.7 copy-done.15
  91.1 1.3 copy-done
  92.4 1.8 copy-done.3
  94.2 1.0 copy-done.10
  95.2 1.0 copy-done.13
  96.1 1.0 copy-done.16
  97.1 3.6 %hidden.1 = (bf16[4,224,768]{2,1,0:T(8,128)(2,1)S(1)}, bf16[224,768]{1,0:T(8,128)(2,1)S(1)}, bf16[224,768]{1,0:T(8,128)(2,1)}, bf16[224,768]{1,0:T(8,128)(2,1)}, bf16[224,768]{1,0:T(8,128)(2,1)S(1)}) custom-call(bf16[224,768]{1,0:T(8,128)(2,1)S(1)} %bitcast.58, bf16[224,768]{1,0:T(8,128)(2,1)S(1)} %copy-done.10, bf16[224,768]{1,0:T(8,128)(2,1)S(1)} %copy-done.13, ...), custom_call_target="tpu_custom_call" | custom-call | tf_op jit(solution)/shard_map/hidden/pallas_call | solution.py:218
  100.8 0.7 copy-done.20
  101.5 0.7 copy-done.26
  102.3 2.8 %weight_grads.1 = (bf16[64,80,128]{2,1,0:T(8,128)(2,1)S(1)}, bf16[64,80,128]{2,1,0:T(8,128)(2,1)S(1)}, f32[8,768]{1,0:T(8,128)S(1)}) custom-call(bf16[224,768]{1,0:T(8,128)(2,1)S(1)} %get-tuple-element.34.refs_0_, bf16[224,768]{1,0:T(8,128)(2,1)S(1)} %collective-permute-done.4.refs_1_, bf16[224,768]{1,0:T(8,128)(2,1)S(1)} %collective-permute-done.5.refs_2_, ...), custom_call_target="tpu_custom_call" | custom-call | tf_op jit(solution)/shard_map/weight_grads/pallas_call | solution.py:276
  105.1 3.0 %collective-permute-start.13 = (bf16[64,80,128]{2,1,0:T(8,128)(2,1)S(1)}, bf16[64,80,128]{2,1,0:T(8,128)(2,1)S(1)}, u32[]{:S(2)}, u32[]{:S(2)}) collective-permute-start(bf16[64,80,128]{2,1,0:T(8,128)(2,1)S(1)} %get-tuple-element.51), channel_id=1, source_target_pairs={{0,16},{16,0},{1,17},{17,1},{2,18},{18,2},{3,19},{19,3},{4,20},{20... | collective-permute-start | bytes 3932168 | tf_op jit(solution)/shard_map/ppermute | solution.py:458
  108.2 2.6 %collective-permute-done.13 = bf16[64,80,128]{2,1,0:T(8,128)(2,1)S(1)} collective-permute-done((bf16[64,80,128]{2,1,0:T(8,128)(2,1)S(1)}, bf16[64,80,128]{2,1,0:T(8,128)(2,1)S(1)}, u32[]{:S(2)}, u32[]{:S(2)}) %collective-permute-start.13) | collective-permute-done | bytes 1310752 | tf_op jit(solution)/shard_map/ppermute | solution.py:458
  110.8 1.5 add_convert_fusion
  112.3 8.3 %all-to-all-start.1 = ((bf16[64,80,128]{2,1,0:T(8,128)(2,1)}), bf16[64,80,128]{2,1,0:T(8,128)(2,1)}, u32[]{:S(2)}, u32[]{:S(2)}) async-start(bf16[64,80,128]{2,1,0:T(8,128)(2,1)} %add_convert_fusion), calls=%async_computation.1 | async-start | bytes 2621440 | tf_op jit(solution)/shard_map/all_to_all | solution.py:506
  120.6 4.3 %collective-permute-start.7 = (bf16[224,768]{1,0:T(8,128)(2,1)}, bf16[224,768]{1,0:T(8,128)(2,1)S(1)}, u32[]{:S(2)}, u32[]{:S(2)}) collective-permute-start(bf16[224,768]{1,0:T(8,128)(2,1)} %get-tuple-element.43), channel_id=1, source_target_pairs={{0,40},{8,0},{32,8},{40,32},{1,41},{9,1},{33,9},{41,33},{2,42},{10... | collective-permute-start | bytes 1032200 | tf_op jit(solution)/shard_map/ppermute | solution.py:462
  124.8 3.4 %collective-permute-start.8 = (bf16[224,768]{1,0:T(8,128)(2,1)}, bf16[224,768]{1,0:T(8,128)(2,1)S(1)}, u32[]{:S(2)}, u32[]{:S(2)}) collective-permute-start(bf16[224,768]{1,0:T(8,128)(2,1)} %get-tuple-element.44), channel_id=1, source_target_pairs={{0,32},{8,40},{32,0},{40,8},{1,33},{9,41},{33,1},{41,9},{2,34},{10... | collective-permute-start | bytes 1032200 | tf_op jit(solution)/shard_map/ppermute | solution.py:462
  128.3 1.9 collective-permute-start.9
  130.2 2.5 %collective-permute-done.7.one_ref = bf16[224,768]{1,0:T(8,128)(2,1)S(1)} collective-permute-done((bf16[224,768]{1,0:T(8,128)(2,1)}, bf16[224,768]{1,0:T(8,128)(2,1)S(1)}, u32[]{:S(2)}, u32[]{:S(2)}) %collective-permute-start.7) | collective-permute-done | bytes 344096 | tf_op jit(solution)/shard_map/ppermute | solution.py:462
  132.7 4.6 %collective-permute-done.8.two_ref = bf16[224,768]{1,0:T(8,128)(2,1)S(1)} collective-permute-done((bf16[224,768]{1,0:T(8,128)(2,1)}, bf16[224,768]{1,0:T(8,128)(2,1)S(1)}, u32[]{:S(2)}, u32[]{:S(2)}) %collective-permute-start.8) | collective-permute-done | bytes 344096 | tf_op jit(solution)/shard_map/ppermute | solution.py:462
  137.2 8.7 %collective-permute-done.9.three_ref = bf16[224,768]{1,0:T(8,128)(2,1)S(1)} collective-permute-done((bf16[224,768]{1,0:T(8,128)(2,1)S(1)}, bf16[224,768]{1,0:T(8,128)(2,1)S(1)}, u32[]{:S(2)}, u32[]{:S(2)}) %collective-permute-start.9) | collective-permute-done | bytes 344096 | tf_op jit(solution)/shard_map/ppermute | solution.py:462
  145.9 0.7 copy-done.22
  146.7 1.0 copy-done.23
  147.6 3.8 %norm_back.1 = (f32[6,64,128]{2,1,0:T(8,128)S(1)}, f32[6,14,16,128]{3,2,1,0:T(8,128)S(1)}) custom-call(f32[1]{0:T(128)} %bitcast.1.weight_ref, bf16[224,768]{1,0:T(8,128)(2,1)S(1)} %copy-done.21, bf16[224,768]{1,0:T(8,128)(2,1)S(1)} %collective-permute-done.7.one_ref, bf16[224,768]{1,0:T(8,128)(2,1)S(1)} %collective-permute-done.8.two_ref, ...), custom_call_target="tpu_custom_call" | custom-call | tf_op jit(solution)/shard_map/norm_back/pallas_call | solution.py:348
  151.5 2.5 %collective-permute-start.10 = (f32[2,2,48,128]{3,2,1,0:T(8,128)S(1)}, f32[2,2,48,128]{3,2,1,0:T(8,128)S(1)}, u32[]{:S(2)}, u32[]{:S(2)}) collective-permute-start(f32[2,2,48,128]{3,2,1,0:T(8,128)S(1)} %dynamic-slice_bitcast_fusion), channel_id=1, source_target_pairs={{0,16},{16,0},{1,17},{17,1},{2,18},{18,2},{3,19},{19,3},{4,20},{20... | collective-permute-start | bytes 294920 | tf_op jit(solution)/shard_map/ppermute | solution.py:473
  154.0 0.7 collective-permute-done.10
  154.8 1.9 collective-permute-start.11
  156.7 2.9 %collective-permute-done.11 = f32[2,48,128]{2,1,0:T(8,128)S(1)} collective-permute-done((f32[2,48,128]{2,1,0:T(8,128)S(1)}, f32[2,48,128]{2,1,0:T(8,128)S(1)}, u32[]{:S(2)}, u32[]{:S(2)}) %collective-permute-start.11) | collective-permute-done | bytes 49184 | tf_op jit(solution)/shard_map/ppermute | solution.py:473
  159.6 3.4 %collective-permute-start.12 = (f32[48,128]{1,0:T(8,128)S(1)}, f32[48,128]{1,0:T(8,128)S(1)}, u32[]{:S(2)}, u32[]{:S(2)}) collective-permute-start(f32[48,128]{1,0:T(8,128)S(1)} %dynamic-slice_bitcast_fusion.2), channel_id=1, source_target_pairs={{0,32},{32,0},{1,33},{33,1},{2,34},{34,2},{3,35},{35,3},{4,36},{36... | collective-permute-start | bytes 73736 | tf_op jit(solution)/shard_map/ppermute | solution.py:473
  163.0 2.7 %collective-permute-done.12 = f32[48,128]{1,0:T(8,128)S(1)} collective-permute-done((f32[48,128]{1,0:T(8,128)S(1)}, f32[48,128]{1,0:T(8,128)S(1)}, u32[]{:S(2)}, u32[]{:S(2)}) %collective-permute-start.12) | collective-permute-done | bytes 24608 | tf_op jit(solution)/shard_map/ppermute | solution.py:473
  165.7 1.5 convert_reduce_fusion
  167.3 14.7 %all_to_all.25 = f32[8,48,128]{2,1,0:T(8,128)S(1)} all-to-all(f32[8,48,128]{2,1,0:T(8,128)S(1)} %broadcast_in_dim.18), channel_id=1, replica_groups=mesh['y'=8,'xh'=2,'core'=2,'xl'=2,'z'=8] {'z'}, dimensions={0} | all-to-all | bytes 393216 | tf_op jit(solution)/shard_map/all_to_all | solution.py:454
  182.0 16.8 %all_to_all.26 = bf16[8,176,128]{2,1,0:T(8,128)(2,1)S(1)} all-to-all(bf16[8,176,128]{2,1,0:T(8,128)(2,1)S(1)} %broadcast_in_dim.19), channel_id=1, replica_groups=mesh['y'=8,'xh'=2,'core'=2,'xl'=2,'z'=8] {'y'}, dimensions={0} | all-to-all | bytes 720896 | tf_op jit(solution)/shard_map/all_to_all | solution.py:454
  198.9 3.4 %collective-permute-start.14 = (bf16[8,80,128]{2,1,0:T(8,128)(2,1)S(1)}, bf16[8,80,128]{2,1,0:T(8,128)(2,1)S(1)}, u32[]{:S(2)}, u32[]{:S(2)}) collective-permute-start(bf16[8,80,128]{2,1,0:T(8,128)(2,1)S(1)} %get-tuple-element.83), channel_id=1, source_target_pairs={{0,32},{32,0},{1,33},{33,1},{2,34},{34,2},{3,35},{35,3},{4,36},{36... | collective-permute-start | bytes 491528 | tf_op jit(solution)/shard_map/ppermute | solution.py:525
  202.3 2.6 %input_grad.1 = f32[1,14,14,768]{3,2,1,0:T(8,128)S(1)} custom-call(f32[6,14,16,128]{3,2,1,0:T(8,128)S(1)} %get-tuple-element.54.conv_ref, bf16[49,768]{1,0:T(8,128)(2,1)S(1)} %reshape.72.kernel_ref, bf16[224,768]{1,0:T(8,128)(2,1)S(1)} %bitcast.60), custom_call_target="tpu_custom_call" | custom-call | tf_op jit(solution)/shard_map/input_grad/pallas_call | solution.py:397
  205.7 8.9 %all-to-all-start.4 = ((f32[8,48,128]{2,1,0:T(8,128)}), f32[8,48,128]{2,1,0:T(8,128)S(1)}, u32[]{:S(2)}, u32[]{:S(2)}) async-start(f32[8,48,128]{2,1,0:T(8,128)} %broadcast_in_dim.20), calls=%async_computation.4 | async-start | bytes 393216 | tf_op jit(solution)/shard_map/all_to_all | solution.py:454
  214.6 2.0 collective-permute-start.15
  216.6 3.8 %all-to-all-done.4 = f32[8,48,128]{2,1,0:T(8,128)S(1)} async-done(((f32[8,48,128]{2,1,0:T(8,128)}), f32[8,48,128]{2,1,0:T(8,128)S(1)}, u32[]{:S(2)}, u32[]{:S(2)}) %all-to-all-start.4) | async-done | bytes 196640 | tf_op jit(solution)/shard_map/all_to_all | solution.py:454
  223.0 0.8 multiply_convert_fusion
  224.5 1.1 unpack.1
  225.6 1.1 copy.26
  (95 shorter events, 6.4 us)
Async XLA Ops:
  8.4 1.0 copy-start.24
  9.4 0.7 copy-start.25
  11.5 37.9 %copy-start.29 = (bf16[7,7,768]{2,1,0:T(8,128)(2,1)S(1)}, bf16[7,7,768]{2,1,0:T(8,128)(2,1)}, u32[]{:S(2)}) copy-start(bf16[7,7,768]{2,1,0:T(8,128)(2,1)} %param.14) | copy-start | bytes 225796
  11.5 38.0 %copy-start.30 = (f32[768]{0:T(1024)S(1)}, f32[768]{0:T(1024)}, u32[]{:S(2)}) copy-start(f32[768]{0:T(1024)} %param.15) | copy-start | bytes 9220
  11.5 38.0 %copy-start.4 = (bf16[1,14,14,768]{3,2,1,0:T(8,128)(2,1)S(1)}, bf16[1,14,14,768]{3,2,1,0:T(8,128)(2,1)}, u32[]{:S(2)}) copy-start(bf16[1,14,14,768]{3,2,1,0:T(8,128)(2,1)} %param.10) | copy-start | bytes 903172
  12.5 52.0 %copy-start.32 = (f32[4]{0:T(128)S(1)}, f32[4]{0:T(128)}, u32[]{:S(2)}) copy-start(f32[4]{0:T(128)} %param.13) | copy-start | bytes 52
  12.5 52.6 %copy-start.28 = (bf16[1,14,14,768]{3,2,1,0:T(8,128)(2,1)S(1)}, bf16[1,14,14,768]{3,2,1,0:T(8,128)(2,1)}, u32[]{:S(2)}) copy-start(bf16[1,14,14,768]{3,2,1,0:T(8,128)(2,1)} %param.11) | copy-start | bytes 903172
  12.5 34.6 %all-to-all-start = ((bf16[8,64,768]{2,1,0:T(8,128)(2,1)}), bf16[8,64,768]{2,1,0:T(8,128)(2,1)S(1)}, u32[]{:S(2)}, u32[]{:S(2)}) async-start(bf16[8,64,768]{2,1,0:T(8,128)(2,1)} %broadcast_in_dim.17), calls=%async_computation | async-start | bytes 1572864 | tf_op jit(solution)/shard_map/all_to_all | solution.py:454
  23.5 52.8 %copy-start.31 = (f32[768]{0:T(1024)S(1)}, f32[768]{0:T(1024)}, u32[]{:S(2)}) copy-start(f32[768]{0:T(1024)} %param.19) | copy-start | bytes 9220
  23.5 67.6 %all-gather.2.cloned.1.call-start = ((), (), s32[]{:S(2)}) async-start(), calls=%async_computation.5 | async-start | bytes 1327104 | tf_op jit(solution)/shard_map/all_gather | solution.py:484
  47.1 29.3 %collective-permute-start.3 = (bf16[8,64,768]{2,1,0:T(8,128)(2,1)S(1)}, bf16[8,64,768]{2,1,0:T(8,128)(2,1)S(1)}, u32[]{:S(2)}, u32[]{:S(2)}) collective-permute-start(bf16[8,64,768]{2,1,0:T(8,128)(2,1)S(1)} %all-to-all-done.refs_4_), channel_id=1, source_target_pairs={{0,16},{16,0},{1,17},{17,1},{2,18},{18,2},{3,19},{19,3},{4,20},{20... | collective-permute-start | bytes 2359304 | tf_op jit(solution)/shard_map/ppermute | solution.py:458
  52.4 0.9 copy-start.18
  53.2 14.8 %collective-permute-start.4 = (bf16[224,768]{1,0:T(8,128)(2,1)S(1)}, bf16[224,768]{1,0:T(8,128)(2,1)S(1)}, u32[]{:S(2)}, u32[]{:S(2)}) collective-permute-start(bf16[224,768]{1,0:T(8,128)(2,1)S(1)} %get-tuple-element.34.refs_0_), channel_id=1, source_target_pairs={{0,8},{8,32},{32,40},{40,0},{1,9},{9,33},{33,41},{41,1},{2,10},{10... | collective-permute-start | bytes 1032200 | tf_op jit(solution)/shard_map/ppermute | solution.py:462
  56.4 18.1 %collective-permute-start.5 = (bf16[224,768]{1,0:T(8,128)(2,1)S(1)}, bf16[224,768]{1,0:T(8,128)(2,1)S(1)}, u32[]{:S(2)}, u32[]{:S(2)}) collective-permute-start(bf16[224,768]{1,0:T(8,128)(2,1)S(1)} %get-tuple-element.34.refs_0_), channel_id=1, source_target_pairs={{0,32},{8,40},{32,0},{40,8},{1,33},{9,41},{33,1},{41,9},{2,34},{10... | collective-permute-start | bytes 1032200 | tf_op jit(solution)/shard_map/ppermute | solution.py:462
  60.7 15.6 %collective-permute-start.6 = (bf16[224,768]{1,0:T(8,128)(2,1)S(1)}, bf16[224,768]{1,0:T(8,128)(2,1)S(1)}, u32[]{:S(2)}, u32[]{:S(2)}) collective-permute-start(bf16[224,768]{1,0:T(8,128)(2,1)S(1)} %get-tuple-element.34.refs_0_), channel_id=1, source_target_pairs={{0,40},{8,0},{32,8},{40,32},{1,41},{9,1},{33,9},{41,33},{2,42},{10... | collective-permute-start | bytes 1032200 | tf_op jit(solution)/shard_map/ppermute | solution.py:462
  65.8 16.5 %collective-permute-start = (bf16[224,768]{1,0:T(8,128)(2,1)S(1)}, bf16[224,768]{1,0:T(8,128)(2,1)S(1)}, u32[]{:S(2)}, u32[]{:S(2)}) collective-permute-start(bf16[224,768]{1,0:T(8,128)(2,1)S(1)} %bitcast.55), channel_id=1, source_target_pairs={{0,8},{8,32},{32,40},{40,0},{1,9},{9,33},{33,41},{41,1},{2,10},{10... | collective-permute-start | bytes 1032200 | tf_op jit(solution)/shard_map/ppermute | solution.py:462
  68.0 21.1 %collective-permute-start.1 = (bf16[224,768]{1,0:T(8,128)(2,1)S(1)}, bf16[224,768]{1,0:T(8,128)(2,1)S(1)}, u32[]{:S(2)}, u32[]{:S(2)}) collective-permute-start(bf16[224,768]{1,0:T(8,128)(2,1)S(1)} %bitcast.56), channel_id=1, source_target_pairs={{0,32},{8,40},{32,0},{40,8},{1,33},{9,41},{33,1},{41,9},{2,34},{10... | collective-permute-start | bytes 1032200 | tf_op jit(solution)/shard_map/ppermute | solution.py:462
  74.4 16.0 %collective-permute-start.2 = (bf16[224,768]{1,0:T(8,128)(2,1)S(1)}, bf16[224,768]{1,0:T(8,128)(2,1)S(1)}, u32[]{:S(2)}, u32[]{:S(2)}) collective-permute-start(bf16[224,768]{1,0:T(8,128)(2,1)S(1)} %bitcast.57), channel_id=1, source_target_pairs={{0,40},{8,0},{32,8},{40,32},{1,41},{9,1},{33,9},{41,33},{2,42},{10... | collective-permute-start | bytes 1032200 | tf_op jit(solution)/shard_map/ppermute | solution.py:462
  76.4 1.9 copy-start.7
  78.3 1.5 copy-start.2
  79.8 1.1 copy-start.5
  82.3 0.7 copy-start.9
  89.2 0.7 copy-start.12
  90.4 0.7 copy-start.15
  91.1 1.3 copy-start
  92.4 1.8 copy-start.3
  94.2 1.0 copy-start.10
  95.2 1.0 copy-start.13
  96.1 1.0 copy-start.16
  97.1 5.1 %copy-start.1 = (bf16[768,768]{1,0:T(8,128)(2,1)S(1)}, bf16[768,768]{1,0:T(8,128)(2,1)}, u32[]{:S(2)}) copy-start(bf16[768,768]{1,0:T(8,128)(2,1)} %all-gather.2.cloned.1.call-done) | copy-start | bytes 3538948
  97.1 5.1 %copy-start.6 = (bf16[4,224,768]{2,1,0:T(8,128)(2,1)S(1)}, bf16[4,224,768]{2,1,0:T(8,128)(2,1)}, u32[]{:S(2)}) copy-start(bf16[4,224,768]{2,1,0:T(8,128)(2,1)} %copy-done.5) | copy-start | bytes 4128772
  97.1 5.1 %copy-start.8 = (bf16[224,768]{1,0:T(8,128)(2,1)S(1)}, bf16[224,768]{1,0:T(8,128)(2,1)}, u32[]{:S(2)}) copy-start(bf16[224,768]{1,0:T(8,128)(2,1)} %copy-done.7) | copy-start | bytes 1032196
  97.1 5.1 %copy-start.11 = (bf16[224,768]{1,0:T(8,128)(2,1)S(1)}, bf16[224,768]{1,0:T(8,128)(2,1)}, u32[]{:S(2)}) copy-start(bf16[224,768]{1,0:T(8,128)(2,1)} %copy-done.9) | copy-start | bytes 1032196
  97.1 5.1 %copy-start.14 = (bf16[224,768]{1,0:T(8,128)(2,1)S(1)}, bf16[224,768]{1,0:T(8,128)(2,1)}, u32[]{:S(2)}) copy-start(bf16[224,768]{1,0:T(8,128)(2,1)} %copy-done.12) | copy-start | bytes 1032196
  97.1 5.1 %copy-start.17 = (bf16[224,768]{1,0:T(8,128)(2,1)S(1)}, bf16[224,768]{1,0:T(8,128)(2,1)}, u32[]{:S(2)}) copy-start(bf16[224,768]{1,0:T(8,128)(2,1)} %copy-done.15) | copy-start | bytes 1032196
  100.8 0.7 copy-start.20
  101.5 0.7 copy-start.26
  105.1 5.7 %collective-permute-start.13 = (bf16[64,80,128]{2,1,0:T(8,128)(2,1)S(1)}, bf16[64,80,128]{2,1,0:T(8,128)(2,1)S(1)}, u32[]{:S(2)}, u32[]{:S(2)}) collective-permute-start(bf16[64,80,128]{2,1,0:T(8,128)(2,1)S(1)} %get-tuple-element.51), channel_id=1, source_target_pairs={{0,16},{16,0},{1,17},{17,1},{2,18},{18,2},{3,19},{19,3},{4,20},{20... | collective-permute-start | bytes 3932168 | tf_op jit(solution)/shard_map/ppermute | solution.py:458
  112.3 16.0 %copy-start.27 = (bf16[224,768]{1,0:T(8,128)(2,1)S(1)}, bf16[224,768]{1,0:T(8,128)(2,1)}, u32[]{:S(2)}) copy-start(bf16[224,768]{1,0:T(8,128)(2,1)} %copy-done.26) | copy-start | bytes 1032196
  112.3 34.4 %copy-start.19 = (f32[6,14,16,128]{3,2,1,0:T(8,128)S(1)}, f32[6,14,16,128]{3,2,1,0:T(8,128)}, u32[]{:S(2)}) copy-start(f32[6,14,16,128]{3,2,1,0:T(8,128)} %copy-done.18) | copy-start | bytes 2064388
  112.3 34.4 %copy-start.21 = (bf16[224,768]{1,0:T(8,128)(2,1)S(1)}, bf16[224,768]{1,0:T(8,128)(2,1)}, u32[]{:S(2)}) copy-start(bf16[224,768]{1,0:T(8,128)(2,1)} %copy-done.20) | copy-start | bytes 1032196
  112.3 53.4 %all-to-all-start.1 = ((bf16[64,80,128]{2,1,0:T(8,128)(2,1)}), bf16[64,80,128]{2,1,0:T(8,128)(2,1)}, u32[]{:S(2)}, u32[]{:S(2)}) async-start(bf16[64,80,128]{2,1,0:T(8,128)(2,1)} %add_convert_fusion), calls=%async_computation.1 | async-start | bytes 2621440 | tf_op jit(solution)/shard_map/all_to_all | solution.py:506
  120.6 12.1 %collective-permute-start.7 = (bf16[224,768]{1,0:T(8,128)(2,1)}, bf16[224,768]{1,0:T(8,128)(2,1)S(1)}, u32[]{:S(2)}, u32[]{:S(2)}) collective-permute-start(bf16[224,768]{1,0:T(8,128)(2,1)} %get-tuple-element.43), channel_id=1, source_target_pairs={{0,40},{8,0},{32,8},{40,32},{1,41},{9,1},{33,9},{41,33},{2,42},{10... | collective-permute-start | bytes 1032200 | tf_op jit(solution)/shard_map/ppermute | solution.py:462
  124.8 12.4 %collective-permute-start.8 = (bf16[224,768]{1,0:T(8,128)(2,1)}, bf16[224,768]{1,0:T(8,128)(2,1)S(1)}, u32[]{:S(2)}, u32[]{:S(2)}) collective-permute-start(bf16[224,768]{1,0:T(8,128)(2,1)} %get-tuple-element.44), channel_id=1, source_target_pairs={{0,32},{8,40},{32,0},{40,8},{1,33},{9,41},{33,1},{41,9},{2,34},{10... | collective-permute-start | bytes 1032200 | tf_op jit(solution)/shard_map/ppermute | solution.py:462
  128.3 17.7 %collective-permute-start.9 = (bf16[224,768]{1,0:T(8,128)(2,1)S(1)}, bf16[224,768]{1,0:T(8,128)(2,1)S(1)}, u32[]{:S(2)}, u32[]{:S(2)}) collective-permute-start(bf16[224,768]{1,0:T(8,128)(2,1)S(1)} %copy-done.27), channel_id=1, source_target_pairs={{0,8},{8,32},{32,40},{40,0},{1,9},{9,33},{33,41},{41,1},{2,10},{10... | collective-permute-start | bytes 1032200 | tf_op jit(solution)/shard_map/ppermute | solution.py:462
  145.9 0.7 copy-start.22
  146.7 1.0 copy-start.23
  151.5 3.2 %collective-permute-start.10 = (f32[2,2,48,128]{3,2,1,0:T(8,128)S(1)}, f32[2,2,48,128]{3,2,1,0:T(8,128)S(1)}, u32[]{:S(2)}, u32[]{:S(2)}) collective-permute-start(f32[2,2,48,128]{3,2,1,0:T(8,128)S(1)} %dynamic-slice_bitcast_fusion), channel_id=1, source_target_pairs={{0,16},{16,0},{1,17},{17,1},{2,18},{18,2},{3,19},{19,3},{4,20},{20... | collective-permute-start | bytes 294920 | tf_op jit(solution)/shard_map/ppermute | solution.py:473
  154.8 4.8 %collective-permute-start.11 = (f32[2,48,128]{2,1,0:T(8,128)S(1)}, f32[2,48,128]{2,1,0:T(8,128)S(1)}, u32[]{:S(2)}, u32[]{:S(2)}) collective-permute-start(f32[2,48,128]{2,1,0:T(8,128)S(1)} %dynamic-slice_bitcast_fusion.1), channel_id=1, source_target_pairs={{0,8},{8,0},{1,9},{9,1},{2,10},{10,2},{3,11},{11,3},{4,12},{12,4},... | collective-permute-start | bytes 147464 | tf_op jit(solution)/shard_map/ppermute | solution.py:473
  159.6 6.1 %collective-permute-start.12 = (f32[48,128]{1,0:T(8,128)S(1)}, f32[48,128]{1,0:T(8,128)S(1)}, u32[]{:S(2)}, u32[]{:S(2)}) collective-permute-start(f32[48,128]{1,0:T(8,128)S(1)} %dynamic-slice_bitcast_fusion.2), channel_id=1, source_target_pairs={{0,32},{32,0},{1,33},{33,1},{2,34},{34,2},{3,35},{35,3},{4,36},{36... | collective-permute-start | bytes 73736 | tf_op jit(solution)/shard_map/ppermute | solution.py:473
  198.9 15.7 %collective-permute-start.14 = (bf16[8,80,128]{2,1,0:T(8,128)(2,1)S(1)}, bf16[8,80,128]{2,1,0:T(8,128)(2,1)S(1)}, u32[]{:S(2)}, u32[]{:S(2)}) collective-permute-start(bf16[8,80,128]{2,1,0:T(8,128)(2,1)S(1)} %get-tuple-element.83), channel_id=1, source_target_pairs={{0,32},{32,0},{1,33},{33,1},{2,34},{34,2},{3,35},{35,3},{4,36},{36... | collective-permute-start | bytes 491528 | tf_op jit(solution)/shard_map/ppermute | solution.py:525
  205.7 14.8 %all-to-all-start.4 = ((f32[8,48,128]{2,1,0:T(8,128)}), f32[8,48,128]{2,1,0:T(8,128)S(1)}, u32[]{:S(2)}, u32[]{:S(2)}) async-start(f32[8,48,128]{2,1,0:T(8,128)} %broadcast_in_dim.20), calls=%async_computation.4 | async-start | bytes 393216 | tf_op jit(solution)/shard_map/all_to_all | solution.py:454
  214.6 9.2 %collective-permute-start.15 = (bf16[2,8,80,128]{3,2,1,0:T(8,128)(2,1)S(1)}, bf16[2,8,80,128]{3,2,1,0:T(8,128)(2,1)S(1)}, u32[]{:S(2)}, u32[]{:S(2)}) collective-permute-start(bf16[2,8,80,128]{3,2,1,0:T(8,128)(2,1)S(1)} %maximum_select_fusion.mine_ref), channel_id=1, source_target_pairs={{0,16},{16,0},{1,17},{17,1},{2,18},{18,2},{3,19},{19,3},{4,20},{20... | collective-permute-start | bytes 983048 | tf_op jit(solution)/shard_map/ppermute | solution.py:458
Sparse Core Ops, SparseCore 0:
  27.0 40.1 all-gather.1

commit v3 on v2

--- a/solution.py
+++ b/solution.py
@@ -1,3 +1,5 @@
+import functools
+
 import jax
 import jax.numpy as jnp
 import numpy as np
@@ -16,8 +18,8 @@
 LANES = 128
 BLOCKS = CH // LANES
 OWN = 48
-HALF = 384
-PACK = 64
+UNITS = 2 * OWN
+PACK = 2 * UNITS + 16
 REPLICA = ("y", "xh", "core")
 SHARD = ("xl", "z")
 RING = ("xh", "xl")
@@ -45,36 +47,43 @@
     return pl.BlockSpec(memory_space=pltpu.SMEM)
 
 
-def pack_kernel(place_ref, first_ref, bias_ref, second_ref, one_ref, two_ref):
-    block = place_ref[0]
+def block(*shape):
+    return pl.BlockSpec(shape, lambda i: (0,) * len(shape))
+
+
+def pack_kernel(place_ref, first_ref, bias_ref, second_ref, out_ref):
+    q = place_ref[0]
     column = place_ref[1]
-    row = lax.broadcasted_iota(jnp.int32, (2 * OWN, 192), 0)
-    lane = lax.broadcasted_iota(jnp.int32, (2 * OWN, 192), 1)
-    partner = block + 1 - 2 * lax.rem(block, 2)
-    wanted = jnp.where(row < OWN, row + block * OWN, row - OWN + partner * OWN)
+    partner = q + 1 - 2 * lax.rem(q, 2)
+    row = lax.broadcasted_iota(jnp.int32, (UNITS, 192), 0)
+    lane = lax.broadcasted_iota(jnp.int32, (UNITS, 192), 1)
+    wanted = jnp.where(row < OWN, row + q * OWN, row - OWN + partner * OWN)
     pick = (lane == wanted).astype(BF16)
-    one_ref[0:OWN, :] = nt(pick[0:OWN], first_ref[...]).astype(BF16)
-    two_ref[...] = jnp.dot(pick, second_ref[...], preferred_element_type=F32).astype(BF16)
-    unit = lax.broadcasted_iota(jnp.int32, (192, HALF), 0) - block * OWN
-    spot = lax.broadcasted_iota(jnp.int32, (192, HALF), 1) - column * OWN
-    put = ((unit == spot) & (unit >= 0) & (unit < OWN)).astype(BF16)
+    out_ref[0:UNITS, :] = jnp.dot(pick, first_ref[...], preferred_element_type=F32).astype(BF16)
+    out_ref[UNITS : 2 * UNITS, :] = jnp.dot(pick, second_ref[...], preferred_element_type=F32).astype(BF16)
+    unit = lax.broadcasted_iota(jnp.int32, (192, CH), 0)
+    spot = lax.broadcasted_iota(jnp.int32, (192, CH), 1) - column * UNITS
+    wanted = jnp.where(spot < OWN, spot + q * OWN, spot - OWN + partner * OWN)
+    put = ((unit == wanted) & (spot >= 0) & (spot < UNITS)).astype(BF16)
     bias = jnp.broadcast_to(bias_ref[...], (16, 192))
     high = bias.astype(BF16)
     low = (bias - high.astype(F32)).astype(BF16)
-    one_ref[OWN:PACK, 0:HALF] = jnp.dot(high, put, preferred_element_type=F32).astype(BF16)
-    one_ref[OWN:PACK, HALF:CH] = jnp.dot(low, put, preferred_element_type=F32).astype(BF16)
+    bias_row = lax.broadcasted_iota(jnp.int32, (16, 192), 0)
+    both = jnp.where(bias_row == 0, high.astype(F32), low.astype(F32)).astype(BF16)
+    out_ref[2 * UNITS : PACK, :] = jnp.dot(both, put, preferred_element_type=F32).astype(BF16)
 
 
 def pack_weights(place, first_weight, first_bias, second_weight):
     return pl.pallas_call(
         pack_kernel,
-        out_shape=(jax.ShapeDtypeStruct((PACK, CH), BF16), jax.ShapeDtypeStruct((2 * OWN, CH), BF16)),
-        in_specs=[scalars(), whole(), whole(), whole()],
-        out_specs=(whole(), whole()),
+        grid=(1,),
+        out_shape=jax.ShapeDtypeStruct((PACK, CH), BF16),
+        in_specs=[scalars(), block(192, CH), block(1, 192), block(192, CH)],
+        out_specs=block(PACK, CH),
         compiler_params=params(8),
         interpret=INTERPRET,
         name="pack",
-    )(place, first_weight, first_bias.reshape(1, 192), second_weight)
+    )(place, first_weight.T, first_bias.reshape(1, 192), second_weight)
 
 
 def taps_sum(padded_ref, kernel, flip):
@@ -156,136 +165,91 @@
     )(image, kernel, gain)
 
 
-def first_of(mine_ref, other_ref):
-    return jnp.concatenate(
-        [ref[:, 0:OWN, :].reshape(HALF, CH) for ref in (mine_ref, other_ref)], axis=0
-    )
-
-
-def second_of(two_ref):
-    return jnp.concatenate(
-        [two_ref[:, k * OWN : (k + 1) * OWN, :].reshape(HALF, CH) for k in range(2)], axis=0
-    )
-
-
-def activation_kernel(*refs):
-    normed = refs[0:4]
-    mine_ref, other_ref, act_ref, slope_ref = refs[4:8]
-    first = first_of(mine_ref, other_ref)
-    biases = []
-    for ref in (mine_ref, other_ref):
-        bias = jnp.sum(ref[:, OWN:PACK, :].astype(F32), axis=0)[0:1, :]
-        biases.append(bias[:, 0:HALF] + bias[:, HALF:CH])
-    bias = jnp.concatenate(biases, axis=1)
+def hidden_kernel(*refs):
+    normed_in = refs[0:4]
+    scaled_in = refs[4:8]
+    pack_in, layer_ref = refs[8:10]
+    parts = refs[10:14]
+    outs = refs[14:16]
+    scale_ref = refs[16]
+    normed, scaled, pack, act, grad, sems = refs[17:23]
+    copies = [pltpu.make_async_copy(pack_in, pack, sems.at[8])]
     for i in range(4):
-        preact = nt(normed[i][...], first) + bias
+        rows = pl.ds(i * PIX, PIX)
+        copies.append(pltpu.make_async_copy(normed_in[i], normed.at[rows], sems.at[i]))
+        copies.append(pltpu.make_async_copy(scaled_in[i], scaled.at[rows], sems.at[4 + i]))
+    for copy in copies:
+        copy.start()
+    copies[0].wait()
+    first = pack[:, 0:UNITS, :].reshape(CH, CH)
+    second = pack[:, UNITS : 2 * UNITS, :].reshape(CH, CH)
+    bias = jnp.sum(pack[:, 2 * UNITS : PACK, :].astype(F32), axis=0)
+    bias = bias[0:1, :] + bias[1:2, :]
+    layer = layer_ref[...]
+    for i in range(4):
+        rows = slice(i * PIX, (i + 1) * PIX)
+        copies[1 + 2 * i].wait()
+        copies[2 + 2 * i].wait()
+        preact = nt(normed[rows, :], first) + bias
         cumulative = 0.5 * (1.0 + lax.erf(preact * 0.7071067811865476))
-        slope_ref[i] = cumulative + preact * jnp.exp(-0.5 * preact * preact) * 0.3989422804014327
-        act_ref[i] = (preact * cumulative).astype(BF16)
-
-
-def activations(normed, mine, other):
-    return pl.pallas_call(
-        activation_kernel,
-        out_shape=(
-            jax.ShapeDtypeStruct((4, PIX, CH), BF16),
-            jax.ShapeDtypeStruct((4, PIX, CH), F32),
-        ),
-        in_specs=[whole()] * 6,
-        out_specs=(whole(),) * 2,
-        compiler_params=params(16),
-        interpret=INTERPRET,
-        name="activations",
-    )(*normed, mine, other)
-
-
-def hidden_kernel(*refs):
-    scaled = refs[0:4]
-    mine_ref, other_ref, two_ref, layer_ref, slope_ref = refs[4:9]
-    grad_ref = refs[9]
-    parts = refs[10:14]
-    first = first_of(mine_ref, other_ref)
-    second = second_of(two_ref)
-    layer = layer_ref[...]
-    for i in (2, 1, 3, 0):
-        branch_grad = (scaled[i][...].astype(F32) * layer).astype(BF16)
-        preact_grad = (nt(branch_grad, second) * slope_ref[i]).astype(BF16)
-        grad_ref[i] = preact_grad
+        slope = cumulative + preact * jnp.exp(-0.5 * preact * preact) * 0.3989422804014327
+        act[rows, :] = (preact * cumulative).astype(BF16)
+        branch_grad = (scaled[rows, :].astype(F32) * layer).astype(BF16)
+        preact_grad = (nt(branch_grad, second) * slope).astype(BF16)
+        grad[rows, :] = preact_grad
         parts[i][...] = jnp.dot(preact_grad, first, preferred_element_type=F32).astype(BF16)
-
-
-def hidden(scaled, mine, other, two, layer, slope):
-    return pl.pallas_call(
-        hidden_kernel,
-        out_shape=(jax.ShapeDtypeStruct((4, PIX, CH), BF16),)
-        + (jax.ShapeDtypeStruct((PIX, CH), BF16),) * 4,
-        in_specs=[whole()] * 9,
-        out_specs=(whole(),) * 5,
-        compiler_params=params(16),
-        interpret=INTERPRET,
-        name="hidden",
-    )(*scaled, mine, other, two, layer, slope)
-
-
-def weights_kernel(*refs):
-    normed = refs[0:4]
-    scaled = refs[4:8]
-    act_ref, grad_ref, two_ref, layer_ref = refs[8:12]
-    outs = refs[12:14]
-    scale_ref = refs[14]
-    product = tn(
-        act_ref[...].reshape(4 * PIX, CH), jnp.concatenate([ref[...] for ref in scaled], axis=0)
-    )
-    weighted = second_of(two_ref).astype(F32) * product
-    scale_ref[...] = jnp.sum(weighted.reshape(CH // 8, 8, CH), axis=0)
-    product = (product * layer_ref[...]).astype(BF16)
-    for half in range(2):
-        spread(outs[half], product[half * HALF : (half + 1) * HALF], 0)
-    product = tn(
-        grad_ref[...].reshape(4 * PIX, CH), jnp.concatenate([ref[...] for ref in normed], axis=0)
-    ).astype(BF16)
-    for half in range(2):
-        spread(outs[half], product[half * HALF : (half + 1) * HALF], 18)
-    ones = jnp.ones((16, 4 * PIX), BF16)
-    bias = jnp.dot(ones, grad_ref[...].reshape(4 * PIX, CH), preferred_element_type=F32)
+    product = tn(act[...], scaled[...])
+    scale_ref[...] = jnp.sum((second.astype(F32) * product).reshape(CH // 8, 8, CH), axis=0)
+    spread(outs, (product * layer).astype(BF16), 0)
+    spread(outs, tn(grad[...], normed[...]).astype(BF16), 18)
+    bias = jnp.dot(jnp.ones((16, 4 * PIX), BF16), grad[...], preferred_element_type=F32)
     row = lax.broadcasted_iota(jnp.int32, (16, LANES), 0)
     empty = jnp.zeros((16, LANES), BF16)
     for half in range(2):
-        block = jnp.zeros((16, LANES), F32)
-        for k in range(3):
-            start = half * HALF + k * LANES
-            block = jnp.where(row == k, bias[:, start : start + LANES], block)
-        block = block.astype(BF16)
+        if half == 1:
+            bias = pltpu.roll(bias, CH - OWN, 1)
+        rows = jnp.zeros((16, LANES), F32)
+        for k in range(BLOCKS):
+            rows = jnp.where(row == k, bias[:, k * LANES : (k + 1) * LANES], rows)
+        rows = rows.astype(BF16)
         for z in range(8):
             for s in range(36, 40):
-                outs[half][(s // 5) * 8 + z, (s % 5) * 16 : (s % 5) * 16 + 16, :] = block if s == 36 else empty
-
-
-def spread(out_ref, matrix, start):
-    for z in range(8):
-        for j in range(BLOCKS):
-            for part in range(3):
-                s = start + j * 3 + part
-                row = z * OWN + part * 16
-                out_ref[(s // 5) * 8 + z, (s % 5) * 16 : (s % 5) * 16 + 16, :] = matrix[
-                    row : row + 16, j * LANES : (j + 1) * LANES
-                ]
-
-
-def weight_grads(normed, scaled, act, grad, two, layer):
+                outs[half][(s // 5) * 8 + z, (s % 5) * 16 : (s % 5) * 16 + 16, :] = rows if s == 36 else empty
+
+
+def spread(outs, matrix, start):
+    for half in range(2):
+        for z in range(8):
+            for j in range(BLOCKS):
+                for part in range(3):
+                    s = start + j * 3 + part
+                    row = z * UNITS + half * OWN + part * 16
+                    outs[half][(s // 5) * 8 + z, (s % 5) * 16 : (s % 5) * 16 + 16, :] = matrix[
+                        row : row + 16, j * LANES : (j + 1) * LANES
+                    ]
+
+
+def hidden(normed, scaled, pack, layer):
     return pl.pallas_call(
-        weights_kernel,
-        out_shape=(
-            jax.ShapeDtypeStruct((64, 80, LANES), BF16),
-            jax.ShapeDtypeStruct((64, 80, LANES), BF16),
-            jax.ShapeDtypeStruct((8, CH), F32),
-        ),
-        in_specs=[whole()] * 12,
-        out_specs=(whole(),) * 3,
-        compiler_params=params(24),
+        hidden_kernel,
+        grid=(1,),
+        out_shape=(jax.ShapeDtypeStruct((PIX, CH), BF16),) * 4
+        + (jax.ShapeDtypeStruct((64, 80, LANES), BF16),) * 2
+        + (jax.ShapeDtypeStruct((8, CH), F32),),
+        in_specs=[pl.BlockSpec(memory_space=pl.ANY)] * 9 + [block(1, CH)],
+        out_specs=(block(PIX, CH),) * 4 + (block(64, 80, LANES),) * 2 + (block(8, CH),),
+        scratch_shapes=[
+            pltpu.VMEM((4 * PIX, CH), BF16),
+            pltpu.VMEM((4 * PIX, CH), BF16),
+            pltpu.VMEM((8, PACK, CH), BF16),
+            pltpu.VMEM((4 * PIX, CH), BF16),
+            pltpu.VMEM((4 * PIX, CH), BF16),
+            pltpu.SemaphoreType.DMA((9,)),
+        ],
+        compiler_params=params(40),
         interpret=INTERPRET,
-        name="weight_grads",
-    )(*normed, *scaled, act, grad, two, layer)
+        name="hidden",
+    )(*normed, *scaled, pack, layer)
 
 
 def backward_kernel(
@@ -411,42 +375,69 @@
     )(conv, kernel, scaled)
 
 
-def unpack_kernel(factor_ref, core_ref, mine_ref, other_ref, first_ref, second_ref):
-    factor = factor_ref[0]
-    even = core_ref[0] == 0
-
-    def column(kind, j):
-        pieces = []
-        for xh in range(2):
-            own, got = [], []
-            for part in range(3):
-                s = kind * 18 + j * 3 + part
-                rows = slice((s % 5) * 16, (s % 5) * 16 + 16)
-                own.append(mine_ref[xh, s // 5, rows, :].astype(F32))
-                got.append(other_ref[xh, s // 5, rows, :].astype(F32))
-            own, got = jnp.concatenate(own), jnp.concatenate(got)
-            pieces += [jnp.where(even, own, got), jnp.where(even, got, own)]
-        return jnp.concatenate(pieces) * factor
-
+def finish_kernel(
+    images, place_ref, small_ref, pre_ref, mine_ref, mine_core_ref, across_ref, across_core_ref,
+    image_ref, first_ref, second_ref, bias_ref, kernel_ref, gain_ref, scale_ref, gathered,
+):
+    half, core, column = place_ref[0], place_ref[1], place_ref[2]
+    factor = images / small_ref[0, 51:52, :]
+    gathered[half * 2 + core] = mine_ref[...]
+    gathered[half * 2 + 1 - core] = mine_core_ref[...]
+    gathered[(1 - half) * 2 + core] = across_ref[...]
+    gathered[(1 - half) * 2 + 1 - core] = across_core_ref[...]
+    lane = lax.broadcasted_iota(jnp.int32, (8, CH), 1)
+    bias = jnp.zeros((8, CH), F32)
+    for q in range(4):
+        rows = gathered[q, 7, 16:32, :].astype(F32)
+        line = jnp.concatenate([rows[k : k + 1, :] for k in range(BLOCKS)], axis=1)
+        line = pltpu.roll(jnp.broadcast_to(line, (8, CH)), lax.rem(CH - column * UNITS + q * OWN, CH), 1)
+        bias = jnp.where((lane >= q * OWN) & (lane < (q + 1) * OWN), line, bias)
+    bias_ref[...] = bias[0:1, 0:192] * jnp.concatenate([factor, factor[:, 0:64]], axis=1)
     for j in range(BLOCKS):
         lanes = slice(j * LANES, (j + 1) * LANES)
-        second_ref[:, lanes] = column(0, j)
-        first_ref[lanes, :] = column(1, j).T
-
-
-def unpack(factor, core, mine, other):
+        image_ref[0, :, :, lanes] = (pre_ref[0, :, :, lanes] * factor.reshape(1, 1, LANES)).astype(BF16)
+        for a in range(7):
+            kernel_ref[a, :, lanes] = small_ref[j, a * 7 : a * 7 + 7, :] * factor
+        gain_ref[:, lanes] = small_ref[j, 49:50, :] * factor
+        scale_ref[:, lanes] = small_ref[j, 50:51, :] * factor
+        for q in range(4):
+            for part in range(3):
+                rows = slice(q * OWN + part * 16, q * OWN + part * 16 + 16)
+                for out_ref, start in ((second_ref, 0), (first_ref, 18)):
+                    s = start + j * 3 + part
+                    piece = gathered[q, s // 5, (s % 5) * 16 : (s % 5) * 16 + 16, :]
+                    out_ref[rows, lanes] = piece.astype(F32) * factor
+
+
+def finish(images, place, small, pre, mine, mine_core, across, across_core):
     return pl.pallas_call(
-        unpack_kernel,
+        functools.partial(finish_kernel, images),
+        grid=(1,),
         out_shape=(
-            jax.ShapeDtypeStruct((CH, 192), F32),
+            jax.ShapeDtypeStruct((1, ROWS, COLS, CH), BF16),
             jax.ShapeDtypeStruct((192, CH), F32),
-        ),
-        in_specs=[scalars(), scalars(), whole(), whole()],
-        out_specs=(whole(),) * 2,
-        compiler_params=params(16),
+            jax.ShapeDtypeStruct((192, CH), F32),
+            jax.ShapeDtypeStruct((1, 192), F32),
+            jax.ShapeDtypeStruct((7, 7, CH), F32),
+            jax.ShapeDtypeStruct((1, CH), F32),
+            jax.ShapeDtypeStruct((1, CH), F32),
+        ),
+        in_specs=[scalars(), block(BLOCKS, 64, LANES), block(1, ROWS, COLS, CH)]
+        + [block(8, 80, LANES)] * 4,
+        out_specs=(
+            block(1, ROWS, COLS, CH),
+            block(192, CH),
+            block(192, CH),
+            block(1, 192),
+            block(7, 7, CH),
+            block(1, CH),
+            block(1, CH),
+        ),
+        scratch_shapes=[pltpu.VMEM((4, 8, 80, LANES), BF16)],
+        compiler_params=params(24),
         interpret=INTERPRET,
-        name="unpack",
-    )(factor, core, mine, other)
+        name="finish",
+    )(place, small, pre, mine, mine_core, across, across_core)
 
 
 def to_all(value, axes):
@@ -480,10 +471,8 @@
     half = lax.axis_index("xh")
     column = lax.axis_index("z")
     place = jnp.stack([half * 2 + core, column]).astype(jnp.int32)
-    one, two = pack_weights(place, first_weight, first_bias, second_weight)
-    two = lax.all_gather(two, "z", axis=0, tiled=True).reshape(8, 2 * OWN, CH)
-    one = to_all(one, "z")
-    one_other = swap_core(one)
+    packed = pack_weights(place, first_weight, first_bias, second_weight)
+    packed = lax.all_gather(packed, "z", axis=0, tiled=True).reshape(8, PACK, CH)
 
     kernel = conv_kernel.reshape(49, CH)
     gain = norm_gain.reshape(1, CH)
@@ -497,10 +486,7 @@
     scaled = jnp.pad(scaled, ((0, 0), (0, WIDE - COLS), (0, 0))).reshape(PIX, CH)
     scaled_all = ring_share(scaled)
 
-    act, slope = activations(normed_all, one, one_other)
-    preact_grad, *parts = hidden(scaled_all, one, one_other, two, layer, slope)
-    grads, other, scale = weight_grads(normed_all, scaled_all, act, preact_grad, two, layer)
-    parts[1], parts[2], parts[3], other = lax.optimization_barrier((parts[1], parts[2], parts[3], other))
+    *parts, grads, other, scale = hidden(normed_all, scaled_all, packed, layer)
     got = swap_core(other)
     grads = (grads.astype(F32) + got.astype(F32)).astype(BF16)
     grads = lax.all_to_all(grads, ("y", "z"), 0, 0, tiled=True)
@@ -519,33 +505,24 @@
     both = to_all(jnp.concatenate([grads.astype(BF16), high, low], axis=0), "y")
     small = jnp.sum(both[:, 80:128, :].astype(F32) + both[:, 128:176, :].astype(F32), axis=0)
     small = to_all(small, TEAM).reshape(BLOCKS, 64, LANES)
-    small = small.transpose(1, 0, 2).reshape(64, CH)
 
     mine = both[:, 0:80, :]
     across = lax.ppermute(mine, "xh", [(0, 1), (1, 0)])
-    mine = jnp.where(half == 0, jnp.stack([mine, across]), jnp.stack([across, mine]))
-    other = swap_core(mine)
-
-    images = lax.axis_size(REPLICA) * lax.axis_size(SHARD)
-    factor = images / small[51, 0]
-    grad_first, grad_second = unpack(factor.reshape(1), core.reshape(1).astype(jnp.int32), mine, other)
-
-    def bias_of(gathered):
-        rows = gathered[:, 7, 16:19, :].reshape(2, HALF).astype(F32)
-        return lax.dynamic_slice(rows, (0, column * OWN), (2, OWN))
-
-    bias_mine, bias_other = bias_of(mine), bias_of(other)
-    bias = jnp.stack([jnp.where(core == 0, bias_mine, bias_other), jnp.where(core == 0, bias_other, bias_mine)], axis=1)
-    grad_image = (factor * input_grad(conv_grad, kernel, scaled)).astype(BF16)
-    small = factor * small
+    pre = input_grad(conv_grad, kernel, scaled)
+    images = float(lax.axis_size(REPLICA) * lax.axis_size(SHARD))
+    grad_image, grad_first, grad_second, grad_bias, grad_kernel, grad_gain, grad_scale = finish(
+        images,
+        jnp.stack([half, core, column]).astype(jnp.int32),
+        small, pre, mine, swap_core(mine), across, swap_core(across),
+    )
     return (
         grad_image,
-        grad_first,
-        factor * bias.reshape(4 * OWN),
+        grad_first.T,
+        grad_bias.reshape(4 * OWN),
         grad_second,
-        small[0:49].reshape(7, 7, CH),
-        small[49],
-        small[50],
+        grad_kernel,
+        grad_gain.reshape(CH),
+        grad_scale.reshape(CH),
     )
 
 

time: 235 us -> 204 us (0.87)
  waiting for transfers between devices: 63.6 us -> 45.3 us
  local copies, waits for them, and re-layouts: 23.1 us -> 13.7 us
  starting transfers between devices: 73.9 us -> 68.1 us
    all_to_all x2 -> x1, waiting for transfers between devices: 26.6 us -> 0.01 us  [to_all(): lax.all_to_all(jnp.broadcast_to(value, (count, *value.shape)), axes, 0, 0...]
    all_to_all x2 -> x1, starting transfers between devices: 19.9 us -> 9.53 us  [to_all(): lax.all_to_all(jnp.broadcast_to(value, (count, *value.shape)), axes, 0, 0...]
    unnamed x70 -> x36, local copies, waits for them, and re-layouts: 18.7 us -> 11.9 us
    all_gather x1, waiting for transfers between devices: 0.01 us -> 4.68 us  [per_device(): lax.all_gather(packed, 'z', axis=0, tiled=True).reshape(8, PACK, CH)]
    ppermute x9, waiting for transfers between devices: 27.3 us -> 30.6 us  [ring(): return lax.ppermute(value, RING, [(i, (i + shift) % 4) for i in range(4)])]
    ppermute x3, starting transfers between devices: 7.41 us -> 9.95 us  [swap_core(): return lax.ppermute(value, 'core', [(0, 1), (1, 0)])]
    pallas_call x5 -> x3, Pallas kernels: 10.9 us -> 12.8 us  [the longest x1 9.47 us: hidden(): pl.pallas_call(hidden_kernel, grid=(1,), out_shape=(jax.ShapeDtypeStruct(...]
  transfers between devices with their start and end apart: 20 -> 19, of which waited for: 13 -> 9; matrix products, arithmetic and copies ran while one was open for 2% -> 2% of each run, Pallas kernels for 5% -> 5%
where the time goes in v3:
time: 204 us; the launch traced here: 202 us
  starting transfers between devices  68.1 us (33%)
  waiting for transfers between devices  45.3 us (22%)
  blocking collectives  31.5 us (15%)
  Pallas kernels  22.1 us (11%)
  between operations  15.1 us (7%)
  local copies, waits for them, and re-layouts  13.7 us (7%)
  other arithmetic  6.67 us (3%)
    all_to_all x2, blocking collectives, to_all(): lax.all_to_all(jnp.broadcast_to(value, (count, *value.shape)), axes, 0, 0...  31.5 us
    ppermute x9, waiting for transfers between devices, ring(): return lax.ppermute(value, RING, [(i, (i + shift) % 4) for i in range(4)])  30.6 us
    ppermute x9, starting transfers between devices, ring(): return lax.ppermute(value, RING, [(i, (i + shift) % 4) for i in range(4)])  29.1 us
    unnamed x36, local copies, waits for them, and re-layouts  11.9 us
    all_to_all x1, starting transfers between devices, per_device(): grads = lax.all_to_all(grads, ('y', 'z'), 0, 0, tiled=True)  10.3 us
    ppermute x3, starting transfers between devices, swap_core(): return lax.ppermute(value, 'core', [(0, 1), (1, 0)])  9.95 us
    all_to_all x1, starting transfers between devices, to_all(): lax.all_to_all(jnp.broadcast_to(value, (count, *value.shape)), axes, 0, 0...  9.53 us
    pallas_call x1, Pallas kernels, hidden(): pl.pallas_call(hidden_kernel, grid=(1,), out_shape=(jax.ShapeDtypeStruct(...  9.47 us
  transfers between devices with their start and end apart: 19, of which 9 were waited for; matrix products, arithmetic and copies ran while one was open for 2% of the time, Pallas kernels for 5%

profile of v3, /device:TPU:1, one launch (start us, length us, event | category | flops | bytes accessed | tf_op | source)
XLA Modules:
  0.0 202.4 jit_solution(13218956381063298046)
XLA Ops:
  7.2 0.0 all-gather.2.cloned.1.call-start
  7.2 0.1 pad_add_fusion.1.place_ref
  7.3 1.0 copy-done.10
  8.3 1.0 copy-done.11
  9.2 0.7 copy-done.12
  9.9 1.5 pack.1
  11.5 0.0 all-gather.2.cloned.1.call-update
  11.5 0.9 reshape.55.kernel_ref
  12.4 2.8 %conv_norm.1 = (bf16[224,768]{1,0:T(8,128)(2,1)S(1)}, f32[6,14,16,128]{3,2,1,0:T(8,128)S(1)}, f32[14,16,128]{2,1,0:T(8,128)S(1)}) custom-call(bf16[14,14,768]{2,1,0:T(8,128)(2,1)S(1)} %bitcast.36, bf16[49,768]{1,0:T(8,128)(2,1)S(1)} %reshape.55.kernel_ref, f32[1,768]{1,0:T(1,128)S(1)} %reshape.56.gain_ref), custom_call_target="tpu_custom_call" | custom-call | tf_op jit(solution)/shard_map/conv_norm/pallas_call | solution.py:140
  15.3 4.0 %collective-permute-start = (bf16[224,768]{1,0:T(8,128)(2,1)S(1)}, bf16[224,768]{1,0:T(8,128)(2,1)S(1)}, u32[]{:S(2)}, u32[]{:S(2)}) collective-permute-start(bf16[224,768]{1,0:T(8,128)(2,1)S(1)} %get-tuple-element.28.refs_0_), channel_id=1, source_target_pairs={{0,8},{8,32},{32,40},{40,0},{1,9},{9,33},{33,41},{41,1},{2,10},{10... | collective-permute-start | bytes 1032200 | tf_op jit(solution)/shard_map/ppermute | solution.py:453
  19.2 4.4 %collective-permute-start.1 = (bf16[224,768]{1,0:T(8,128)(2,1)S(1)}, bf16[224,768]{1,0:T(8,128)(2,1)S(1)}, u32[]{:S(2)}, u32[]{:S(2)}) collective-permute-start(bf16[224,768]{1,0:T(8,128)(2,1)S(1)} %get-tuple-element.28.refs_0_), channel_id=1, source_target_pairs={{0,32},{8,40},{32,0},{40,8},{1,33},{9,41},{33,1},{41,9},{2,34},{10... | collective-permute-start | bytes 1032200 | tf_op jit(solution)/shard_map/ppermute | solution.py:453
  23.6 3.1 %collective-permute-start.2 = (bf16[224,768]{1,0:T(8,128)(2,1)S(1)}, bf16[224,768]{1,0:T(8,128)(2,1)S(1)}, u32[]{:S(2)}, u32[]{:S(2)}) collective-permute-start(bf16[224,768]{1,0:T(8,128)(2,1)S(1)} %get-tuple-element.28.refs_0_), channel_id=1, source_target_pairs={{0,40},{8,0},{32,8},{40,32},{1,41},{9,1},{33,9},{41,33},{2,42},{10... | collective-permute-start | bytes 1032200 | tf_op jit(solution)/shard_map/ppermute | solution.py:453
  27.3 0.6 fusion.1
  28.0 1.7 fusion
  29.7 2.2 %collective-permute-start.3 = (bf16[224,768]{1,0:T(8,128)(2,1)S(1)}, bf16[224,768]{1,0:T(8,128)(2,1)S(1)}, u32[]{:S(2)}, u32[]{:S(2)}) collective-permute-start(bf16[224,768]{1,0:T(8,128)(2,1)S(1)} %bitcast.30), channel_id=1, source_target_pairs={{0,8},{8,32},{32,40},{40,0},{1,9},{9,33},{33,41},{41,1},{2,10},{10... | collective-permute-start | bytes 1032200 | tf_op jit(solution)/shard_map/ppermute | solution.py:453
  31.9 2.8 %collective-permute-start.4 = (bf16[224,768]{1,0:T(8,128)(2,1)S(1)}, bf16[224,768]{1,0:T(8,128)(2,1)S(1)}, u32[]{:S(2)}, u32[]{:S(2)}) collective-permute-start(bf16[224,768]{1,0:T(8,128)(2,1)S(1)} %bitcast.31), channel_id=1, source_target_pairs={{0,32},{8,40},{32,0},{40,8},{1,33},{9,41},{33,1},{41,9},{2,34},{10... | collective-permute-start | bytes 1032200 | tf_op jit(solution)/shard_map/ppermute | solution.py:453
  34.7 0.0 collective-permute-done.refs_1_
  34.7 3.4 %collective-permute-start.5 = (bf16[224,768]{1,0:T(8,128)(2,1)S(1)}, bf16[224,768]{1,0:T(8,128)(2,1)S(1)}, u32[]{:S(2)}, u32[]{:S(2)}) collective-permute-start(bf16[224,768]{1,0:T(8,128)(2,1)S(1)} %bitcast.32), channel_id=1, source_target_pairs={{0,40},{8,0},{32,8},{40,32},{1,41},{9,1},{33,9},{41,33},{2,42},{10... | collective-permute-start | bytes 1032200 | tf_op jit(solution)/shard_map/ppermute | solution.py:453
  38.2 0.0 collective-permute-done.1.refs_2_
  38.2 14.5 %collective-permute-done.3.refs_5_ = bf16[224,768]{1,0:T(8,128)(2,1)S(1)} collective-permute-done((bf16[224,768]{1,0:T(8,128)(2,1)S(1)}, bf16[224,768]{1,0:T(8,128)(2,1)S(1)}, u32[]{:S(2)}, u32[]{:S(2)}) %collective-permute-start.3) | collective-permute-done | bytes 344096 | tf_op jit(solution)/shard_map/ppermute | solution.py:453
  52.7 0.7 copy-done.4
  53.4 0.7 copy-done.6
  54.1 0.0 collective-permute-done.5.refs_7_
  54.1 0.7 copy-done.8
  54.9 4.7 %all-gather.2.cloned.1.call-done = bf16[1664,768]{1,0:T(8,128)(2,1)} async-done(((bf16[208,768]{1,0:T(8,128)(2,1)}), bf16[1664,768]{1,0:T(8,128)(2,1)}) %all-gather.2.cloned.1.call-update) | async-done | bytes 2555920 | tf_op jit(solution)/shard_map/all_gather | solution.py:475
  59.6 1.7 copy-done
  61.3 1.0 copy-done.5
  62.3 1.0 copy-done.7
  63.2 1.0 copy-done.9
  64.2 9.5 %hidden.1 = (bf16[224,768]{1,0:T(8,128)(2,1)S(1)}, bf16[224,768]{1,0:T(8,128)(2,1)}, bf16[224,768]{1,0:T(8,128)(2,1)}, bf16[224,768]{1,0:T(8,128)(2,1)S(1)}, bf1...) custom-call(bf16[224,768]{1,0:T(8,128)(2,1)S(1)} %get-tuple-element.28.refs_0_, ...), custom_call_target="tpu_custom_call" | custom-call | tf_op jit(solution)/shard_map/hidden/pallas_call | solution.py:233
  73.7 0.0 copy-start.13
  73.7 0.7 copy-done.13
  74.4 5.6 %collective-permute-start.12 = (bf16[64,80,128]{2,1,0:T(8,128)(2,1)S(1)}, bf16[64,80,128]{2,1,0:T(8,128)(2,1)S(1)}, u32[]{:S(2)}, u32[]{:S(2)}) collective-permute-start(bf16[64,80,128]{2,1,0:T(8,128)(2,1)S(1)} %get-tuple-element.38), channel_id=1, source_target_pairs={{0,16},{16,0},{1,17},{17,1},{2,18},{18,2},{3,19},{19,3},{4,20},{20... | collective-permute-start | bytes 3932168 | tf_op jit(solution)/shard_map/ppermute | solution.py:449
  80.1 2.6 %collective-permute-done.12 = bf16[64,80,128]{2,1,0:T(8,128)(2,1)S(1)} collective-permute-done((bf16[64,80,128]{2,1,0:T(8,128)(2,1)S(1)}, bf16[64,80,128]{2,1,0:T(8,128)(2,1)S(1)}, u32[]{:S(2)}, u32[]{:S(2)}) %collective-permute-start.12) | collective-permute-done | bytes 1310752 | tf_op jit(solution)/shard_map/ppermute | solution.py:449
  82.7 1.4 add_convert_fusion
  84.1 10.3 %all-to-all-start = ((bf16[64,80,128]{2,1,0:T(8,128)(2,1)}), bf16[64,80,128]{2,1,0:T(8,128)(2,1)}, u32[]{:S(2)}, u32[]{:S(2)}) async-start(bf16[64,80,128]{2,1,0:T(8,128)(2,1)} %add_convert_fusion), calls=%async_computation | async-start | bytes 2621440 | tf_op jit(solution)/shard_map/all_to_all | solution.py:492
  94.4 4.3 %collective-permute-start.6 = (bf16[224,768]{1,0:T(8,128)(2,1)}, bf16[224,768]{1,0:T(8,128)(2,1)S(1)}, u32[]{:S(2)}, u32[]{:S(2)}) collective-permute-start(bf16[224,768]{1,0:T(8,128)(2,1)} %get-tuple-element.30), channel_id=1, source_target_pairs={{0,40},{8,0},{32,8},{40,32},{1,41},{9,1},{33,9},{41,33},{2,42},{10... | collective-permute-start | bytes 1032200 | tf_op jit(solution)/shard_map/ppermute | solution.py:453
  98.7 2.5 %collective-permute-start.7 = (bf16[224,768]{1,0:T(8,128)(2,1)}, bf16[224,768]{1,0:T(8,128)(2,1)S(1)}, u32[]{:S(2)}, u32[]{:S(2)}) collective-permute-start(bf16[224,768]{1,0:T(8,128)(2,1)} %get-tuple-element.31), channel_id=1, source_target_pairs={{0,32},{8,40},{32,0},{40,8},{1,33},{9,41},{33,1},{41,9},{2,34},{10... | collective-permute-start | bytes 1032200 | tf_op jit(solution)/shard_map/ppermute | solution.py:453
  101.2 2.5 %collective-permute-start.8 = (bf16[224,768]{1,0:T(8,128)(2,1)S(1)}, bf16[224,768]{1,0:T(8,128)(2,1)S(1)}, u32[]{:S(2)}, u32[]{:S(2)}) collective-permute-start(bf16[224,768]{1,0:T(8,128)(2,1)S(1)} %copy-done.14), channel_id=1, source_target_pairs={{0,8},{8,32},{32,40},{40,0},{1,9},{9,33},{33,41},{41,1},{2,10},{10... | collective-permute-start | bytes 1032200 | tf_op jit(solution)/shard_map/ppermute | solution.py:453
  103.7 2.8 %collective-permute-done.6.one_ref = bf16[224,768]{1,0:T(8,128)(2,1)S(1)} collective-permute-done((bf16[224,768]{1,0:T(8,128)(2,1)}, bf16[224,768]{1,0:T(8,128)(2,1)S(1)}, u32[]{:S(2)}, u32[]{:S(2)}) %collective-permute-start.6) | collective-permute-done | bytes 344096 | tf_op jit(solution)/shard_map/ppermute | solution.py:453
  106.5 4.6 %collective-permute-done.7.two_ref = bf16[224,768]{1,0:T(8,128)(2,1)S(1)} collective-permute-done((bf16[224,768]{1,0:T(8,128)(2,1)}, bf16[224,768]{1,0:T(8,128)(2,1)S(1)}, u32[]{:S(2)}, u32[]{:S(2)}) %collective-permute-start.7) | collective-permute-done | bytes 344096 | tf_op jit(solution)/shard_map/ppermute | solution.py:453
  111.1 8.7 %collective-permute-done.8.three_ref = bf16[224,768]{1,0:T(8,128)(2,1)S(1)} collective-permute-done((bf16[224,768]{1,0:T(8,128)(2,1)S(1)}, bf16[224,768]{1,0:T(8,128)(2,1)S(1)}, u32[]{:S(2)}, u32[]{:S(2)}) %collective-permute-start.8) | collective-permute-done | bytes 344096 | tf_op jit(solution)/shard_map/ppermute | solution.py:453
  119.8 0.7 copy-done.2
  120.5 1.0 copy-done.3
  121.5 3.8 %norm_back.1 = (f32[6,64,128]{2,1,0:T(8,128)S(1)}, f32[6,14,16,128]{3,2,1,0:T(8,128)S(1)}) custom-call(f32[1]{0:T(128)} %bitcast.4.weight_ref, bf16[224,768]{1,0:T(8,128)(2,1)S(1)} %get-tuple-element.29.zero_ref, bf16[224,768]{1,0:T(8,128)(2,1)S(1)} %collective-permute-done.6.one_ref, bf16[224,768]{1,0:T(8,128)(2,1)S(1)} %collective-permute-done.7.two_ref, ...), custom_call_target="tpu_custom_call" | custom-call | tf_op jit(solution)/shard_map/norm_back/pallas_call | solution.py:312
  125.4 2.3 %collective-permute-start.9 = (f32[2,2,48,128]{3,2,1,0:T(8,128)S(1)}, f32[2,2,48,128]{3,2,1,0:T(8,128)S(1)}, u32[]{:S(2)}, u32[]{:S(2)}) collective-permute-start(f32[2,2,48,128]{3,2,1,0:T(8,128)S(1)} %dynamic-slice_bitcast_fusion), channel_id=1, source_target_pairs={{0,16},{16,0},{1,17},{17,1},{2,18},{18,2},{3,19},{19,3},{4,20},{20... | collective-permute-start | bytes 294920 | tf_op jit(solution)/shard_map/ppermute | solution.py:464
  127.7 0.9 collective-permute-done.9
  128.6 1.9 collective-permute-start.10
  130.6 2.9 %collective-permute-done.10 = f32[2,48,128]{2,1,0:T(8,128)S(1)} collective-permute-done((f32[2,48,128]{2,1,0:T(8,128)S(1)}, f32[2,48,128]{2,1,0:T(8,128)S(1)}, u32[]{:S(2)}, u32[]{:S(2)}) %collective-permute-start.10) | collective-permute-done | bytes 49184 | tf_op jit(solution)/shard_map/ppermute | solution.py:464
  133.5 2.5 %collective-permute-start.11 = (f32[48,128]{1,0:T(8,128)S(1)}, f32[48,128]{1,0:T(8,128)S(1)}, u32[]{:S(2)}, u32[]{:S(2)}) collective-permute-start(f32[48,128]{1,0:T(8,128)S(1)} %dynamic-slice_bitcast_fusion.2), channel_id=1, source_target_pairs={{0,32},{32,0},{1,33},{33,1},{2,34},{34,2},{3,35},{35,3},{4,36},{36... | collective-permute-start | bytes 73736 | tf_op jit(solution)/shard_map/ppermute | solution.py:464
  136.0 3.6 %collective-permute-done.11 = f32[48,128]{1,0:T(8,128)S(1)} collective-permute-done((f32[48,128]{1,0:T(8,128)S(1)}, f32[48,128]{1,0:T(8,128)S(1)}, u32[]{:S(2)}, u32[]{:S(2)}) %collective-permute-start.11) | collective-permute-done | bytes 24608 | tf_op jit(solution)/shard_map/ppermute | solution.py:464
  139.6 1.5 convert_reduce_fusion
  141.1 14.7 %all_to_all.20 = f32[8,48,128]{2,1,0:T(8,128)S(1)} all-to-all(f32[8,48,128]{2,1,0:T(8,128)S(1)} %broadcast_in_dim.14), channel_id=1, replica_groups=mesh['y'=8,'xh'=2,'core'=2,'xl'=2,'z'=8] {'z'}, dimensions={0} | all-to-all | bytes 393216 | tf_op jit(solution)/shard_map/all_to_all | solution.py:445
  155.9 16.8 %all_to_all.21 = bf16[8,176,128]{2,1,0:T(8,128)(2,1)S(1)} all-to-all(bf16[8,176,128]{2,1,0:T(8,128)(2,1)S(1)} %broadcast_in_dim.15), channel_id=1, replica_groups=mesh['y'=8,'xh'=2,'core'=2,'xl'=2,'z'=8] {'y'}, dimensions={0} | all-to-all | bytes 720896 | tf_op jit(solution)/shard_map/all_to_all | solution.py:445
  172.7 2.5 %collective-permute-start.14 = (bf16[8,80,128]{2,1,0:T(8,128)(2,1)S(1)}, bf16[8,80,128]{2,1,0:T(8,128)(2,1)S(1)}, u32[]{:S(2)}, u32[]{:S(2)}) collective-permute-start(bf16[8,80,128]{2,1,0:T(8,128)(2,1)S(1)} %slice.14.mine_ref), channel_id=1, source_target_pairs={{0,32},{32,0},{1,33},{33,1},{2,34},{34,2},{3,35},{35,3},{4,36},{36... | collective-permute-start | bytes 491528 | tf_op jit(solution)/shard_map/ppermute | solution.py:510
  175.2 0.7 broadcast_in_dim.16
  175.9 9.5 %all-to-all-start.3 = ((f32[8,48,128]{2,1,0:T(8,128)}), f32[8,48,128]{2,1,0:T(8,128)S(1)}, u32[]{:S(2)}, u32[]{:S(2)}) async-start(f32[8,48,128]{2,1,0:T(8,128)} %broadcast_in_dim.16), calls=%async_computation.3 | async-start | bytes 393216 | tf_op jit(solution)/shard_map/all_to_all | solution.py:445
  185.5 1.9 collective-permute-start.13
  187.4 2.4 %collective-permute-start.15 = (bf16[8,80,128]{2,1,0:T(8,128)(2,1)S(1)}, bf16[8,80,128]{2,1,0:T(8,128)(2,1)S(1)}, u32[]{:S(2)}, u32[]{:S(2)}) collective-permute-start(bf16[8,80,128]{2,1,0:T(8,128)(2,1)S(1)} %collective-permute-done.14.across_ref), channel_id=1, source_target_pairs={{0,16},{16,0},{1,17},{17,1},{2,18},{18,2},{3,19},{19,3},{4,20},{20... | collective-permute-start | bytes 491528 | tf_op jit(solution)/shard_map/ppermute | solution.py:449
  189.8 0.1 pad_add_fusion.place_ref
  189.9 2.6 %input_grad.1.pre_ref = f32[1,14,14,768]{3,2,1,0:T(8,128)S(1)} custom-call(f32[6,14,16,128]{3,2,1,0:T(8,128)S(1)} %get-tuple-element.41.conv_ref, bf16[49,768]{1,0:T(8,128)(2,1)S(1)} %reshape.55.kernel_ref, bf16[224,768]{1,0:T(8,128)(2,1)S(1)} %bitcast.34), custom_call_target="tpu_custom_call" | custom-call | tf_op jit(solution)/shard_map/input_grad/pallas_call | solution.py:361
  192.5 1.8 finish.1
  194.4 0.6 reduce
  195.0 0.6 reduce.1
  (45 shorter events, 0.3 us)
Async XLA Ops:
  7.2 5.3 %copy-start.1 = (bf16[1,14,14,768]{3,2,1,0:T(8,128)(2,1)S(1)}, bf16[1,14,14,768]{3,2,1,0:T(8,128)(2,1)}, u32[]{:S(2)}) copy-start(bf16[1,14,14,768]{3,2,1,0:T(8,128)(2,1)} %param.10) | copy-start | bytes 903172
  7.2 52.4 %all-gather.2.cloned.1.call-start = ((), (), s32[]{:S(2)}) async-start(), calls=%async_computation.4 | async-start | bytes 2875392 | tf_op jit(solution)/shard_map/all_gather | solution.py:475
  7.3 1.0 copy-start.10
  8.3 1.0 copy-start.11
  9.2 0.7 copy-start.12
  9.9 2.5 %copy-start.15 = (f32[768]{0:T(1024)S(1)}, f32[768]{0:T(1024)}, u32[]{:S(2)}) copy-start(f32[768]{0:T(1024)} %param.15) | copy-start | bytes 9220
  9.9 17.4 %copy-start.17 = (f32[4]{0:T(128)S(1)}, f32[4]{0:T(128)}, u32[]{:S(2)}) copy-start(f32[4]{0:T(128)} %param.13) | copy-start | bytes 52
  11.5 26.7 %copy-start.16 = (f32[768]{0:T(1024)S(1)}, f32[768]{0:T(1024)}, u32[]{:S(2)}) copy-start(f32[768]{0:T(1024)} %param.19) | copy-start | bytes 9220
  15.3 19.4 %collective-permute-start = (bf16[224,768]{1,0:T(8,128)(2,1)S(1)}, bf16[224,768]{1,0:T(8,128)(2,1)S(1)}, u32[]{:S(2)}, u32[]{:S(2)}) collective-permute-start(bf16[224,768]{1,0:T(8,128)(2,1)S(1)} %get-tuple-element.28.refs_0_), channel_id=1, source_target_pairs={{0,8},{8,32},{32,40},{40,0},{1,9},{9,33},{33,41},{41,1},{2,10},{10... | collective-permute-start | bytes 1032200 | tf_op jit(solution)/shard_map/ppermute | solution.py:453
  19.2 18.9 %collective-permute-start.1 = (bf16[224,768]{1,0:T(8,128)(2,1)S(1)}, bf16[224,768]{1,0:T(8,128)(2,1)S(1)}, u32[]{:S(2)}, u32[]{:S(2)}) collective-permute-start(bf16[224,768]{1,0:T(8,128)(2,1)S(1)} %get-tuple-element.28.refs_0_), channel_id=1, source_target_pairs={{0,32},{8,40},{32,0},{40,8},{1,33},{9,41},{33,1},{41,9},{2,34},{10... | collective-permute-start | bytes 1032200 | tf_op jit(solution)/shard_map/ppermute | solution.py:453
  23.6 14.6 %collective-permute-start.2 = (bf16[224,768]{1,0:T(8,128)(2,1)S(1)}, bf16[224,768]{1,0:T(8,128)(2,1)S(1)}, u32[]{:S(2)}, u32[]{:S(2)}) collective-permute-start(bf16[224,768]{1,0:T(8,128)(2,1)S(1)} %get-tuple-element.28.refs_0_), channel_id=1, source_target_pairs={{0,40},{8,0},{32,8},{40,32},{1,41},{9,1},{33,9},{41,33},{2,42},{10... | collective-permute-start | bytes 1032200 | tf_op jit(solution)/shard_map/ppermute | solution.py:453
  29.7 23.0 %collective-permute-start.3 = (bf16[224,768]{1,0:T(8,128)(2,1)S(1)}, bf16[224,768]{1,0:T(8,128)(2,1)S(1)}, u32[]{:S(2)}, u32[]{:S(2)}) collective-permute-start(bf16[224,768]{1,0:T(8,128)(2,1)S(1)} %bitcast.30), channel_id=1, source_target_pairs={{0,8},{8,32},{32,40},{40,0},{1,9},{9,33},{33,41},{41,1},{2,10},{10... | collective-permute-start | bytes 1032200 | tf_op jit(solution)/shard_map/ppermute | solution.py:453
  31.9 21.5 %collective-permute-start.4 = (bf16[224,768]{1,0:T(8,128)(2,1)S(1)}, bf16[224,768]{1,0:T(8,128)(2,1)S(1)}, u32[]{:S(2)}, u32[]{:S(2)}) collective-permute-start(bf16[224,768]{1,0:T(8,128)(2,1)S(1)} %bitcast.31), channel_id=1, source_target_pairs={{0,32},{8,40},{32,0},{40,8},{1,33},{9,41},{33,1},{41,9},{2,34},{10... | collective-permute-start | bytes 1032200 | tf_op jit(solution)/shard_map/ppermute | solution.py:453
  34.7 19.4 %collective-permute-start.5 = (bf16[224,768]{1,0:T(8,128)(2,1)S(1)}, bf16[224,768]{1,0:T(8,128)(2,1)S(1)}, u32[]{:S(2)}, u32[]{:S(2)}) collective-permute-start(bf16[224,768]{1,0:T(8,128)(2,1)S(1)} %bitcast.32), channel_id=1, source_target_pairs={{0,40},{8,0},{32,8},{40,32},{1,41},{9,1},{33,9},{41,33},{2,42},{10... | collective-permute-start | bytes 1032200 | tf_op jit(solution)/shard_map/ppermute | solution.py:453
  52.7 0.7 copy-start.4
  53.4 0.7 copy-start.6
  54.1 0.7 copy-start.8
  59.6 1.7 copy-start
  61.3 1.0 copy-start.5
  62.3 1.0 copy-start.7
  63.2 1.0 copy-start.9
  73.7 0.7 copy-start.13
  74.4 8.3 %collective-permute-start.12 = (bf16[64,80,128]{2,1,0:T(8,128)(2,1)S(1)}, bf16[64,80,128]{2,1,0:T(8,128)(2,1)S(1)}, u32[]{:S(2)}, u32[]{:S(2)}) collective-permute-start(bf16[64,80,128]{2,1,0:T(8,128)(2,1)S(1)} %get-tuple-element.38), channel_id=1, source_target_pairs={{0,16},{16,0},{1,17},{17,1},{2,18},{18,2},{3,19},{19,3},{4,20},{20... | collective-permute-start | bytes 3932168 | tf_op jit(solution)/shard_map/ppermute | solution.py:449
  84.1 17.1 %copy-start.14 = (bf16[224,768]{1,0:T(8,128)(2,1)S(1)}, bf16[224,768]{1,0:T(8,128)(2,1)}, u32[]{:S(2)}) copy-start(bf16[224,768]{1,0:T(8,128)(2,1)} %copy-done.13) | copy-start | bytes 1032196
  84.1 55.5 %all-to-all-start = ((bf16[64,80,128]{2,1,0:T(8,128)(2,1)}), bf16[64,80,128]{2,1,0:T(8,128)(2,1)}, u32[]{:S(2)}, u32[]{:S(2)}) async-start(bf16[64,80,128]{2,1,0:T(8,128)(2,1)} %add_convert_fusion), calls=%async_computation | async-start | bytes 2621440 | tf_op jit(solution)/shard_map/all_to_all | solution.py:492
  94.4 12.1 %collective-permute-start.6 = (bf16[224,768]{1,0:T(8,128)(2,1)}, bf16[224,768]{1,0:T(8,128)(2,1)S(1)}, u32[]{:S(2)}, u32[]{:S(2)}) collective-permute-start(bf16[224,768]{1,0:T(8,128)(2,1)} %get-tuple-element.30), channel_id=1, source_target_pairs={{0,40},{8,0},{32,8},{40,32},{1,41},{9,1},{33,9},{41,33},{2,42},{10... | collective-permute-start | bytes 1032200 | tf_op jit(solution)/shard_map/ppermute | solution.py:453
  98.7 12.4 %collective-permute-start.7 = (bf16[224,768]{1,0:T(8,128)(2,1)}, bf16[224,768]{1,0:T(8,128)(2,1)S(1)}, u32[]{:S(2)}, u32[]{:S(2)}) collective-permute-start(bf16[224,768]{1,0:T(8,128)(2,1)} %get-tuple-element.31), channel_id=1, source_target_pairs={{0,32},{8,40},{32,0},{40,8},{1,33},{9,41},{33,1},{41,9},{2,34},{10... | collective-permute-start | bytes 1032200 | tf_op jit(solution)/shard_map/ppermute | solution.py:453
  101.2 18.6 %collective-permute-start.8 = (bf16[224,768]{1,0:T(8,128)(2,1)S(1)}, bf16[224,768]{1,0:T(8,128)(2,1)S(1)}, u32[]{:S(2)}, u32[]{:S(2)}) collective-permute-start(bf16[224,768]{1,0:T(8,128)(2,1)S(1)} %copy-done.14), channel_id=1, source_target_pairs={{0,8},{8,32},{32,40},{40,0},{1,9},{9,33},{33,41},{41,1},{2,10},{10... | collective-permute-start | bytes 1032200 | tf_op jit(solution)/shard_map/ppermute | solution.py:453
  119.8 0.7 copy-start.2
  120.5 1.0 copy-start.3
  125.4 3.2 %collective-permute-start.9 = (f32[2,2,48,128]{3,2,1,0:T(8,128)S(1)}, f32[2,2,48,128]{3,2,1,0:T(8,128)S(1)}, u32[]{:S(2)}, u32[]{:S(2)}) collective-permute-start(f32[2,2,48,128]{3,2,1,0:T(8,128)S(1)} %dynamic-slice_bitcast_fusion), channel_id=1, source_target_pairs={{0,16},{16,0},{1,17},{17,1},{2,18},{18,2},{3,19},{19,3},{4,20},{20... | collective-permute-start | bytes 294920 | tf_op jit(solution)/shard_map/ppermute | solution.py:464
  128.6 4.8 %collective-permute-start.10 = (f32[2,48,128]{2,1,0:T(8,128)S(1)}, f32[2,48,128]{2,1,0:T(8,128)S(1)}, u32[]{:S(2)}, u32[]{:S(2)}) collective-permute-start(f32[2,48,128]{2,1,0:T(8,128)S(1)} %dynamic-slice_bitcast_fusion.1), channel_id=1, source_target_pairs={{0,8},{8,0},{1,9},{9,1},{2,10},{10,2},{3,11},{11,3},{4,12},{12,4},... | collective-permute-start | bytes 147464 | tf_op jit(solution)/shard_map/ppermute | solution.py:464
  133.5 6.1 %collective-permute-start.11 = (f32[48,128]{1,0:T(8,128)S(1)}, f32[48,128]{1,0:T(8,128)S(1)}, u32[]{:S(2)}, u32[]{:S(2)}) collective-permute-start(f32[48,128]{1,0:T(8,128)S(1)} %dynamic-slice_bitcast_fusion.2), channel_id=1, source_target_pairs={{0,32},{32,0},{1,33},{33,1},{2,34},{34,2},{3,35},{35,3},{4,36},{36... | collective-permute-start | bytes 73736 | tf_op jit(solution)/shard_map/ppermute | solution.py:464
  172.7 14.7 %collective-permute-start.14 = (bf16[8,80,128]{2,1,0:T(8,128)(2,1)S(1)}, bf16[8,80,128]{2,1,0:T(8,128)(2,1)S(1)}, u32[]{:S(2)}, u32[]{:S(2)}) collective-permute-start(bf16[8,80,128]{2,1,0:T(8,128)(2,1)S(1)} %slice.14.mine_ref), channel_id=1, source_target_pairs={{0,32},{32,0},{1,33},{33,1},{2,34},{34,2},{3,35},{35,3},{4,36},{36... | collective-permute-start | bytes 491528 | tf_op jit(solution)/shard_map/ppermute | solution.py:510
  175.9 16.6 %all-to-all-start.3 = ((f32[8,48,128]{2,1,0:T(8,128)}), f32[8,48,128]{2,1,0:T(8,128)S(1)}, u32[]{:S(2)}, u32[]{:S(2)}) async-start(f32[8,48,128]{2,1,0:T(8,128)} %broadcast_in_dim.16), calls=%async_computation.3 | async-start | bytes 393216 | tf_op jit(solution)/shard_map/all_to_all | solution.py:445
  185.5 7.1 %collective-permute-start.13 = (bf16[8,80,128]{2,1,0:T(8,128)(2,1)S(1)}, bf16[8,80,128]{2,1,0:T(8,128)(2,1)S(1)}, u32[]{:S(2)}, u32[]{:S(2)}) collective-permute-start(bf16[8,80,128]{2,1,0:T(8,128)(2,1)S(1)} %slice.14.mine_ref), channel_id=1, source_target_pairs={{0,16},{16,0},{1,17},{17,1},{2,18},{18,2},{3,19},{19,3},{4,20},{20... | collective-permute-start | bytes 491528 | tf_op jit(solution)/shard_map/ppermute | solution.py:449
  187.4 5.1 %collective-permute-start.15 = (bf16[8,80,128]{2,1,0:T(8,128)(2,1)S(1)}, bf16[8,80,128]{2,1,0:T(8,128)(2,1)S(1)}, u32[]{:S(2)}, u32[]{:S(2)}) collective-permute-start(bf16[8,80,128]{2,1,0:T(8,128)(2,1)S(1)} %collective-permute-done.14.across_ref), channel_id=1, source_target_pairs={{0,16},{16,0},{1,17},{17,1},{2,18},{18,2},{3,19},{19,3},{4,20},{20... | collective-permute-start | bytes 491528 | tf_op jit(solution)/shard_map/ppermute | solution.py:449
Sparse Core Ops, SparseCore 0:
  11.6 47.8 all-gather.1

commit v4 on v3

--- a/solution.py
+++ b/solution.py
@@ -25,6 +25,7 @@
 RING = ("xh", "xl")
 TEAM = ("core", "xl", "xh")
 INTERPRET = False
+HIDDEN_MIB = 52
 
 
 def params(limit_mib, **more):
@@ -51,7 +52,13 @@
     return pl.BlockSpec(shape, lambda i: (0,) * len(shape))
 
 
-def pack_kernel(place_ref, first_ref, bias_ref, second_ref, out_ref):
+def pack_kernel(place_ref, first_in, bias_in, second_in, out_ref, first_ref, bias_ref, second_ref, sems):
+    pairs = ((first_in, first_ref), (second_in, second_ref), (bias_in, bias_ref))
+    copies = [pltpu.make_async_copy(source, target, sems.at[i]) for i, (source, target) in enumerate(pairs)]
+    for copy in copies:
+        copy.start()
+    for copy in copies:
+        copy.wait()
     q = place_ref[0]
     column = place_ref[1]
     partner = q + 1 - 2 * lax.rem(q, 2)
@@ -78,9 +85,15 @@
         pack_kernel,
         grid=(1,),
         out_shape=jax.ShapeDtypeStruct((PACK, CH), BF16),
-        in_specs=[scalars(), block(192, CH), block(1, 192), block(192, CH)],
+        in_specs=[scalars()] + [pl.BlockSpec(memory_space=pl.ANY)] * 3,
         out_specs=block(PACK, CH),
-        compiler_params=params(8),
+        scratch_shapes=[
+            pltpu.VMEM((192, CH), BF16),
+            pltpu.VMEM((1, 192), F32),
+            pltpu.VMEM((192, CH), BF16),
+            pltpu.SemaphoreType.DMA((3,)),
+        ],
+        compiler_params=params(58),
         interpret=INTERPRET,
         name="pack",
     )(place, first_weight.T, first_bias.reshape(1, 192), second_weight)
@@ -159,7 +172,7 @@
             pltpu.VMEM((20, 24, LANES), F32),
             pltpu.VMEM((BLOCKS, ROWS, WIDE, LANES), F32),
         ],
-        compiler_params=params(24),
+        compiler_params=params(8),
         interpret=INTERPRET,
         name="conv_norm",
     )(image, kernel, gain)
@@ -214,7 +227,7 @@
         rows = rows.astype(BF16)
         for z in range(8):
             for s in range(36, 40):
-                outs[half][(s // 5) * 8 + z, (s % 5) * 16 : (s % 5) * 16 + 16, :] = rows if s == 36 else empty
+                outs[half][z, s * 16 : s * 16 + 16, :] = rows if s == 36 else empty
 
 
 def spread(outs, matrix, start):
@@ -224,7 +237,7 @@
                 for part in range(3):
                     s = start + j * 3 + part
                     row = z * UNITS + half * OWN + part * 16
-                    outs[half][(s // 5) * 8 + z, (s % 5) * 16 : (s % 5) * 16 + 16, :] = matrix[
+                    outs[half][z, s * 16 : s * 16 + 16, :] = matrix[
                         row : row + 16, j * LANES : (j + 1) * LANES
                     ]
 
@@ -234,10 +247,10 @@
         hidden_kernel,
         grid=(1,),
         out_shape=(jax.ShapeDtypeStruct((PIX, CH), BF16),) * 4
-        + (jax.ShapeDtypeStruct((64, 80, LANES), BF16),) * 2
+        + (jax.ShapeDtypeStruct((8, 640, LANES), BF16),) * 2
         + (jax.ShapeDtypeStruct((8, CH), F32),),
         in_specs=[pl.BlockSpec(memory_space=pl.ANY)] * 9 + [block(1, CH)],
-        out_specs=(block(PIX, CH),) * 4 + (block(64, 80, LANES),) * 2 + (block(8, CH),),
+        out_specs=(block(PIX, CH),) * 4 + (block(8, 640, LANES),) * 2 + (block(8, CH),),
         scratch_shapes=[
             pltpu.VMEM((4 * PIX, CH), BF16),
             pltpu.VMEM((4 * PIX, CH), BF16),
@@ -246,7 +259,7 @@
             pltpu.VMEM((4 * PIX, CH), BF16),
             pltpu.SemaphoreType.DMA((9,)),
         ],
-        compiler_params=params(40),
+        compiler_params=params(HIDDEN_MIB),
         interpret=INTERPRET,
         name="hidden",
     )(*normed, *scaled, pack, layer)
@@ -338,7 +351,7 @@
             pltpu.VMEM((49, 8, LANES), F32),
             pltpu.VMEM((BLOCKS, 8, LANES), F32),
         ],
-        compiler_params=params(32),
+        compiler_params=params(12),
         interpret=INTERPRET,
         name="norm_back",
     )(weight, zero, one, two, three, centred, inv, gain, scale, image)
@@ -369,7 +382,7 @@
         ],
         out_specs=pl.BlockSpec((1, ROWS, COLS, LANES), lambda j: (0, 0, 0, j)),
         scratch_shapes=[pltpu.VMEM((20, 24, LANES), F32)],
-        compiler_params=params(24),
+        compiler_params=params(6),
         interpret=INTERPRET,
         name="input_grad",
     )(conv, kernel, scaled)
@@ -398,8 +411,8 @@
         image_ref[0, :, :, lanes] = (pre_ref[0, :, :, lanes] * factor.reshape(1, 1, LANES)).astype(BF16)
         for a in range(7):
             kernel_ref[a, :, lanes] = small_ref[j, a * 7 : a * 7 + 7, :] * factor
-        gain_ref[:, lanes] = small_ref[j, 49:50, :] * factor
-        scale_ref[:, lanes] = small_ref[j, 50:51, :] * factor
+        gain_ref[lanes] = small_ref[j, 49, :] * factor[0]
+        scale_ref[lanes] = small_ref[j, 50, :] * factor[0]
         for q in range(4):
             for part in range(3):
                 rows = slice(q * OWN + part * 16, q * OWN + part * 16 + 16)
@@ -419,8 +432,8 @@
             jax.ShapeDtypeStruct((192, CH), F32),
             jax.ShapeDtypeStruct((1, 192), F32),
             jax.ShapeDtypeStruct((7, 7, CH), F32),
-            jax.ShapeDtypeStruct((1, CH), F32),
-            jax.ShapeDtypeStruct((1, CH), F32),
+            jax.ShapeDtypeStruct((CH,), F32),
+            jax.ShapeDtypeStruct((CH,), F32),
         ),
         in_specs=[scalars(), block(BLOCKS, 64, LANES), block(1, ROWS, COLS, CH)]
         + [block(8, 80, LANES)] * 4,
@@ -430,11 +443,11 @@
             block(192, CH),
             block(1, 192),
             block(7, 7, CH),
-            block(1, CH),
-            block(1, CH),
+            block(CH),
+            block(CH),
         ),
         scratch_shapes=[pltpu.VMEM((4, 8, 80, LANES), BF16)],
-        compiler_params=params(24),
+        compiler_params=params(12),
         interpret=INTERPRET,
         name="finish",
     )(place, small, pre, mine, mine_core, across, across_core)
@@ -455,13 +468,6 @@
 
 def ring_share(value):
     return [value] + [ring(value, r) for r in range(1, 4)]
-
-
-def halve(value, axis):
-    at = lax.axis_index(axis)
-    keep = lax.dynamic_index_in_dim(value, at, 0, keepdims=False)
-    send = lax.dynamic_index_in_dim(value, 1 - at, 0, keepdims=False)
-    return keep + lax.ppermute(send, axis, [(0, 1), (1, 0)])
 
 
 def per_device(
@@ -487,26 +493,22 @@
     scaled_all = ring_share(scaled)
 
     *parts, grads, other, scale = hidden(normed_all, scaled_all, packed, layer)
-    got = swap_core(other)
-    grads = (grads.astype(F32) + got.astype(F32)).astype(BF16)
-    grads = lax.all_to_all(grads, ("y", "z"), 0, 0, tiled=True)
-    grads = jnp.sum(grads.astype(F32), axis=0)
+    grads = (grads.astype(F32) + swap_core(other).astype(F32)).astype(BF16)
+    grads = lax.psum_scatter(grads, "z", scatter_dimension=0, tiled=True).reshape(8, 80, LANES)
 
     returned = [ring(parts[r], 4 - r) for r in range(1, 4)]
     small, conv_grad = backward(own_weight.reshape(1), parts[0], *returned, centred, inv, gain, scale, image[0])
-    small = small.reshape(2, 2, 2, OWN, LANES)
-    small = halve(small, "core")
-    small = halve(small, "xl")
-    small = halve(small, "xh")
-    small, grads = lax.optimization_barrier((small, grads))
-    small = jnp.sum(to_all(small, "z"), axis=0)
+    small = lax.all_to_all(small.reshape(8, OWN, LANES), TEAM, 0, 0, tiled=True)
+    small = jnp.sum(to_all(jnp.sum(small, axis=0), "z"), axis=0)
     high = small.astype(BF16)
     low = (small - high.astype(F32)).astype(BF16)
-    both = to_all(jnp.concatenate([grads.astype(BF16), high, low], axis=0), "y")
-    small = jnp.sum(both[:, 80:128, :].astype(F32) + both[:, 128:176, :].astype(F32), axis=0)
+    both = jnp.broadcast_to(jnp.concatenate([high, low], axis=0), (8, 2 * OWN, LANES))
+    both = lax.all_to_all(jnp.concatenate([grads, both], axis=1), "y", 0, 0, tiled=True).astype(F32)
+    mine = to_all(jnp.sum(both[:, 0:80, :], axis=0).astype(BF16), "y")
+    small = jnp.sum(both[:, 80:128, :] + both[:, 128:176, :], axis=0)
+    small, mine = lax.optimization_barrier((small, mine))
     small = to_all(small, TEAM).reshape(BLOCKS, 64, LANES)
 
-    mine = both[:, 0:80, :]
     across = lax.ppermute(mine, "xh", [(0, 1), (1, 0)])
     pre = input_grad(conv_grad, kernel, scaled)
     images = float(lax.axis_size(REPLICA) * lax.axis_size(SHARD))
@@ -521,8 +523,8 @@
         grad_bias.reshape(4 * OWN),
         grad_second,
         grad_kernel,
-        grad_gain.reshape(CH),
-        grad_scale.reshape(CH),
+        grad_gain,
+        grad_scale,
     )
 
 

time: 204 us -> 194 us (0.951)
  starting transfers between devices: 68.1 us -> 55 us
  local copies, waits for them, and re-layouts: 13.7 us -> 2.28 us
  blocking collectives: 31.5 us -> 39.5 us
  waiting for transfers between devices: 45.3 us -> 49.3 us
  Pallas kernels: 22.1 us -> 25.2 us
    all_to_all x0 -> x2, blocking collectives: none -> 26.3 us  [the longest x1 17.5 us: per_device(): lax.all_to_all(jnp.concatenate([grads, both], axis=1), 'y', 0, 0, tiled=T...]
    all_to_all x2 -> x1, blocking collectives: 31.5 us -> 13.2 us  [to_all(): lax.all_to_all(jnp.broadcast_to(value, (count, *value.shape)), axes, 0, 0...]
    unnamed x36 -> x24, local copies, waits for them, and re-layouts: 11.9 us -> 0.78 us
    all_to_all x1 -> x0, starting transfers between devices: 10.3 us -> none  [per_device(): grads = lax.all_to_all(grads, ('y', 'z'), 0, 0, tiled=True)]
    all_to_all x1 -> x2, waiting for transfers between devices: 0.01 us -> 8.26 us  [to_all(): lax.all_to_all(jnp.broadcast_to(value, (count, *value.shape)), axes, 0, 0...]
    ppermute x3 -> x0, waiting for transfers between devices: 7.41 us -> none  [halve(): return keep + lax.ppermute(send, axis, [(0, 1), (1, 0)])]
    ppermute x3 -> x0, starting transfers between devices: 6.69 us -> none  [halve(): return keep + lax.ppermute(send, axis, [(0, 1), (1, 0)])]
    ppermute x1, starting transfers between devices: 2.48 us -> 6.33 us  [per_device(): across = lax.ppermute(mine, 'xh', [(0, 1), (1, 0)])]
  transfers between devices with their start and end apart: 19 -> 17, of which waited for: 9 -> 10; matrix products, arithmetic and copies ran while one was open for 2% -> 2% of each run, Pallas kernels for 5% -> 5%
where the time goes in v4:
time: 194 us; the launch traced here: 193 us
  starting transfers between devices  55 us (28%)
  waiting for transfers between devices  49.3 us (25%)
  blocking collectives  39.5 us (20%)
  Pallas kernels  25.2 us (13%)
  between operations  15.1 us (8%)
  other arithmetic  6.46 us (3%)
  local copies, waits for them, and re-layouts  2.28 us (1%)
    ppermute x9, waiting for transfers between devices, ring(): return lax.ppermute(value, RING, [(i, (i + shift) % 4) for i in range(4)])  32.4 us
    ppermute x9, starting transfers between devices, ring(): return lax.ppermute(value, RING, [(i, (i + shift) % 4) for i in range(4)])  28.5 us
    all_to_all x1, blocking collectives, per_device(): lax.all_to_all(jnp.concatenate([grads, both], axis=1), 'y', 0, 0, tiled=T...  17.5 us
    all_to_all x1, blocking collectives, to_all(): lax.all_to_all(jnp.broadcast_to(value, (count, *value.shape)), axes, 0, 0...  13.2 us
    pallas_call x1, Pallas kernels, hidden(): pl.pallas_call(hidden_kernel, grid=(1,), out_shape=(jax.ShapeDtypeStruct(...  11.2 us
    all_to_all x2, starting transfers between devices, to_all(): lax.all_to_all(jnp.broadcast_to(value, (count, *value.shape)), axes, 0, 0...  10.1 us
    ppermute x3, starting transfers between devices, swap_core(): return lax.ppermute(value, 'core', [(0, 1), (1, 0)])  9.95 us
    all_to_all x1, blocking collectives, per_device(): small = lax.all_to_all(small.reshape(8, OWN, LANES), TEAM, 0, 0, tiled=True)  8.77 us
  transfers between devices with their start and end apart: 17, of which 10 were waited for; matrix products, arithmetic and copies ran while one was open for 2% of the time, Pallas kernels for 5%

profile of v4, /device:TPU:1, one launch (start us, length us, event | category | flops | bytes accessed | tf_op | source)
XLA Modules:
  0.0 192.9 jit_solution(16091050712212417699)
XLA Ops:
  7.2 0.0 copy-start.3
  7.2 0.0 all-gather.2.cloned.1.call-start
  7.2 0.6 pad_add_fusion.1.place_ref
  7.8 2.9 %pack.1 = bf16[208,768]{1,0:T(8,128)(2,1)} custom-call(s32[2]{0:T(128)} %pad_add_fusion.1.place_ref, bf16[192,768]{1,0:T(8,128)(2,1)} %bitcast.29, f32[1,192]{1,0:T(1,128)} %bitcast.31, bf16[192,768]{1,0:T(8,128)(2,1)} %second_in.1), custom_call_target="tpu_custom_call" | custom-call | tf_op jit(solution)/shard_map/pack/pallas_call | solution.py:84
  10.7 0.0 copy-start.11
  10.7 0.0 all-gather.2.cloned.1.call-update
  10.8 0.0 reduce-scatter.2.cloned.1.call-start
  11.4 1.3 fusion.2
  12.7 0.0 copy-done.3
  12.7 0.7 fusion
  13.5 0.0 copy-start
  13.5 5.2 %collective-permute-start.5 = (bf16[224,768]{1,0:T(8,128)(2,1)S(1)}, bf16[224,768]{1,0:T(8,128)(2,1)S(1)}, u32[]{:S(2)}, u32[]{:S(2)}) collective-permute-start(bf16[224,768]{1,0:T(8,128)(2,1)S(1)} %bitcast.19), channel_id=1, source_target_pairs={{0,40},{8,0},{32,8},{40,32},{1,41},{9,1},{33,9},{41,33},{2,42},{10... | collective-permute-start | bytes 1032200 | tf_op jit(solution)/shard_map/ppermute | solution.py:466
  18.7 2.4 %collective-permute-start.4 = (bf16[224,768]{1,0:T(8,128)(2,1)S(1)}, bf16[224,768]{1,0:T(8,128)(2,1)S(1)}, u32[]{:S(2)}, u32[]{:S(2)}) collective-permute-start(bf16[224,768]{1,0:T(8,128)(2,1)S(1)} %bitcast.20), channel_id=1, source_target_pairs={{0,32},{8,40},{32,0},{40,8},{1,33},{9,41},{33,1},{41,9},{2,34},{10... | collective-permute-start | bytes 1032200 | tf_op jit(solution)/shard_map/ppermute | solution.py:466
  21.2 2.5 %collective-permute-start.3 = (bf16[224,768]{1,0:T(8,128)(2,1)S(1)}, bf16[224,768]{1,0:T(8,128)(2,1)S(1)}, u32[]{:S(2)}, u32[]{:S(2)}) collective-permute-start(bf16[224,768]{1,0:T(8,128)(2,1)S(1)} %bitcast.21), channel_id=1, source_target_pairs={{0,8},{8,32},{32,40},{40,0},{1,9},{9,33},{33,41},{41,1},{2,10},{10... | collective-permute-start | bytes 1032200 | tf_op jit(solution)/shard_map/ppermute | solution.py:466
  23.7 0.0 copy-done.10
  23.7 0.0 copy-done.9
  23.8 0.0 copy-done.2
  23.8 2.8 %conv_norm.1 = (bf16[224,768]{1,0:T(8,128)(2,1)S(1)}, f32[6,14,16,128]{3,2,1,0:T(8,128)S(1)}, f32[14,16,128]{2,1,0:T(8,128)S(1)}) custom-call(bf16[14,14,768]{2,1,0:T(8,128)(2,1)S(1)} %bitcast.24, bf16[49,768]{1,0:T(8,128)(2,1)S(1)} %reshape.51.kernel_ref, f32[1,768]{1,0:T(1,128)S(1)} %reshape.52.gain_ref), custom_call_target="tpu_custom_call" | custom-call | tf_op jit(solution)/shard_map/conv_norm/pallas_call | solution.py:153
  26.6 4.0 %collective-permute-start.2 = (bf16[224,768]{1,0:T(8,128)(2,1)S(1)}, bf16[224,768]{1,0:T(8,128)(2,1)S(1)}, u32[]{:S(2)}, u32[]{:S(2)}) collective-permute-start(bf16[224,768]{1,0:T(8,128)(2,1)S(1)} %get-tuple-element.28.refs_0_), channel_id=1, source_target_pairs={{0,40},{8,0},{32,8},{40,32},{1,41},{9,1},{33,9},{41,33},{2,42},{10... | collective-permute-start | bytes 1032200 | tf_op jit(solution)/shard_map/ppermute | solution.py:466
  30.6 3.1 %collective-permute-start.1 = (bf16[224,768]{1,0:T(8,128)(2,1)S(1)}, bf16[224,768]{1,0:T(8,128)(2,1)S(1)}, u32[]{:S(2)}, u32[]{:S(2)}) collective-permute-start(bf16[224,768]{1,0:T(8,128)(2,1)S(1)} %get-tuple-element.28.refs_0_), channel_id=1, source_target_pairs={{0,32},{8,40},{32,0},{40,8},{1,33},{9,41},{33,1},{41,9},{2,34},{10... | collective-permute-start | bytes 1032200 | tf_op jit(solution)/shard_map/ppermute | solution.py:466
  33.7 0.0 collective-permute-done.5.refs_7_
  33.8 0.0 copy-start.4
  33.8 1.9 collective-permute-start
  35.7 0.0 copy-done.11
  35.7 0.0 collective-permute-done.4.refs_6_
  35.7 0.0 copy-start.5
  35.7 2.8 %collective-permute-done.3.refs_5_ = bf16[224,768]{1,0:T(8,128)(2,1)S(1)} collective-permute-done((bf16[224,768]{1,0:T(8,128)(2,1)S(1)}, bf16[224,768]{1,0:T(8,128)(2,1)S(1)}, u32[]{:S(2)}, u32[]{:S(2)}) %collective-permute-start.3) | collective-permute-done | bytes 344096 | tf_op jit(solution)/shard_map/ppermute | solution.py:466
  38.5 1.0 collective-permute-done.2.refs_3_
  39.6 4.6 %collective-permute-done.1.refs_2_ = bf16[224,768]{1,0:T(8,128)(2,1)S(1)} collective-permute-done((bf16[224,768]{1,0:T(8,128)(2,1)S(1)}, bf16[224,768]{1,0:T(8,128)(2,1)S(1)}, u32[]{:S(2)}, u32[]{:S(2)}) %collective-permute-start.1) | collective-permute-done | bytes 344096 | tf_op jit(solution)/shard_map/ppermute | solution.py:466
  44.1 0.7 copy-done.8
  44.9 8.2 %collective-permute-done.refs_1_ = bf16[224,768]{1,0:T(8,128)(2,1)} collective-permute-done((bf16[224,768]{1,0:T(8,128)(2,1)S(1)}, bf16[224,768]{1,0:T(8,128)(2,1)}, u32[]{:S(2)}, u32[]{:S(2)}) %collective-permute-start) | collective-permute-done | bytes 344096 | tf_op jit(solution)/shard_map/ppermute | solution.py:466
  53.1 5.7 %all-gather.2.cloned.1.call-done = bf16[1664,768]{1,0:T(8,128)(2,1)} async-done(((bf16[208,768]{1,0:T(8,128)(2,1)}), bf16[1664,768]{1,0:T(8,128)(2,1)}) %all-gather.2.cloned.1.call-update) | async-done | bytes 2555920 | tf_op jit(solution)/shard_map/all_gather | solution.py:481
  58.8 11.2 %hidden.1 = (bf16[224,768]{1,0:T(8,128)(2,1)S(1)}, bf16[224,768]{1,0:T(8,128)(2,1)S(1)}, bf16[224,768]{1,0:T(8,128)(2,1)S(1)}, bf16[224,768]{1,0:T(8,128)(2,1)S(...) custom-call(bf16[224,768]{1,0:T(8,128)(2,1)S(1)} %get-tuple-element.28.refs_0_, ...), custom_call_target="tpu_custom_call" | custom-call | tf_op jit(solution)/shard_map/hidden/pallas_call | solution.py:246
  70.1 5.6 %collective-permute-start.6 = (bf16[8,640,128]{2,1,0:T(8,128)(2,1)}, bf16[8,640,128]{2,1,0:T(8,128)(2,1)S(1)}, u32[]{:S(2)}, u32[]{:S(2)}) collective-permute-start(bf16[8,640,128]{2,1,0:T(8,128)(2,1)} %get-tuple-element.30), channel_id=1, source_target_pairs={{0,16},{16,0},{1,17},{17,1},{2,18},{18,2},{3,19},{19,3},{4,20},{20... | collective-permute-start | bytes 3932168 | tf_op jit(solution)/shard_map/ppermute | solution.py:462
  75.7 2.9 %collective-permute-done.6 = bf16[8,640,128]{2,1,0:T(8,128)(2,1)S(1)} collective-permute-done((bf16[8,640,128]{2,1,0:T(8,128)(2,1)}, bf16[8,640,128]{2,1,0:T(8,128)(2,1)S(1)}, u32[]{:S(2)}, u32[]{:S(2)}) %collective-permute-start.6) | collective-permute-done | bytes 1310752 | tf_op jit(solution)/shard_map/ppermute | solution.py:462
  78.6 2.7 %add_convert_fusion = bf16[8,640,128]{2,1,0:T(8,128)(2,1)} fusion(bf16[8,640,128]{2,1,0:T(8,128)(2,1)S(1)} %collective-permute-done.6, bf16[8,640,128]{2,1,0:T(8,128)(2,1)} %get-tuple-element.29), kind=kLoop, calls=%fused_computation | loop fusion | flops 2621440 | bytes 3932160 | tf_op jit(solution)/shard_map/convert_element_type | solution.py:496
  81.3 0.0 reduce-scatter.2.cloned.1.call-update
  81.3 4.3 %collective-permute-start.7 = (bf16[224,768]{1,0:T(8,128)(2,1)S(1)}, bf16[224,768]{1,0:T(8,128)(2,1)S(1)}, u32[]{:S(2)}, u32[]{:S(2)}) collective-permute-start(bf16[224,768]{1,0:T(8,128)(2,1)S(1)} %get-tuple-element.32), channel_id=1, source_target_pairs={{0,40},{8,0},{32,8},{40,32},{1,41},{9,1},{33,9},{41,33},{2,42},{10... | collective-permute-start | bytes 1032200 | tf_op jit(solution)/shard_map/ppermute | solution.py:466
  85.7 2.5 %collective-permute-start.8 = (bf16[224,768]{1,0:T(8,128)(2,1)S(1)}, bf16[224,768]{1,0:T(8,128)(2,1)S(1)}, u32[]{:S(2)}, u32[]{:S(2)}) collective-permute-start(bf16[224,768]{1,0:T(8,128)(2,1)S(1)} %get-tuple-element.33), channel_id=1, source_target_pairs={{0,32},{8,40},{32,0},{40,8},{1,33},{9,41},{33,1},{41,9},{2,34},{10... | collective-permute-start | bytes 1032200 | tf_op jit(solution)/shard_map/ppermute | solution.py:466
  88.1 2.5 %collective-permute-start.9 = (bf16[224,768]{1,0:T(8,128)(2,1)S(1)}, bf16[224,768]{1,0:T(8,128)(2,1)S(1)}, u32[]{:S(2)}, u32[]{:S(2)}) collective-permute-start(bf16[224,768]{1,0:T(8,128)(2,1)S(1)} %get-tuple-element.34), channel_id=1, source_target_pairs={{0,8},{8,32},{32,40},{40,0},{1,9},{9,33},{33,41},{41,1},{2,10},{10... | collective-permute-start | bytes 1032200 | tf_op jit(solution)/shard_map/ppermute | solution.py:466
  90.7 2.7 %collective-permute-done.7.one_ref = bf16[224,768]{1,0:T(8,128)(2,1)S(1)} collective-permute-done((bf16[224,768]{1,0:T(8,128)(2,1)S(1)}, bf16[224,768]{1,0:T(8,128)(2,1)S(1)}, u32[]{:S(2)}, u32[]{:S(2)}) %collective-permute-start.7) | collective-permute-done | bytes 344096 | tf_op jit(solution)/shard_map/ppermute | solution.py:466
  93.4 4.7 %collective-permute-done.8.two_ref = bf16[224,768]{1,0:T(8,128)(2,1)S(1)} collective-permute-done((bf16[224,768]{1,0:T(8,128)(2,1)S(1)}, bf16[224,768]{1,0:T(8,128)(2,1)S(1)}, u32[]{:S(2)}, u32[]{:S(2)}) %collective-permute-start.8) | collective-permute-done | bytes 344096 | tf_op jit(solution)/shard_map/ppermute | solution.py:466
  98.1 8.4 %collective-permute-done.9.three_ref = bf16[224,768]{1,0:T(8,128)(2,1)S(1)} collective-permute-done((bf16[224,768]{1,0:T(8,128)(2,1)S(1)}, bf16[224,768]{1,0:T(8,128)(2,1)S(1)}, u32[]{:S(2)}, u32[]{:S(2)}) %collective-permute-start.9) | collective-permute-done | bytes 344096 | tf_op jit(solution)/shard_map/ppermute | solution.py:466
  106.4 3.8 %norm_back.1 = (f32[6,64,128]{2,1,0:T(8,128)S(1)}, f32[6,14,16,128]{3,2,1,0:T(8,128)S(1)}) custom-call(f32[1]{0:T(128)} %bitcast.12.weight_ref, bf16[224,768]{1,0:T(8,128)(2,1)S(1)} %get-tuple-element.31.zero_ref, bf16[224,768]{1,0:T(8,128)(2,1)S(1)} %collective-permute-done.7.one_ref, bf16[224,768]{1,0:T(8,128)(2,1)S(1)} %collective-permute-done.8.two_ref, ...), custom_call_target="tpu_custom_call" | custom-call | tf_op jit(solution)/shard_map/norm_back/pallas_call | solution.py:325
  110.3 8.8 %all_to_all.25 = f32[8,48,128]{2,1,0:T(8,128)S(1)} all-to-all(f32[8,48,128]{2,1,0:T(8,128)S(1)} %bitcast.27), channel_id=1, replica_groups=mesh['y'=8,'xh'=2,'core'=2,'xl'=2,'z'=8] {'core','xl','xh'}, dimensions={0} | all-to-all | bytes 393216 | tf_op jit(solution)/shard_map/all_to_all | solution.py:501
  119.1 13.2 %all_to_all.26 = f32[8,48,128]{2,1,0:T(8,128)S(1)} all-to-all(f32[8,48,128]{2,1,0:T(8,128)S(1)} %broadcast_in_dim.17), channel_id=1, replica_groups=mesh['y'=8,'xh'=2,'core'=2,'xl'=2,'z'=8] {'z'}, dimensions={0} | all-to-all | bytes 393216 | tf_op jit(solution)/shard_map/all_to_all | solution.py:458
  132.3 0.0 reduce-scatter.2.cloned.1.call-done
  132.4 0.9 pad_maximum_fusion
  133.4 17.5 %all_to_all.27 = bf16[8,176,128]{2,1,0:T(8,128)(2,1)S(1)} all-to-all(bf16[8,176,128]{2,1,0:T(8,128)(2,1)S(1)} %pad_maximum_fusion), channel_id=1, replica_groups=mesh['y'=8,'xh'=2,'core'=2,'xl'=2,'z'=8] {'y'}, dimensions={0} | all-to-all | bytes 720896 | tf_op jit(solution)/shard_map/all_to_all | solution.py:506
  151.0 0.7 broadcast_in_dim.19
  151.6 3.4 %all-to-all-start.3 = ((bf16[8,80,128]{2,1,0:T(8,128)(2,1)}), bf16[8,80,128]{2,1,0:T(8,128)(2,1)S(1)}, u32[]{:S(2)}, u32[]{:S(2)}) async-start(bf16[8,80,128]{2,1,0:T(8,128)(2,1)} %broadcast_in_dim.19), calls=%async_computation.4 | async-start | bytes 327680 | tf_op jit(solution)/shard_map/all_to_all | solution.py:458
  155.1 8.3 %all-to-all-done.3.mine_ref = bf16[8,80,128]{2,1,0:T(8,128)(2,1)S(1)} async-done(((bf16[8,80,128]{2,1,0:T(8,128)(2,1)}), bf16[8,80,128]{2,1,0:T(8,128)(2,1)S(1)}, u32[]{:S(2)}, u32[]{:S(2)}) %all-to-all-start.3) | async-done | bytes 163872 | tf_op jit(solution)/shard_map/all_to_all | solution.py:458
  163.3 6.3 %collective-permute-start.11 = (bf16[8,80,128]{2,1,0:T(8,128)(2,1)S(1)}, bf16[8,80,128]{2,1,0:T(8,128)(2,1)S(1)}, u32[]{:S(2)}, u32[]{:S(2)}) collective-permute-start(bf16[8,80,128]{2,1,0:T(8,128)(2,1)S(1)} %all-to-all-done.3.mine_ref), channel_id=1, source_target_pairs={{0,32},{32,0},{1,33},{33,1},{2,34},{34,2},{3,35},{35,3},{4,36},{36... | collective-permute-start | bytes 491528 | tf_op jit(solution)/shard_map/ppermute | solution.py:512
  169.7 0.7 broadcast_in_dim.20
  170.3 6.8 %all-to-all-start.4 = ((f32[8,48,128]{2,1,0:T(8,128)}), f32[8,48,128]{2,1,0:T(8,128)S(1)}, u32[]{:S(2)}, u32[]{:S(2)}) async-start(f32[8,48,128]{2,1,0:T(8,128)} %broadcast_in_dim.20), calls=%async_computation.5 | async-start | bytes 393216 | tf_op jit(solution)/shard_map/all_to_all | solution.py:458
  177.1 2.0 %collective-permute-start.10 = (bf16[8,80,128]{2,1,0:T(8,128)(2,1)S(1)}, bf16[8,80,128]{2,1,0:T(8,128)(2,1)S(1)}, u32[]{:S(2)}, u32[]{:S(2)}) collective-permute-start(bf16[8,80,128]{2,1,0:T(8,128)(2,1)S(1)} %all-to-all-done.3.mine_ref), channel_id=1, source_target_pairs={{0,16},{16,0},{1,17},{17,1},{2,18},{18,2},{3,19},{19,3},{4,20},{20... | collective-permute-start | bytes 491528 | tf_op jit(solution)/shard_map/ppermute | solution.py:462
  179.1 0.0 collective-permute-done.11.across_ref
  179.1 2.3 %collective-permute-start.12 = (bf16[8,80,128]{2,1,0:T(8,128)(2,1)S(1)}, bf16[8,80,128]{2,1,0:T(8,128)(2,1)S(1)}, u32[]{:S(2)}, u32[]{:S(2)}) collective-permute-start(bf16[8,80,128]{2,1,0:T(8,128)(2,1)S(1)} %collective-permute-done.11.across_ref), channel_id=1, source_target_pairs={{0,16},{16,0},{1,17},{17,1},{2,18},{18,2},{3,19},{19,3},{4,20},{20... | collective-permute-start | bytes 491528 | tf_op jit(solution)/shard_map/ppermute | solution.py:462
  181.5 0.1 pad_add_fusion.place_ref
  181.5 2.6 %input_grad.1.pre_ref = f32[1,14,14,768]{3,2,1,0:T(8,128)S(1)} custom-call(f32[6,14,16,128]{3,2,1,0:T(8,128)S(1)} %get-tuple-element.40.conv_ref, bf16[49,768]{1,0:T(8,128)(2,1)S(1)} %reshape.51.kernel_ref, bf16[224,768]{1,0:T(8,128)(2,1)S(1)} %bitcast.23), custom_call_target="tpu_custom_call" | custom-call | tf_op jit(solution)/shard_map/input_grad/pallas_call | solution.py:374
  184.2 0.0 collective-permute-done.10.mine_core_ref
  184.2 0.0 all-to-all-done.4
  184.2 0.0 collective-permute-done.12.across_core_ref
  184.2 1.8 finish.1
  (26 shorter events, 0.3 us)
Async XLA Ops:
  7.2 5.6 %copy-start.3 = (bf16[1,14,14,768]{3,2,1,0:T(8,128)(2,1)S(1)}, bf16[1,14,14,768]{3,2,1,0:T(8,128)(2,1)}, u32[]{:S(2)}) copy-start(bf16[1,14,14,768]{3,2,1,0:T(8,128)(2,1)} %param.11) | copy-start | bytes 903172
  7.2 51.6 %all-gather.2.cloned.1.call-start = ((), (), s32[]{:S(2)}) async-start(), calls=%async_computation.6 | async-start | bytes 2875392 | tf_op jit(solution)/shard_map/all_gather | solution.py:481
  7.8 15.9 %copy-start.10 = (f32[768]{0:T(1024)S(1)}, f32[768]{0:T(1024)}, u32[]{:S(2)}) copy-start(f32[768]{0:T(1024)} %param.15) | copy-start | bytes 9220
  7.8 15.9 %copy-start.9 = (bf16[7,7,768]{2,1,0:T(8,128)(2,1)S(1)}, bf16[7,7,768]{2,1,0:T(8,128)(2,1)}, u32[]{:S(2)}) copy-start(bf16[7,7,768]{2,1,0:T(8,128)(2,1)} %param.14) | copy-start | bytes 225796
  7.8 15.9 %copy-start.2 = (bf16[1,14,14,768]{3,2,1,0:T(8,128)(2,1)S(1)}, bf16[1,14,14,768]{3,2,1,0:T(8,128)(2,1)}, u32[]{:S(2)}) copy-start(bf16[1,14,14,768]{3,2,1,0:T(8,128)(2,1)} %param.10) | copy-start | bytes 903172
  10.7 25.0 %copy-start.11 = (f32[768]{0:T(1024)S(1)}, f32[768]{0:T(1024)}, u32[]{:S(2)}) copy-start(f32[768]{0:T(1024)} %param.19) | copy-start | bytes 9220
  10.8 121.6 %reduce-scatter.2.cloned.1.call-start = ((), (), s32[]{:S(2)}) async-start(), calls=%async_computation.7 | async-start | bytes 1474560 | tf_op jit(solution)/shard_map/reduce_scatter | solution.py:497
  13.5 45.3 %copy-start = (bf16[14,16,768]{2,1,0:T(8,128)(2,1)}, bf16[14,16,768]{2,1,0:T(8,128)(2,1)S(1)}, u32[]{:S(2)}) copy-start(bf16[14,16,768]{2,1,0:T(8,128)(2,1)S(1)} %pad.4) | copy-start | bytes 1032196
  13.5 20.2 %collective-permute-start.5 = (bf16[224,768]{1,0:T(8,128)(2,1)S(1)}, bf16[224,768]{1,0:T(8,128)(2,1)S(1)}, u32[]{:S(2)}, u32[]{:S(2)}) collective-permute-start(bf16[224,768]{1,0:T(8,128)(2,1)S(1)} %bitcast.19), channel_id=1, source_target_pairs={{0,40},{8,0},{32,8},{40,32},{1,41},{9,1},{33,9},{41,33},{2,42},{10... | collective-permute-start | bytes 1032200 | tf_op jit(solution)/shard_map/ppermute | solution.py:466
  18.7 17.0 %collective-permute-start.4 = (bf16[224,768]{1,0:T(8,128)(2,1)S(1)}, bf16[224,768]{1,0:T(8,128)(2,1)S(1)}, u32[]{:S(2)}, u32[]{:S(2)}) collective-permute-start(bf16[224,768]{1,0:T(8,128)(2,1)S(1)} %bitcast.20), channel_id=1, source_target_pairs={{0,32},{8,40},{32,0},{40,8},{1,33},{9,41},{33,1},{41,9},{2,34},{10... | collective-permute-start | bytes 1032200 | tf_op jit(solution)/shard_map/ppermute | solution.py:466
  21.2 17.3 %collective-permute-start.3 = (bf16[224,768]{1,0:T(8,128)(2,1)S(1)}, bf16[224,768]{1,0:T(8,128)(2,1)S(1)}, u32[]{:S(2)}, u32[]{:S(2)}) collective-permute-start(bf16[224,768]{1,0:T(8,128)(2,1)S(1)} %bitcast.21), channel_id=1, source_target_pairs={{0,8},{8,32},{32,40},{40,0},{1,9},{9,33},{33,41},{41,1},{2,10},{10... | collective-permute-start | bytes 1032200 | tf_op jit(solution)/shard_map/ppermute | solution.py:466
  26.6 12.9 %collective-permute-start.2 = (bf16[224,768]{1,0:T(8,128)(2,1)S(1)}, bf16[224,768]{1,0:T(8,128)(2,1)S(1)}, u32[]{:S(2)}, u32[]{:S(2)}) collective-permute-start(bf16[224,768]{1,0:T(8,128)(2,1)S(1)} %get-tuple-element.28.refs_0_), channel_id=1, source_target_pairs={{0,40},{8,0},{32,8},{40,32},{1,41},{9,1},{33,9},{41,33},{2,42},{10... | collective-permute-start | bytes 1032200 | tf_op jit(solution)/shard_map/ppermute | solution.py:466
  30.6 13.5 %collective-permute-start.1 = (bf16[224,768]{1,0:T(8,128)(2,1)S(1)}, bf16[224,768]{1,0:T(8,128)(2,1)S(1)}, u32[]{:S(2)}, u32[]{:S(2)}) collective-permute-start(bf16[224,768]{1,0:T(8,128)(2,1)S(1)} %get-tuple-element.28.refs_0_), channel_id=1, source_target_pairs={{0,32},{8,40},{32,0},{40,8},{1,33},{9,41},{33,1},{41,9},{2,34},{10... | collective-permute-start | bytes 1032200 | tf_op jit(solution)/shard_map/ppermute | solution.py:466
  33.8 25.1 %copy-start.4 = (bf16[224,768]{1,0:T(8,128)(2,1)}, bf16[224,768]{1,0:T(8,128)(2,1)S(1)}, u32[]{:S(2)}) copy-start(bf16[224,768]{1,0:T(8,128)(2,1)S(1)} %collective-permute-done.5.refs_7_) | copy-start | bytes 1032196
  33.8 19.3 %collective-permute-start = (bf16[224,768]{1,0:T(8,128)(2,1)S(1)}, bf16[224,768]{1,0:T(8,128)(2,1)}, u32[]{:S(2)}, u32[]{:S(2)}) collective-permute-start(bf16[224,768]{1,0:T(8,128)(2,1)S(1)} %get-tuple-element.28.refs_0_), channel_id=1, source_target_pairs={{0,8},{8,32},{32,40},{40,0},{1,9},{9,33},{33,41},{41,1},{2,10},{10... | collective-permute-start | bytes 1032200 | tf_op jit(solution)/shard_map/ppermute | solution.py:466
  35.7 23.1 %copy-start.5 = (bf16[224,768]{1,0:T(8,128)(2,1)}, bf16[224,768]{1,0:T(8,128)(2,1)S(1)}, u32[]{:S(2)}) copy-start(bf16[224,768]{1,0:T(8,128)(2,1)S(1)} %collective-permute-done.4.refs_6_) | copy-start | bytes 1032196
  38.5 20.3 %copy-start.6 = (bf16[224,768]{1,0:T(8,128)(2,1)}, bf16[224,768]{1,0:T(8,128)(2,1)S(1)}, u32[]{:S(2)}) copy-start(bf16[224,768]{1,0:T(8,128)(2,1)S(1)} %collective-permute-done.3.refs_5_) | copy-start | bytes 1032196
  39.5 4.6 %copy-start.7 = (bf16[224,768]{1,0:T(8,128)(2,1)}, bf16[224,768]{1,0:T(8,128)(2,1)S(1)}, u32[]{:S(2)}) copy-start(bf16[224,768]{1,0:T(8,128)(2,1)S(1)} %collective-permute-done.2.refs_3_) | copy-start | bytes 1032196
  44.1 0.7 copy-start.8
  70.1 8.5 %collective-permute-start.6 = (bf16[8,640,128]{2,1,0:T(8,128)(2,1)}, bf16[8,640,128]{2,1,0:T(8,128)(2,1)S(1)}, u32[]{:S(2)}, u32[]{:S(2)}) collective-permute-start(bf16[8,640,128]{2,1,0:T(8,128)(2,1)} %get-tuple-element.30), channel_id=1, source_target_pairs={{0,16},{16,0},{1,17},{17,1},{2,18},{18,2},{3,19},{19,3},{4,20},{20... | collective-permute-start | bytes 3932168 | tf_op jit(solution)/shard_map/ppermute | solution.py:462
  81.3 12.1 %collective-permute-start.7 = (bf16[224,768]{1,0:T(8,128)(2,1)S(1)}, bf16[224,768]{1,0:T(8,128)(2,1)S(1)}, u32[]{:S(2)}, u32[]{:S(2)}) collective-permute-start(bf16[224,768]{1,0:T(8,128)(2,1)S(1)} %get-tuple-element.32), channel_id=1, source_target_pairs={{0,40},{8,0},{32,8},{40,32},{1,41},{9,1},{33,9},{41,33},{2,42},{10... | collective-permute-start | bytes 1032200 | tf_op jit(solution)/shard_map/ppermute | solution.py:466
  85.7 12.4 %collective-permute-start.8 = (bf16[224,768]{1,0:T(8,128)(2,1)S(1)}, bf16[224,768]{1,0:T(8,128)(2,1)S(1)}, u32[]{:S(2)}, u32[]{:S(2)}) collective-permute-start(bf16[224,768]{1,0:T(8,128)(2,1)S(1)} %get-tuple-element.33), channel_id=1, source_target_pairs={{0,32},{8,40},{32,0},{40,8},{1,33},{9,41},{33,1},{41,9},{2,34},{10... | collective-permute-start | bytes 1032200 | tf_op jit(solution)/shard_map/ppermute | solution.py:466
  88.1 18.3 %collective-permute-start.9 = (bf16[224,768]{1,0:T(8,128)(2,1)S(1)}, bf16[224,768]{1,0:T(8,128)(2,1)S(1)}, u32[]{:S(2)}, u32[]{:S(2)}) collective-permute-start(bf16[224,768]{1,0:T(8,128)(2,1)S(1)} %get-tuple-element.34), channel_id=1, source_target_pairs={{0,8},{8,32},{32,40},{40,0},{1,9},{9,33},{33,41},{41,1},{2,10},{10... | collective-permute-start | bytes 1032200 | tf_op jit(solution)/shard_map/ppermute | solution.py:466
  150.9 30.7 %copy-start.1 = (bf16[14,16,768]{2,1,0:T(8,128)(2,1)S(1)}, bf16[14,16,768]{2,1,0:T(8,128)(2,1)}, u32[]{:S(2)}) copy-start(bf16[14,16,768]{2,1,0:T(8,128)(2,1)} %copy-done) | copy-start | bytes 1032196
  151.6 11.7 %all-to-all-start.3 = ((bf16[8,80,128]{2,1,0:T(8,128)(2,1)}), bf16[8,80,128]{2,1,0:T(8,128)(2,1)S(1)}, u32[]{:S(2)}, u32[]{:S(2)}) async-start(bf16[8,80,128]{2,1,0:T(8,128)(2,1)} %broadcast_in_dim.19), calls=%async_computation.4 | async-start | bytes 327680 | tf_op jit(solution)/shard_map/all_to_all | solution.py:458
  163.3 15.8 %collective-permute-start.11 = (bf16[8,80,128]{2,1,0:T(8,128)(2,1)S(1)}, bf16[8,80,128]{2,1,0:T(8,128)(2,1)S(1)}, u32[]{:S(2)}, u32[]{:S(2)}) collective-permute-start(bf16[8,80,128]{2,1,0:T(8,128)(2,1)S(1)} %all-to-all-done.3.mine_ref), channel_id=1, source_target_pairs={{0,32},{32,0},{1,33},{33,1},{2,34},{34,2},{3,35},{35,3},{4,36},{36... | collective-permute-start | bytes 491528 | tf_op jit(solution)/shard_map/ppermute | solution.py:512
  170.3 13.8 %all-to-all-start.4 = ((f32[8,48,128]{2,1,0:T(8,128)}), f32[8,48,128]{2,1,0:T(8,128)S(1)}, u32[]{:S(2)}, u32[]{:S(2)}) async-start(f32[8,48,128]{2,1,0:T(8,128)} %broadcast_in_dim.20), calls=%async_computation.5 | async-start | bytes 393216 | tf_op jit(solution)/shard_map/all_to_all | solution.py:458
  177.1 7.1 %collective-permute-start.10 = (bf16[8,80,128]{2,1,0:T(8,128)(2,1)S(1)}, bf16[8,80,128]{2,1,0:T(8,128)(2,1)S(1)}, u32[]{:S(2)}, u32[]{:S(2)}) collective-permute-start(bf16[8,80,128]{2,1,0:T(8,128)(2,1)S(1)} %all-to-all-done.3.mine_ref), channel_id=1, source_target_pairs={{0,16},{16,0},{1,17},{17,1},{2,18},{18,2},{3,19},{19,3},{4,20},{20... | collective-permute-start | bytes 491528 | tf_op jit(solution)/shard_map/ppermute | solution.py:462
  179.1 5.1 %collective-permute-start.12 = (bf16[8,80,128]{2,1,0:T(8,128)(2,1)S(1)}, bf16[8,80,128]{2,1,0:T(8,128)(2,1)S(1)}, u32[]{:S(2)}, u32[]{:S(2)}) collective-permute-start(bf16[8,80,128]{2,1,0:T(8,128)(2,1)S(1)} %collective-permute-done.11.across_ref), channel_id=1, source_target_pairs={{0,16},{16,0},{1,17},{17,1},{2,18},{18,2},{3,19},{19,3},{4,20},{20... | collective-permute-start | bytes 491528 | tf_op jit(solution)/shard_map/ppermute | solution.py:462
Sparse Core Ops, SparseCore 0:
  10.9 47.8 all-gather.1
  81.5 36.7 reduce-scatter.1

commit v5 on v4

--- a/solution.py
+++ b/solution.py
@@ -183,9 +183,8 @@
     scaled_in = refs[4:8]
     pack_in, layer_ref = refs[8:10]
     parts = refs[10:14]
-    outs = refs[14:16]
-    scale_ref = refs[16]
-    normed, scaled, pack, act, grad, sems = refs[17:23]
+    out_ref, scale_ref = refs[14:16]
+    normed, scaled, pack, act, grad, sems = refs[16:22]
     copies = [pltpu.make_async_copy(pack_in, pack, sems.at[8])]
     for i in range(4):
         rows = pl.ds(i * PIX, PIX)
@@ -213,8 +212,8 @@
         parts[i][...] = jnp.dot(preact_grad, first, preferred_element_type=F32).astype(BF16)
     product = tn(act[...], scaled[...])
     scale_ref[...] = jnp.sum((second.astype(F32) * product).reshape(CH // 8, 8, CH), axis=0)
-    spread(outs, (product * layer).astype(BF16), 0)
-    spread(outs, tn(grad[...], normed[...]).astype(BF16), 18)
+    spread(out_ref, (product * layer).astype(BF16), 0)
+    spread(out_ref, tn(grad[...], normed[...]).astype(BF16), 18)
     bias = jnp.dot(jnp.ones((16, 4 * PIX), BF16), grad[...], preferred_element_type=F32)
     row = lax.broadcasted_iota(jnp.int32, (16, LANES), 0)
     empty = jnp.zeros((16, LANES), BF16)
@@ -227,17 +226,17 @@
         rows = rows.astype(BF16)
         for z in range(8):
             for s in range(36, 40):
-                outs[half][z, s * 16 : s * 16 + 16, :] = rows if s == 36 else empty
-
-
-def spread(outs, matrix, start):
+                out_ref[z, half * 640 + s * 16 : half * 640 + s * 16 + 16, :] = rows if s == 36 else empty
+
+
+def spread(out_ref, matrix, start):
     for half in range(2):
         for z in range(8):
             for j in range(BLOCKS):
                 for part in range(3):
                     s = start + j * 3 + part
                     row = z * UNITS + half * OWN + part * 16
-                    outs[half][z, s * 16 : s * 16 + 16, :] = matrix[
+                    out_ref[z, half * 640 + s * 16 : half * 640 + s * 16 + 16, :] = matrix[
                         row : row + 16, j * LANES : (j + 1) * LANES
                     ]
 
@@ -247,10 +246,10 @@
         hidden_kernel,
         grid=(1,),
         out_shape=(jax.ShapeDtypeStruct((PIX, CH), BF16),) * 4
-        + (jax.ShapeDtypeStruct((8, 640, LANES), BF16),) * 2
+        + (jax.ShapeDtypeStruct((8, 1280, LANES), BF16),)
         + (jax.ShapeDtypeStruct((8, CH), F32),),
         in_specs=[pl.BlockSpec(memory_space=pl.ANY)] * 9 + [block(1, CH)],
-        out_specs=(block(PIX, CH),) * 4 + (block(8, 640, LANES),) * 2 + (block(8, CH),),
+        out_specs=(block(PIX, CH),) * 4 + (block(8, 1280, LANES),) + (block(8, CH),),
         scratch_shapes=[
             pltpu.VMEM((4 * PIX, CH), BF16),
             pltpu.VMEM((4 * PIX, CH), BF16),
@@ -389,15 +388,20 @@
 
 
 def finish_kernel(
-    images, place_ref, small_ref, pre_ref, mine_ref, mine_core_ref, across_ref, across_core_ref,
-    image_ref, first_ref, second_ref, bias_ref, kernel_ref, gain_ref, scale_ref, gathered,
+    images, place_ref, small_in, small_core_in, pre_ref, mine_ref, other_ref,
+    image_ref, first_ref, second_ref, bias_ref, kernel_ref, gain_ref, scale_ref, gathered, small_ref,
 ):
-    half, core, column = place_ref[0], place_ref[1], place_ref[2]
-    factor = images / small_ref[0, 51:52, :]
-    gathered[half * 2 + core] = mine_ref[...]
-    gathered[half * 2 + 1 - core] = mine_core_ref[...]
-    gathered[(1 - half) * 2 + core] = across_ref[...]
-    gathered[(1 - half) * 2 + 1 - core] = across_core_ref[...]
+    half, core, column, pair = place_ref[0], place_ref[1], place_ref[2], place_ref[3]
+    for b in range(2):
+        gathered[b * 2 + core] = mine_ref[:, b]
+        gathered[b * 2 + 1 - core] = other_ref[:, b]
+    for a in range(2):
+        for b in range(2):
+            part = 2 * (pair + a - 2 * a * pair) + (half + b - 2 * b * half)
+            rows = slice((a * 2 + b) * OWN, (a * 2 + b + 1) * OWN)
+            for first, source in ((core, small_in), (1 - core, small_core_in)):
+                small_ref[pl.ds(pl.multiple_of((first * 4 + part) * OWN, OWN), OWN), :] = source[rows, :]
+    factor = images / small_ref[51:52, :]
     lane = lax.broadcasted_iota(jnp.int32, (8, CH), 1)
     bias = jnp.zeros((8, CH), F32)
     for q in range(4):
@@ -410,9 +414,9 @@
         lanes = slice(j * LANES, (j + 1) * LANES)
         image_ref[0, :, :, lanes] = (pre_ref[0, :, :, lanes] * factor.reshape(1, 1, LANES)).astype(BF16)
         for a in range(7):
-            kernel_ref[a, :, lanes] = small_ref[j, a * 7 : a * 7 + 7, :] * factor
-        gain_ref[lanes] = small_ref[j, 49, :] * factor[0]
-        scale_ref[lanes] = small_ref[j, 50, :] * factor[0]
+            kernel_ref[a, :, lanes] = small_ref[j * 64 + a * 7 : j * 64 + a * 7 + 7, :] * factor
+        gain_ref[lanes] = small_ref[j * 64 + 49, :] * factor[0]
+        scale_ref[lanes] = small_ref[j * 64 + 50, :] * factor[0]
         for q in range(4):
             for part in range(3):
                 rows = slice(q * OWN + part * 16, q * OWN + part * 16 + 16)
@@ -422,7 +426,7 @@
                     out_ref[rows, lanes] = piece.astype(F32) * factor
 
 
-def finish(images, place, small, pre, mine, mine_core, across, across_core):
+def finish(images, place, small, small_core, pre, mine, other):
     return pl.pallas_call(
         functools.partial(finish_kernel, images),
         grid=(1,),
@@ -435,8 +439,8 @@
             jax.ShapeDtypeStruct((CH,), F32),
             jax.ShapeDtypeStruct((CH,), F32),
         ),
-        in_specs=[scalars(), block(BLOCKS, 64, LANES), block(1, ROWS, COLS, CH)]
-        + [block(8, 80, LANES)] * 4,
+        in_specs=[scalars(), block(4 * OWN, LANES), block(4 * OWN, LANES), block(1, ROWS, COLS, CH)]
+        + [block(8, 2, 80, LANES)] * 2,
         out_specs=(
             block(1, ROWS, COLS, CH),
             block(192, CH),
@@ -446,11 +450,11 @@
             block(CH),
             block(CH),
         ),
-        scratch_shapes=[pltpu.VMEM((4, 8, 80, LANES), BF16)],
+        scratch_shapes=[pltpu.VMEM((4, 8, 80, LANES), BF16), pltpu.VMEM((8 * OWN, LANES), F32)],
         compiler_params=params(12),
         interpret=INTERPRET,
         name="finish",
-    )(place, small, pre, mine, mine_core, across, across_core)
+    )(place, small, small_core, pre, mine, other)
 
 
 def to_all(value, axes):
@@ -458,8 +462,23 @@
     return lax.all_to_all(jnp.broadcast_to(value, (count, *value.shape)), axes, 0, 0, tiled=True)
 
 
+def swap(axis, value):
+    return lax.ppermute(value, axis, [(0, 1), (1, 0)])
+
+
 def swap_core(value):
-    return lax.ppermute(value, "core", [(0, 1), (1, 0)])
+    return swap("core", value)
+
+
+def split(small, holds):
+    row = lax.broadcasted_iota(jnp.int32, small.shape, 0)
+    rest = small - small.astype(BF16).astype(F32)
+    return jnp.where((row == 4) & holds, jnp.roll(rest, 1, 0), small).astype(BF16)
+
+
+def join(small, holds):
+    row = lax.broadcasted_iota(jnp.int32, small.shape, 0)
+    return jnp.where((row == 3) & holds, small + jnp.roll(small, -1, 0), small)
 
 
 def ring(value, shift):
@@ -492,30 +511,28 @@
     scaled = jnp.pad(scaled, ((0, 0), (0, WIDE - COLS), (0, 0))).reshape(PIX, CH)
     scaled_all = ring_share(scaled)
 
-    *parts, grads, other, scale = hidden(normed_all, scaled_all, packed, layer)
-    grads = (grads.astype(F32) + swap_core(other).astype(F32)).astype(BF16)
-    grads = lax.psum_scatter(grads, "z", scatter_dimension=0, tiled=True).reshape(8, 80, LANES)
+    *parts, grads, scale = hidden(normed_all, scaled_all, packed, layer)
+    grads = lax.psum_scatter(grads, "z", scatter_dimension=0, tiled=True).reshape(2, 8, 80, LANES)
+    grads = (grads[0].astype(F32) + swap_core(grads[1]).astype(F32)).astype(BF16)
 
     returned = [ring(parts[r], 4 - r) for r in range(1, 4)]
     small, conv_grad = backward(own_weight.reshape(1), parts[0], *returned, centred, inv, gain, scale, image[0])
     small = lax.all_to_all(small.reshape(8, OWN, LANES), TEAM, 0, 0, tiled=True)
-    small = jnp.sum(to_all(jnp.sum(small, axis=0), "z"), axis=0)
-    high = small.astype(BF16)
-    low = (small - high.astype(F32)).astype(BF16)
-    both = jnp.broadcast_to(jnp.concatenate([high, low], axis=0), (8, 2 * OWN, LANES))
+    holds = lax.axis_index(TEAM) == 1
+    small = join(jnp.sum(to_all(split(jnp.sum(small, axis=0), holds), "z").astype(F32), axis=0), holds)
+    both = jnp.broadcast_to(split(small, holds), (8, OWN, LANES))
     both = lax.all_to_all(jnp.concatenate([grads, both], axis=1), "y", 0, 0, tiled=True).astype(F32)
-    mine = to_all(jnp.sum(both[:, 0:80, :], axis=0).astype(BF16), "y")
-    small = jnp.sum(both[:, 80:128, :] + both[:, 128:176, :], axis=0)
+    mine = to_all(jnp.sum(both[:, 0:80, :], axis=0).astype(BF16), ("y", "xh")).reshape(8, 2, 80, LANES)
+    small = join(jnp.sum(both[:, 80:128, :], axis=0), holds)
+    small = jnp.concatenate([small, swap("xh", small)], axis=0)
+    small = jnp.concatenate([small, swap("xl", small)], axis=0)
     small, mine = lax.optimization_barrier((small, mine))
-    small = to_all(small, TEAM).reshape(BLOCKS, 64, LANES)
-
-    across = lax.ppermute(mine, "xh", [(0, 1), (1, 0)])
     pre = input_grad(conv_grad, kernel, scaled)
     images = float(lax.axis_size(REPLICA) * lax.axis_size(SHARD))
     grad_image, grad_first, grad_second, grad_bias, grad_kernel, grad_gain, grad_scale = finish(
         images,
-        jnp.stack([half, core, column]).astype(jnp.int32),
-        small, pre, mine, swap_core(mine), across, swap_core(across),
+        jnp.stack([half, core, column, lax.axis_index("xl")]).astype(jnp.int32),
+        small, swap_core(small), pre, mine, swap_core(mine),
     )
     return (
         grad_image,

time: 194 us -> 184 us (0.948)
  blocking collectives: 39.5 us -> 17.5 us
  waiting for transfers between devices: 49.3 us -> 54.8 us
  starting transfers between devices: 55 us -> 59.6 us
  local copies, waits for them, and re-layouts: 2.28 us -> 5.75 us
  other arithmetic: 6.46 us -> 4.13 us
    all_to_all x2 -> x0, blocking collectives: 22 us -> none  [the longest x1 13.2 us: to_all(): lax.all_to_all(jnp.broadcast_to(value, (count, *value.shape)), axes, 0, 0...]
    all_to_all x0 -> x1, waiting for transfers between devices: none -> 6.06 us  [per_device(): small = lax.all_to_all(small.reshape(8, OWN, LANES), TEAM, 0, 0, tiled=True)]
    all_to_all x0 -> x1, starting transfers between devices: none -> 5.78 us  [per_device(): small = lax.all_to_all(small.reshape(8, OWN, LANES), TEAM, 0, 0, tiled=True)]
    ppermute x4 -> x5, waiting for transfers between devices: 2.86 us -> 5.84 us  [swap(): return lax.ppermute(value, axis, [(0, 1), (1, 0)])]
    convert_element_type x2 -> x3, other arithmetic: 2.74 us -> 0.21 us  [the longest x2 0.16 us: split(): jnp.where((row == 4) & holds, jnp.roll(rest, 1, 0), small).astype(BF16)]
    unnamed x24 -> x26, local copies, waits for them, and re-layouts: 0.78 us -> 3.19 us
    all_to_all x2, starting transfers between devices: 10.1 us -> 7.76 us  [to_all(): lax.all_to_all(jnp.broadcast_to(value, (count, *value.shape)), axes, 0, 0...]
    ppermute x9, waiting for transfers between devices: 32.4 us -> 30.1 us  [ring(): return lax.ppermute(value, RING, [(i, (i + shift) % 4) for i in range(4)])]
  transfers between devices with their start and end apart: 17 -> 19, of which waited for: 10 -> 14; matrix products, arithmetic and copies ran while one was open for 2% -> 2% of each run, Pallas kernels for 5% -> 6%
where the time goes in v5:
time: 184 us; the launch traced here: 183 us
  starting transfers between devices  59.6 us (32%)
  waiting for transfers between devices  54.8 us (30%)
  Pallas kernels  26.1 us (14%)
  blocking collectives  17.5 us (10%)
  between operations  15.1 us (8%)
  local copies, waits for them, and re-layouts  5.75 us (3%)
  other arithmetic  4.13 us (2%)
    ppermute x9, waiting for transfers between devices, ring(): return lax.ppermute(value, RING, [(i, (i + shift) % 4) for i in range(4)])  30.1 us
    ppermute x9, starting transfers between devices, ring(): return lax.ppermute(value, RING, [(i, (i + shift) % 4) for i in range(4)])  28.4 us
    ppermute x5, starting transfers between devices, swap(): return lax.ppermute(value, axis, [(0, 1), (1, 0)])  17.6 us
    all_to_all x1, blocking collectives, per_device(): lax.all_to_all(jnp.concatenate([grads, both], axis=1), 'y', 0, 0, tiled=T...  17.5 us
    pallas_call x1, Pallas kernels, hidden(): pl.pallas_call(hidden_kernel, grid=(1,), out_shape=(jax.ShapeDtypeStruct(...  11.3 us
    all_to_all x2, waiting for transfers between devices, to_all(): lax.all_to_all(jnp.broadcast_to(value, (count, *value.shape)), axes, 0, 0...  8.31 us
    all_to_all x2, starting transfers between devices, to_all(): lax.all_to_all(jnp.broadcast_to(value, (count, *value.shape)), axes, 0, 0...  7.76 us
    all_to_all x1, waiting for transfers between devices, per_device(): small = lax.all_to_all(small.reshape(8, OWN, LANES), TEAM, 0, 0, tiled=True)  6.06 us
  transfers between devices with their start and end apart: 19, of which 14 were waited for; matrix products, arithmetic and copies ran while one was open for 2% of the time, Pallas kernels for 6%

profile of v5, /device:TPU:1, one launch (start us, length us, event | category | flops | bytes accessed | tf_op | source)
XLA Modules:
  0.0 183.1 jit_solution(7362134123516569057)
XLA Ops:
  7.2 0.0 all-gather.2.cloned.1.call-start
  7.3 0.6 pad_add_fusion.1.place_ref
  7.8 2.7 %pack.1 = bf16[208,768]{1,0:T(8,128)(2,1)} custom-call(s32[2]{0:T(128)} %pad_add_fusion.1.place_ref, bf16[192,768]{1,0:T(8,128)(2,1)} %bitcast.35, f32[1,192]{1,0:T(1,128)} %bitcast.39, bf16[192,768]{1,0:T(8,128)(2,1)} %second_in.1), custom_call_target="tpu_custom_call" | custom-call | tf_op jit(solution)/shard_map/pack/pallas_call | solution.py:84
  10.6 0.0 all-gather.2.cloned.1.call-update
  10.6 0.0 reduce-scatter.2.cloned.1.call-start
  11.3 1.3 fusion.4
  12.6 1.7 fusion
  14.3 0.0 copy-start
  14.3 5.2 %collective-permute-start.5 = (bf16[224,768]{1,0:T(8,128)(2,1)S(1)}, bf16[224,768]{1,0:T(8,128)(2,1)S(1)}, u32[]{:S(2)}, u32[]{:S(2)}) collective-permute-start(bf16[224,768]{1,0:T(8,128)(2,1)S(1)} %bitcast.24), channel_id=1, source_target_pairs={{0,40},{8,0},{32,8},{40,32},{1,41},{9,1},{33,9},{41,33},{2,42},{10... | collective-permute-start | bytes 1032200 | tf_op jit(solution)/shard_map/ppermute | solution.py:485
  19.5 2.4 %collective-permute-start.4 = (bf16[224,768]{1,0:T(8,128)(2,1)S(1)}, bf16[224,768]{1,0:T(8,128)(2,1)S(1)}, u32[]{:S(2)}, u32[]{:S(2)}) collective-permute-start(bf16[224,768]{1,0:T(8,128)(2,1)S(1)} %bitcast.25), channel_id=1, source_target_pairs={{0,32},{8,40},{32,0},{40,8},{1,33},{9,41},{33,1},{41,9},{2,34},{10... | collective-permute-start | bytes 1032200 | tf_op jit(solution)/shard_map/ppermute | solution.py:485
  22.0 2.5 %collective-permute-start.3 = (bf16[224,768]{1,0:T(8,128)(2,1)S(1)}, bf16[224,768]{1,0:T(8,128)(2,1)S(1)}, u32[]{:S(2)}, u32[]{:S(2)}) collective-permute-start(bf16[224,768]{1,0:T(8,128)(2,1)S(1)} %bitcast.26), channel_id=1, source_target_pairs={{0,8},{8,32},{32,40},{40,0},{1,9},{9,33},{33,41},{41,1},{2,10},{10... | collective-permute-start | bytes 1032200 | tf_op jit(solution)/shard_map/ppermute | solution.py:485
  24.6 2.8 %conv_norm.1 = (bf16[224,768]{1,0:T(8,128)(2,1)S(1)}, f32[6,14,16,128]{3,2,1,0:T(8,128)S(1)}, f32[14,16,128]{2,1,0:T(8,128)S(1)}) custom-call(bf16[14,14,768]{2,1,0:T(8,128)(2,1)S(1)} %bitcast.29, bf16[49,768]{1,0:T(8,128)(2,1)S(1)} %reshape.55.kernel_ref, f32[1,768]{1,0:T(1,128)S(1)} %reshape.56.gain_ref), custom_call_target="tpu_custom_call" | custom-call | tf_op jit(solution)/shard_map/conv_norm/pallas_call | solution.py:153
  27.4 4.0 %collective-permute-start.2 = (bf16[224,768]{1,0:T(8,128)(2,1)S(1)}, bf16[224,768]{1,0:T(8,128)(2,1)S(1)}, u32[]{:S(2)}, u32[]{:S(2)}) collective-permute-start(bf16[224,768]{1,0:T(8,128)(2,1)S(1)} %get-tuple-element.27.refs_0_), channel_id=1, source_target_pairs={{0,40},{8,0},{32,8},{40,32},{1,41},{9,1},{33,9},{41,33},{2,42},{10... | collective-permute-start | bytes 1032200 | tf_op jit(solution)/shard_map/ppermute | solution.py:485
  31.4 3.1 %collective-permute-start.1 = (bf16[224,768]{1,0:T(8,128)(2,1)S(1)}, bf16[224,768]{1,0:T(8,128)(2,1)S(1)}, u32[]{:S(2)}, u32[]{:S(2)}) collective-permute-start(bf16[224,768]{1,0:T(8,128)(2,1)S(1)} %get-tuple-element.27.refs_0_), channel_id=1, source_target_pairs={{0,32},{8,40},{32,0},{40,8},{1,33},{9,41},{33,1},{41,9},{2,34},{10... | collective-permute-start | bytes 1032200 | tf_op jit(solution)/shard_map/ppermute | solution.py:485
  34.5 0.0 collective-permute-done.5.refs_7_
  34.6 0.7 copy-done.5
  35.3 1.9 %collective-permute-start = (bf16[224,768]{1,0:T(8,128)(2,1)S(1)}, bf16[224,768]{1,0:T(8,128)(2,1)}, u32[]{:S(2)}, u32[]{:S(2)}) collective-permute-start(bf16[224,768]{1,0:T(8,128)(2,1)S(1)} %get-tuple-element.27.refs_0_), channel_id=1, source_target_pairs={{0,8},{8,32},{32,40},{40,0},{1,9},{9,33},{33,41},{41,1},{2,10},{10... | collective-permute-start | bytes 1032200 | tf_op jit(solution)/shard_map/ppermute | solution.py:485
  37.2 0.0 collective-permute-done.4.refs_6_
  37.3 2.0 %collective-permute-done.3.refs_5_ = bf16[224,768]{1,0:T(8,128)(2,1)S(1)} collective-permute-done((bf16[224,768]{1,0:T(8,128)(2,1)S(1)}, bf16[224,768]{1,0:T(8,128)(2,1)S(1)}, u32[]{:S(2)}, u32[]{:S(2)}) %collective-permute-start.3) | collective-permute-done | bytes 344096 | tf_op jit(solution)/shard_map/ppermute | solution.py:485
  39.3 1.1 collective-permute-done.2.refs_3_
  40.4 4.6 %collective-permute-done.1.refs_2_ = bf16[224,768]{1,0:T(8,128)(2,1)S(1)} collective-permute-done((bf16[224,768]{1,0:T(8,128)(2,1)S(1)}, bf16[224,768]{1,0:T(8,128)(2,1)S(1)}, u32[]{:S(2)}, u32[]{:S(2)}) %collective-permute-start.1) | collective-permute-done | bytes 344096 | tf_op jit(solution)/shard_map/ppermute | solution.py:485
  44.9 0.7 copy-done.9
  45.7 8.6 %collective-permute-done.refs_1_ = bf16[224,768]{1,0:T(8,128)(2,1)} collective-permute-done((bf16[224,768]{1,0:T(8,128)(2,1)S(1)}, bf16[224,768]{1,0:T(8,128)(2,1)}, u32[]{:S(2)}, u32[]{:S(2)}) %collective-permute-start) | collective-permute-done | bytes 344096 | tf_op jit(solution)/shard_map/ppermute | solution.py:485
  54.2 4.5 %all-gather.2.cloned.1.call-done = bf16[1664,768]{1,0:T(8,128)(2,1)} async-done(((bf16[208,768]{1,0:T(8,128)(2,1)}), bf16[1664,768]{1,0:T(8,128)(2,1)}) %all-gather.2.cloned.1.call-update) | async-done | bytes 2555920 | tf_op jit(solution)/shard_map/all_gather | solution.py:500
  58.8 11.3 %hidden.1 = (bf16[224,768]{1,0:T(8,128)(2,1)S(1)}, bf16[224,768]{1,0:T(8,128)(2,1)S(1)}, bf16[224,768]{1,0:T(8,128)(2,1)S(1)}, bf16[224,768]{1,0:T(8,128)(2,1)S(...) custom-call(bf16[224,768]{1,0:T(8,128)(2,1)S(1)} %get-tuple-element.27.refs_0_, ...), custom_call_target="tpu_custom_call" | custom-call | tf_op jit(solution)/shard_map/hidden/pallas_call | solution.py:245
  70.0 0.0 copy-start.3
  70.1 0.7 copy-done.3
  70.8 0.0 reduce-scatter.2.cloned.1.call-update
  70.8 1.0 copy-done.4
  71.8 4.3 %collective-permute-start.7 = (bf16[224,768]{1,0:T(8,128)(2,1)S(1)}, bf16[224,768]{1,0:T(8,128)(2,1)S(1)}, u32[]{:S(2)}, u32[]{:S(2)}) collective-permute-start(bf16[224,768]{1,0:T(8,128)(2,1)S(1)} %copy-done.4), channel_id=1, source_target_pairs={{0,40},{8,0},{32,8},{40,32},{1,41},{9,1},{33,9},{41,33},{2,42},{10... | collective-permute-start | bytes 1032200 | tf_op jit(solution)/shard_map/ppermute | solution.py:485
  76.0 2.4 %collective-permute-start.8 = (bf16[224,768]{1,0:T(8,128)(2,1)S(1)}, bf16[224,768]{1,0:T(8,128)(2,1)S(1)}, u32[]{:S(2)}, u32[]{:S(2)}) collective-permute-start(bf16[224,768]{1,0:T(8,128)(2,1)S(1)} %get-tuple-element.31), channel_id=1, source_target_pairs={{0,32},{8,40},{32,0},{40,8},{1,33},{9,41},{33,1},{41,9},{2,34},{10... | collective-permute-start | bytes 1032200 | tf_op jit(solution)/shard_map/ppermute | solution.py:485
  78.5 2.5 %collective-permute-start.9 = (bf16[224,768]{1,0:T(8,128)(2,1)S(1)}, bf16[224,768]{1,0:T(8,128)(2,1)S(1)}, u32[]{:S(2)}, u32[]{:S(2)}) collective-permute-start(bf16[224,768]{1,0:T(8,128)(2,1)S(1)} %get-tuple-element.32), channel_id=1, source_target_pairs={{0,8},{8,32},{32,40},{40,0},{1,9},{9,33},{33,41},{41,1},{2,10},{10... | collective-permute-start | bytes 1032200 | tf_op jit(solution)/shard_map/ppermute | solution.py:485
  81.0 0.4 collective-permute-done.7.one_ref
  81.4 4.3 %collective-permute-done.8.two_ref = bf16[224,768]{1,0:T(8,128)(2,1)S(1)} collective-permute-done((bf16[224,768]{1,0:T(8,128)(2,1)S(1)}, bf16[224,768]{1,0:T(8,128)(2,1)S(1)}, u32[]{:S(2)}, u32[]{:S(2)}) %collective-permute-start.8) | collective-permute-done | bytes 344096 | tf_op jit(solution)/shard_map/ppermute | solution.py:485
  85.6 9.2 %collective-permute-done.9.three_ref = bf16[224,768]{1,0:T(8,128)(2,1)S(1)} collective-permute-done((bf16[224,768]{1,0:T(8,128)(2,1)S(1)}, bf16[224,768]{1,0:T(8,128)(2,1)S(1)}, u32[]{:S(2)}, u32[]{:S(2)}) %collective-permute-start.9) | collective-permute-done | bytes 344096 | tf_op jit(solution)/shard_map/ppermute | solution.py:485
  94.8 4.8 %norm_back.1 = (f32[6,64,128]{2,1,0:T(8,128)}, f32[6,14,16,128]{3,2,1,0:T(8,128)S(1)}) custom-call(f32[1]{0:T(128)} %bitcast.14.weight_ref, bf16[224,768]{1,0:T(8,128)(2,1)S(1)} %get-tuple-element.29.zero_ref, bf16[224,768]{1,0:T(8,128)(2,1)S(1)} %collective-permute-done.7.one_ref, bf16[224,768]{1,0:T(8,128)(2,1)S(1)} %collective-permute-done.8.two_ref, ...), custom_call_target="tpu_custom_call" | custom-call | tf_op jit(solution)/shard_map/norm_back/pallas_call | solution.py:324
  99.6 5.8 %all-to-all-start = ((f32[8,48,128]{2,1,0:T(8,128)}), f32[8,48,128]{2,1,0:T(8,128)S(1)}, u32[]{:S(2)}, u32[]{:S(2)}) async-start(f32[8,48,128]{2,1,0:T(8,128)} %bitcast.15), calls=%async_computation.1 | async-start | bytes 393216 | tf_op jit(solution)/shard_map/all_to_all | solution.py:520
  105.4 6.1 %all-to-all-done = f32[8,48,128]{2,1,0:T(8,128)S(1)} async-done(((f32[8,48,128]{2,1,0:T(8,128)}), f32[8,48,128]{2,1,0:T(8,128)S(1)}, u32[]{:S(2)}, u32[]{:S(2)}) %all-to-all-start) | async-done | bytes 196640 | tf_op jit(solution)/shard_map/all_to_all | solution.py:520
  111.5 0.1 fusion.2
  111.6 0.7 broadcast_in_dim.14
  112.2 4.2 %all-to-all-start.1 = ((bf16[8,48,128]{2,1,0:T(8,128)(2,1)}), bf16[8,48,128]{2,1,0:T(8,128)(2,1)S(1)}, u32[]{:S(2)}, u32[]{:S(2)}) async-start(bf16[8,48,128]{2,1,0:T(8,128)(2,1)} %broadcast_in_dim.14), calls=%async_computation.2 | async-start | bytes 196608 | tf_op jit(solution)/shard_map/all_to_all | solution.py:462
  116.5 7.8 %all-to-all-done.1 = bf16[8,48,128]{2,1,0:T(8,128)(2,1)S(1)} async-done(((bf16[8,48,128]{2,1,0:T(8,128)(2,1)}), bf16[8,48,128]{2,1,0:T(8,128)(2,1)S(1)}, u32[]{:S(2)}, u32[]{:S(2)}) %all-to-all-start.1) | async-done | bytes 98336 | tf_op jit(solution)/shard_map/all_to_all | solution.py:462
  124.3 0.0 copy-start.1
  124.3 0.1 convert_subtract_fusion
  124.4 0.0 reduce-scatter.2.cloned.1.call-done
  124.4 1.0 fusion.5
  125.5 3.4 %collective-permute-start.6 = (bf16[8,80,128]{2,1,0:T(8,128)(2,1)S(1)}, bf16[8,80,128]{2,1,0:T(8,128)(2,1)S(1)}, u32[]{:S(2)}, u32[]{:S(2)}) collective-permute-start(bf16[8,80,128]{2,1,0:T(8,128)(2,1)S(1)} %bitcast.36), channel_id=1, source_target_pairs={{0,16},{16,0},{1,17},{17,1},{2,18},{18,2},{3,19},{19,3},{4,20},{20... | collective-permute-start | bytes 491528 | tf_op jit(solution)/shard_map/ppermute | solution.py:466
  128.9 0.1 fusion.3
  129.0 0.9 collective-permute-done.6
  130.0 17.5 %all_to_all.20 = bf16[8,128,128]{2,1,0:T(8,128)(2,1)S(1)} all-to-all(bf16[8,128,128]{2,1,0:T(8,128)(2,1)S(1)} %pad_maximum_fusion), channel_id=1, replica_groups=mesh['y'=8,'xh'=2,'core'=2,'xl'=2,'z'=8] {'y'}, dimensions={0} | all-to-all | bytes 524288 | tf_op jit(solution)/shard_map/all_to_all | solution.py:524
  147.6 0.8 broadcast_in_dim.16
  148.3 3.5 %all-to-all-start.3 = ((bf16[16,80,128]{2,1,0:T(8,128)(2,1)}), bf16[16,80,128]{2,1,0:T(8,128)(2,1)S(1)}, u32[]{:S(2)}, u32[]{:S(2)}) async-start(bf16[16,80,128]{2,1,0:T(8,128)(2,1)} %broadcast_in_dim.16), calls=%async_computation.4 | async-start | bytes 655360 | tf_op jit(solution)/shard_map/all_to_all | solution.py:462
  151.9 0.1 add_select_fusion
  152.0 4.6 %collective-permute-start.10 = (f32[48,128]{1,0:T(8,128)S(1)}, f32[48,128]{1,0:T(8,128)S(1)}, u32[]{:S(2)}, u32[]{:S(2)}) collective-permute-start(f32[48,128]{1,0:T(8,128)S(1)} %add_select_fusion), channel_id=1, source_target_pairs={{0,32},{32,0},{1,33},{33,1},{2,34},{34,2},{3,35},{35,3},{4,36},{36... | collective-permute-start | bytes 73736 | tf_op jit(solution)/shard_map/ppermute | solution.py:466
  156.7 1.9 %collective-permute-done.10 = f32[48,128]{1,0:T(8,128)S(1)} collective-permute-done((f32[48,128]{1,0:T(8,128)S(1)}, f32[48,128]{1,0:T(8,128)S(1)}, u32[]{:S(2)}, u32[]{:S(2)}) %collective-permute-start.10) | collective-permute-done | bytes 24608 | tf_op jit(solution)/shard_map/ppermute | solution.py:466
  158.5 2.1 %collective-permute-start.11 = (f32[96,128]{1,0:T(8,128)S(1)}, f32[96,128]{1,0:T(8,128)S(1)}, u32[]{:S(2)}, u32[]{:S(2)}) collective-permute-start(f32[96,128]{1,0:T(8,128)S(1)} %pad_maximum_fusion.2), channel_id=1, source_target_pairs={{0,8},{8,0},{1,9},{9,1},{2,10},{10,2},{3,11},{11,3},{4,12},{12,4},... | collective-permute-start | bytes 147464 | tf_op jit(solution)/shard_map/ppermute | solution.py:466
  160.6 3.1 %collective-permute-done.11 = f32[96,128]{1,0:T(8,128)S(1)} collective-permute-done((f32[96,128]{1,0:T(8,128)S(1)}, f32[96,128]{1,0:T(8,128)S(1)}, u32[]{:S(2)}, u32[]{:S(2)}) %collective-permute-start.11) | collective-permute-done | bytes 49184 | tf_op jit(solution)/shard_map/ppermute | solution.py:466
  163.7 0.5 all-to-all-done.3
  164.2 5.6 %collective-permute-start.13 = (bf16[8,2,80,128]{3,2,1,0:T(8,128)(2,1)S(1)}, bf16[8,2,80,128]{3,2,1,0:T(8,128)(2,1)S(1)}, u32[]{:S(2)}, u32[]{:S(2)}) collective-permute-start(bf16[8,2,80,128]{3,2,1,0:T(8,128)(2,1)S(1)} %bitcast.31), channel_id=1, source_target_pairs={{0,16},{16,0},{1,17},{17,1},{2,18},{18,2},{3,19},{19,3},{4,20},{20... | collective-permute-start | bytes 983048 | tf_op jit(solution)/shard_map/ppermute | solution.py:466
  169.8 1.9 %collective-permute-start.12 = (f32[192,128]{1,0:T(8,128)S(1)}, f32[192,128]{1,0:T(8,128)S(1)}, u32[]{:S(2)}, u32[]{:S(2)}) collective-permute-start(f32[192,128]{1,0:T(8,128)S(1)} %pad_maximum_fusion.1.small_in), channel_id=1, source_target_pairs={{0,16},{16,0},{1,17},{17,1},{2,18},{18,2},{3,19},{19,3},{4,20},{20... | collective-permute-start | bytes 294920 | tf_op jit(solution)/shard_map/ppermute | solution.py:466
  171.7 0.1 pad_add_fusion.place_ref
  171.8 2.6 %input_grad.1.pre_ref = f32[1,14,14,768]{3,2,1,0:T(8,128)S(1)} custom-call(f32[6,14,16,128]{3,2,1,0:T(8,128)S(1)} %get-tuple-element.38.conv_ref, bf16[49,768]{1,0:T(8,128)(2,1)S(1)} %reshape.55.kernel_ref, bf16[224,768]{1,0:T(8,128)(2,1)S(1)} %bitcast.28), custom_call_target="tpu_custom_call" | custom-call | tf_op jit(solution)/shard_map/input_grad/pallas_call | solution.py:373
  174.4 0.0 collective-permute-done.13.other_ref
  174.4 1.8 %finish.1 = (bf16[1,14,14,768]{3,2,1,0:T(8,128)(2,1)}, f32[192,768]{1,0:T(8,128)}, f32[192,768]{1,0:T(8,128)}, f32[1,192]{1,0:T(1,128)}, f32[7,7,768]{2,1,0:T(8,128)}, /*index=5*/f32[768]{0:T(1024)}, f32[768]{0:T(1024)}) custom-call(s32[4]{0:T(128)S(1)} %pad_add_fusion.place_ref, f32[192,128]{1,0:T(8,128)S(1)} %pad_maximum_fusion.1.small_in, ...), custom_call_target="tpu_custom_call" | custom-call | tf_op jit(solution)/shard_map/finish/pallas_call | solution.py:430
  (43 shorter events, 0.4 us)
Async XLA Ops:
  7.2 17.3 %copy-start.11 = (f32[768]{0:T(1024)S(1)}, f32[768]{0:T(1024)}, u32[]{:S(2)}) copy-start(f32[768]{0:T(1024)} %param.15) | copy-start | bytes 9220
  7.2 17.3 %copy-start.10 = (bf16[7,7,768]{2,1,0:T(8,128)(2,1)S(1)}, bf16[7,7,768]{2,1,0:T(8,128)(2,1)}, u32[]{:S(2)}) copy-start(bf16[7,7,768]{2,1,0:T(8,128)(2,1)} %param.14) | copy-start | bytes 225796
  7.2 17.4 %copy-start.2 = (bf16[1,14,14,768]{3,2,1,0:T(8,128)(2,1)S(1)}, bf16[1,14,14,768]{3,2,1,0:T(8,128)(2,1)}, u32[]{:S(2)}) copy-start(bf16[1,14,14,768]{3,2,1,0:T(8,128)(2,1)} %param.10) | copy-start | bytes 903172
  7.2 30.0 %copy-start.12 = (f32[768]{0:T(1024)S(1)}, f32[768]{0:T(1024)}, u32[]{:S(2)}) copy-start(f32[768]{0:T(1024)} %param.19) | copy-start | bytes 9220
  7.2 51.5 %all-gather.2.cloned.1.call-start = ((), (), s32[]{:S(2)}) async-start(), calls=%async_computation.5 | async-start | bytes 2875392 | tf_op jit(solution)/shard_map/all_gather | solution.py:500
  10.6 113.8 %reduce-scatter.2.cloned.1.call-start = ((), (), s32[]{:S(2)}) async-start(), calls=%async_computation.6 | async-start | bytes 2949120 | tf_op jit(solution)/shard_map/reduce_scatter | solution.py:515
  14.3 44.5 %copy-start = (bf16[14,16,768]{2,1,0:T(8,128)(2,1)}, bf16[14,16,768]{2,1,0:T(8,128)(2,1)S(1)}, u32[]{:S(2)}) copy-start(bf16[14,16,768]{2,1,0:T(8,128)(2,1)S(1)} %pad.4) | copy-start | bytes 1032196
  14.3 20.2 %collective-permute-start.5 = (bf16[224,768]{1,0:T(8,128)(2,1)S(1)}, bf16[224,768]{1,0:T(8,128)(2,1)S(1)}, u32[]{:S(2)}, u32[]{:S(2)}) collective-permute-start(bf16[224,768]{1,0:T(8,128)(2,1)S(1)} %bitcast.24), channel_id=1, source_target_pairs={{0,40},{8,0},{32,8},{40,32},{1,41},{9,1},{33,9},{41,33},{2,42},{10... | collective-permute-start | bytes 1032200 | tf_op jit(solution)/shard_map/ppermute | solution.py:485
  19.5 17.7 %collective-permute-start.4 = (bf16[224,768]{1,0:T(8,128)(2,1)S(1)}, bf16[224,768]{1,0:T(8,128)(2,1)S(1)}, u32[]{:S(2)}, u32[]{:S(2)}) collective-permute-start(bf16[224,768]{1,0:T(8,128)(2,1)S(1)} %bitcast.25), channel_id=1, source_target_pairs={{0,32},{8,40},{32,0},{40,8},{1,33},{9,41},{33,1},{41,9},{2,34},{10... | collective-permute-start | bytes 1032200 | tf_op jit(solution)/shard_map/ppermute | solution.py:485
  22.0 17.3 %collective-permute-start.3 = (bf16[224,768]{1,0:T(8,128)(2,1)S(1)}, bf16[224,768]{1,0:T(8,128)(2,1)S(1)}, u32[]{:S(2)}, u32[]{:S(2)}) collective-permute-start(bf16[224,768]{1,0:T(8,128)(2,1)S(1)} %bitcast.26), channel_id=1, source_target_pairs={{0,8},{8,32},{32,40},{40,0},{1,9},{9,33},{33,41},{41,1},{2,10},{10... | collective-permute-start | bytes 1032200 | tf_op jit(solution)/shard_map/ppermute | solution.py:485
  27.4 13.0 %collective-permute-start.2 = (bf16[224,768]{1,0:T(8,128)(2,1)S(1)}, bf16[224,768]{1,0:T(8,128)(2,1)S(1)}, u32[]{:S(2)}, u32[]{:S(2)}) collective-permute-start(bf16[224,768]{1,0:T(8,128)(2,1)S(1)} %get-tuple-element.27.refs_0_), channel_id=1, source_target_pairs={{0,40},{8,0},{32,8},{40,32},{1,41},{9,1},{33,9},{41,33},{2,42},{10... | collective-permute-start | bytes 1032200 | tf_op jit(solution)/shard_map/ppermute | solution.py:485
  31.4 13.5 %collective-permute-start.1 = (bf16[224,768]{1,0:T(8,128)(2,1)S(1)}, bf16[224,768]{1,0:T(8,128)(2,1)S(1)}, u32[]{:S(2)}, u32[]{:S(2)}) collective-permute-start(bf16[224,768]{1,0:T(8,128)(2,1)S(1)} %get-tuple-element.27.refs_0_), channel_id=1, source_target_pairs={{0,32},{8,40},{32,0},{40,8},{1,33},{9,41},{33,1},{41,9},{2,34},{10... | collective-permute-start | bytes 1032200 | tf_op jit(solution)/shard_map/ppermute | solution.py:485
  34.6 0.7 copy-start.5
  35.3 18.9 %collective-permute-start = (bf16[224,768]{1,0:T(8,128)(2,1)S(1)}, bf16[224,768]{1,0:T(8,128)(2,1)}, u32[]{:S(2)}, u32[]{:S(2)}) collective-permute-start(bf16[224,768]{1,0:T(8,128)(2,1)S(1)} %get-tuple-element.27.refs_0_), channel_id=1, source_target_pairs={{0,8},{8,32},{32,40},{40,0},{1,9},{9,33},{33,41},{41,1},{2,10},{10... | collective-permute-start | bytes 1032200 | tf_op jit(solution)/shard_map/ppermute | solution.py:485
  37.3 21.5 %copy-start.6 = (bf16[224,768]{1,0:T(8,128)(2,1)}, bf16[224,768]{1,0:T(8,128)(2,1)S(1)}, u32[]{:S(2)}) copy-start(bf16[224,768]{1,0:T(8,128)(2,1)S(1)} %collective-permute-done.4.refs_6_) | copy-start | bytes 1032196
  39.3 19.5 %copy-start.7 = (bf16[224,768]{1,0:T(8,128)(2,1)}, bf16[224,768]{1,0:T(8,128)(2,1)S(1)}, u32[]{:S(2)}) copy-start(bf16[224,768]{1,0:T(8,128)(2,1)S(1)} %collective-permute-done.3.refs_5_) | copy-start | bytes 1032196
  40.4 4.6 %copy-start.8 = (bf16[224,768]{1,0:T(8,128)(2,1)}, bf16[224,768]{1,0:T(8,128)(2,1)S(1)}, u32[]{:S(2)}) copy-start(bf16[224,768]{1,0:T(8,128)(2,1)S(1)} %collective-permute-done.2.refs_3_) | copy-start | bytes 1032196
  44.9 0.7 copy-start.9
  70.0 0.7 copy-start.3
  70.8 1.0 copy-start.4
  71.8 9.6 %collective-permute-start.7 = (bf16[224,768]{1,0:T(8,128)(2,1)S(1)}, bf16[224,768]{1,0:T(8,128)(2,1)S(1)}, u32[]{:S(2)}, u32[]{:S(2)}) collective-permute-start(bf16[224,768]{1,0:T(8,128)(2,1)S(1)} %copy-done.4), channel_id=1, source_target_pairs={{0,40},{8,0},{32,8},{40,32},{1,41},{9,1},{33,9},{41,33},{2,42},{10... | collective-permute-start | bytes 1032200 | tf_op jit(solution)/shard_map/ppermute | solution.py:485
  76.0 9.6 %collective-permute-start.8 = (bf16[224,768]{1,0:T(8,128)(2,1)S(1)}, bf16[224,768]{1,0:T(8,128)(2,1)S(1)}, u32[]{:S(2)}, u32[]{:S(2)}) collective-permute-start(bf16[224,768]{1,0:T(8,128)(2,1)S(1)} %get-tuple-element.31), channel_id=1, source_target_pairs={{0,32},{8,40},{32,0},{40,8},{1,33},{9,41},{33,1},{41,9},{2,34},{10... | collective-permute-start | bytes 1032200 | tf_op jit(solution)/shard_map/ppermute | solution.py:485
  78.5 16.3 %collective-permute-start.9 = (bf16[224,768]{1,0:T(8,128)(2,1)S(1)}, bf16[224,768]{1,0:T(8,128)(2,1)S(1)}, u32[]{:S(2)}, u32[]{:S(2)}) collective-permute-start(bf16[224,768]{1,0:T(8,128)(2,1)S(1)} %get-tuple-element.32), channel_id=1, source_target_pairs={{0,8},{8,32},{32,40},{40,0},{1,9},{9,33},{33,41},{41,1},{2,10},{10... | collective-permute-start | bytes 1032200 | tf_op jit(solution)/shard_map/ppermute | solution.py:485
  99.6 11.9 %all-to-all-start = ((f32[8,48,128]{2,1,0:T(8,128)}), f32[8,48,128]{2,1,0:T(8,128)S(1)}, u32[]{:S(2)}, u32[]{:S(2)}) async-start(f32[8,48,128]{2,1,0:T(8,128)} %bitcast.15), calls=%async_computation.1 | async-start | bytes 393216 | tf_op jit(solution)/shard_map/all_to_all | solution.py:520
  112.2 12.0 %all-to-all-start.1 = ((bf16[8,48,128]{2,1,0:T(8,128)(2,1)}), bf16[8,48,128]{2,1,0:T(8,128)(2,1)S(1)}, u32[]{:S(2)}, u32[]{:S(2)}) async-start(bf16[8,48,128]{2,1,0:T(8,128)(2,1)} %broadcast_in_dim.14), calls=%async_computation.2 | async-start | bytes 196608 | tf_op jit(solution)/shard_map/all_to_all | solution.py:462
  124.3 47.5 %copy-start.1 = (bf16[14,16,768]{2,1,0:T(8,128)(2,1)S(1)}, bf16[14,16,768]{2,1,0:T(8,128)(2,1)}, u32[]{:S(2)}) copy-start(bf16[14,16,768]{2,1,0:T(8,128)(2,1)} %copy-done) | copy-start | bytes 1032196
  125.5 4.4 %collective-permute-start.6 = (bf16[8,80,128]{2,1,0:T(8,128)(2,1)S(1)}, bf16[8,80,128]{2,1,0:T(8,128)(2,1)S(1)}, u32[]{:S(2)}, u32[]{:S(2)}) collective-permute-start(bf16[8,80,128]{2,1,0:T(8,128)(2,1)S(1)} %bitcast.36), channel_id=1, source_target_pairs={{0,16},{16,0},{1,17},{17,1},{2,18},{18,2},{3,19},{19,3},{4,20},{20... | collective-permute-start | bytes 491528 | tf_op jit(solution)/shard_map/ppermute | solution.py:466
  148.3 15.8 %all-to-all-start.3 = ((bf16[16,80,128]{2,1,0:T(8,128)(2,1)}), bf16[16,80,128]{2,1,0:T(8,128)(2,1)S(1)}, u32[]{:S(2)}, u32[]{:S(2)}) async-start(bf16[16,80,128]{2,1,0:T(8,128)(2,1)} %broadcast_in_dim.16), calls=%async_computation.4 | async-start | bytes 655360 | tf_op jit(solution)/shard_map/all_to_all | solution.py:462
  152.0 6.5 %collective-permute-start.10 = (f32[48,128]{1,0:T(8,128)S(1)}, f32[48,128]{1,0:T(8,128)S(1)}, u32[]{:S(2)}, u32[]{:S(2)}) collective-permute-start(f32[48,128]{1,0:T(8,128)S(1)} %add_select_fusion), channel_id=1, source_target_pairs={{0,32},{32,0},{1,33},{33,1},{2,34},{34,2},{3,35},{35,3},{4,36},{36... | collective-permute-start | bytes 73736 | tf_op jit(solution)/shard_map/ppermute | solution.py:466
  158.5 5.1 %collective-permute-start.11 = (f32[96,128]{1,0:T(8,128)S(1)}, f32[96,128]{1,0:T(8,128)S(1)}, u32[]{:S(2)}, u32[]{:S(2)}) collective-permute-start(f32[96,128]{1,0:T(8,128)S(1)} %pad_maximum_fusion.2), channel_id=1, source_target_pairs={{0,8},{8,0},{1,9},{9,1},{2,10},{10,2},{3,11},{11,3},{4,12},{12,4},... | collective-permute-start | bytes 147464 | tf_op jit(solution)/shard_map/ppermute | solution.py:466
  164.2 10.2 %collective-permute-start.13 = (bf16[8,2,80,128]{3,2,1,0:T(8,128)(2,1)S(1)}, bf16[8,2,80,128]{3,2,1,0:T(8,128)(2,1)S(1)}, u32[]{:S(2)}, u32[]{:S(2)}) collective-permute-start(bf16[8,2,80,128]{3,2,1,0:T(8,128)(2,1)S(1)} %bitcast.31), channel_id=1, source_target_pairs={{0,16},{16,0},{1,17},{17,1},{2,18},{18,2},{3,19},{19,3},{4,20},{20... | collective-permute-start | bytes 983048 | tf_op jit(solution)/shard_map/ppermute | solution.py:466
  169.8 4.6 %collective-permute-start.12 = (f32[192,128]{1,0:T(8,128)S(1)}, f32[192,128]{1,0:T(8,128)S(1)}, u32[]{:S(2)}, u32[]{:S(2)}) collective-permute-start(f32[192,128]{1,0:T(8,128)S(1)} %pad_maximum_fusion.1.small_in), channel_id=1, source_target_pairs={{0,16},{16,0},{1,17},{17,1},{2,18},{18,2},{3,19},{19,3},{4,20},{20... | collective-permute-start | bytes 294920 | tf_op jit(solution)/shard_map/ppermute | solution.py:466
Sparse Core Ops, SparseCore 0:
  10.7 47.9 all-gather.1
  70.9 45.0 reduce-scatter.1

commit v6 on v5

--- a/solution.py
+++ b/solution.py
@@ -19,7 +19,7 @@
 BLOCKS = CH // LANES
 OWN = 48
 UNITS = 2 * OWN
-PACK = 2 * UNITS + 16
+PACK = UNITS + 16
 REPLICA = ("y", "xh", "core")
 SHARD = ("xl", "z")
 RING = ("xh", "xl")
@@ -61,32 +61,31 @@
         copy.wait()
     q = place_ref[0]
     column = place_ref[1]
-    partner = q + 1 - 2 * lax.rem(q, 2)
-    row = lax.broadcasted_iota(jnp.int32, (UNITS, 192), 0)
-    lane = lax.broadcasted_iota(jnp.int32, (UNITS, 192), 1)
-    wanted = jnp.where(row < OWN, row + q * OWN, row - OWN + partner * OWN)
-    pick = (lane == wanted).astype(BF16)
-    out_ref[0:UNITS, :] = jnp.dot(pick, first_ref[...], preferred_element_type=F32).astype(BF16)
-    out_ref[UNITS : 2 * UNITS, :] = jnp.dot(pick, second_ref[...], preferred_element_type=F32).astype(BF16)
-    unit = lax.broadcasted_iota(jnp.int32, (192, CH), 0)
-    spot = lax.broadcasted_iota(jnp.int32, (192, CH), 1) - column * UNITS
-    wanted = jnp.where(spot < OWN, spot + q * OWN, spot - OWN + partner * OWN)
-    put = ((unit == wanted) & (spot >= 0) & (spot < UNITS)).astype(BF16)
-    bias = jnp.broadcast_to(bias_ref[...], (16, 192))
-    high = bias.astype(BF16)
-    low = (bias - high.astype(F32)).astype(BF16)
-    bias_row = lax.broadcasted_iota(jnp.int32, (16, 192), 0)
-    both = jnp.where(bias_row == 0, high.astype(F32), low.astype(F32)).astype(BF16)
-    out_ref[2 * UNITS : PACK, :] = jnp.dot(both, put, preferred_element_type=F32).astype(BF16)
+    for k in range(2):
+        at = q + k * (1 - 2 * lax.rem(q, 2))
+        row = lax.broadcasted_iota(jnp.int32, (OWN, 192), 0)
+        lane = lax.broadcasted_iota(jnp.int32, (OWN, 192), 1)
+        pick = (lane == row + at * OWN).astype(BF16)
+        out_ref[k, 0:OWN, :] = jnp.dot(pick, first_ref[...], preferred_element_type=F32).astype(BF16)
+        out_ref[k, OWN:UNITS, :] = jnp.dot(pick, second_ref[...], preferred_element_type=F32).astype(BF16)
+        unit = lax.broadcasted_iota(jnp.int32, (192, CH), 0)
+        spot = lax.broadcasted_iota(jnp.int32, (192, CH), 1) - column * UNITS
+        put = ((unit == spot + at * OWN) & (spot >= 0) & (spot < OWN)).astype(BF16)
+        bias = jnp.broadcast_to(bias_ref[...], (16, 192))
+        high = bias.astype(BF16)
+        low = (bias - high.astype(F32)).astype(BF16)
+        bias_row = lax.broadcasted_iota(jnp.int32, (16, 192), 0)
+        both = jnp.where(bias_row == 0, high.astype(F32), low.astype(F32)).astype(BF16)
+        out_ref[k, UNITS:PACK, :] = jnp.dot(both, put, preferred_element_type=F32).astype(BF16)
 
 
 def pack_weights(place, first_weight, first_bias, second_weight):
     return pl.pallas_call(
         pack_kernel,
         grid=(1,),
-        out_shape=jax.ShapeDtypeStruct((PACK, CH), BF16),
+        out_shape=jax.ShapeDtypeStruct((2, PACK, CH), BF16),
         in_specs=[scalars()] + [pl.BlockSpec(memory_space=pl.ANY)] * 3,
-        out_specs=block(PACK, CH),
+        out_specs=block(2, PACK, CH),
         scratch_shapes=[
             pltpu.VMEM((192, CH), BF16),
             pltpu.VMEM((1, 192), F32),
@@ -182,37 +181,65 @@
     normed_in = refs[0:4]
     scaled_in = refs[4:8]
     pack_in, layer_ref = refs[8:10]
-    parts = refs[10:14]
-    out_ref, scale_ref = refs[14:16]
-    normed, scaled, pack, act, grad, sems = refs[16:22]
-    copies = [pltpu.make_async_copy(pack_in, pack, sems.at[8])]
+    part_outs = refs[10:14]
+    grads_out, scale_ref = refs[14:16]
+    normed, scaled, firsts, seconds, biases, act, grad, parts, out_ref, sems, out_sems = refs[16:27]
+    first_copies, second_copies, normed_copies, scaled_copies, sends = [], [], [], [], []
+    for k in range(2):
+        whole_z = pl.ds(0, 8)
+        first_copies.append(
+            pltpu.make_async_copy(pack_in.at[whole_z, k, pl.ds(0, OWN)], firsts.at[whole_z, k], sems.at[k])
+        )
+        first_copies.append(
+            pltpu.make_async_copy(pack_in.at[whole_z, k, pl.ds(UNITS, 16)], biases.at[k], sems.at[2 + k])
+        )
+        second_copies.append(
+            pltpu.make_async_copy(pack_in.at[whole_z, k, pl.ds(OWN, OWN)], seconds.at[whole_z, k], sems.at[4 + k])
+        )
     for i in range(4):
         rows = pl.ds(i * PIX, PIX)
-        copies.append(pltpu.make_async_copy(normed_in[i], normed.at[rows], sems.at[i]))
-        copies.append(pltpu.make_async_copy(scaled_in[i], scaled.at[rows], sems.at[4 + i]))
-    for copy in copies:
+        normed_copies.append(pltpu.make_async_copy(normed_in[i], normed.at[rows], sems.at[6 + i]))
+        scaled_copies.append(pltpu.make_async_copy(scaled_in[i], scaled.at[rows], sems.at[10 + i]))
+    for copy in [*first_copies, *normed_copies, *second_copies, *scaled_copies]:
         copy.start()
-    copies[0].wait()
-    first = pack[:, 0:UNITS, :].reshape(CH, CH)
-    second = pack[:, UNITS : 2 * UNITS, :].reshape(CH, CH)
-    bias = jnp.sum(pack[:, 2 * UNITS : PACK, :].astype(F32), axis=0)
-    bias = bias[0:1, :] + bias[1:2, :]
+    for copy in first_copies:
+        copy.wait()
+    first = firsts[...].reshape(CH, CH)
+    halves = []
+    for k in range(2):
+        rows = jnp.sum(biases[k].astype(F32), axis=0)
+        halves.append(jnp.broadcast_to(rows[0:1, :] + rows[1:2, :], (8, CH)))
+    bias = (halves[0] + pltpu.roll(halves[1], OWN, 1))[0:1, :]
     layer = layer_ref[...]
     for i in range(4):
         rows = slice(i * PIX, (i + 1) * PIX)
-        copies[1 + 2 * i].wait()
-        copies[2 + 2 * i].wait()
+        normed_copies[i].wait()
         preact = nt(normed[rows, :], first) + bias
         cumulative = 0.5 * (1.0 + lax.erf(preact * 0.7071067811865476))
         slope = cumulative + preact * jnp.exp(-0.5 * preact * preact) * 0.3989422804014327
         act[rows, :] = (preact * cumulative).astype(BF16)
+        if i == 0:
+            for copy in second_copies:
+                copy.wait()
+            second = seconds[...].reshape(CH, CH)
+        scaled_copies[i].wait()
         branch_grad = (scaled[rows, :].astype(F32) * layer).astype(BF16)
         preact_grad = (nt(branch_grad, second) * slope).astype(BF16)
         grad[rows, :] = preact_grad
-        parts[i][...] = jnp.dot(preact_grad, first, preferred_element_type=F32).astype(BF16)
+        parts[rows, :] = jnp.dot(preact_grad, first, preferred_element_type=F32).astype(BF16)
+        sends.append(pltpu.make_async_copy(parts.at[pl.ds(i * PIX, PIX)], part_outs[i], out_sems.at[i]))
+        sends[-1].start()
     product = tn(act[...], scaled[...])
     scale_ref[...] = jnp.sum((second.astype(F32) * product).reshape(CH // 8, 8, CH), axis=0)
     spread(out_ref, (product * layer).astype(BF16), 0)
+    for half in range(2):
+        rows = pl.ds(half * 640, 288)
+        sends.append(
+            pltpu.make_async_copy(
+                out_ref.at[pl.ds(0, 8), rows], grads_out.at[pl.ds(0, 8), rows], out_sems.at[4 + half]
+            )
+        )
+        sends[-1].start()
     spread(out_ref, tn(grad[...], normed[...]).astype(BF16), 18)
     bias = jnp.dot(jnp.ones((16, 4 * PIX), BF16), grad[...], preferred_element_type=F32)
     row = lax.broadcasted_iota(jnp.int32, (16, LANES), 0)
@@ -227,6 +254,15 @@
         for z in range(8):
             for s in range(36, 40):
                 out_ref[z, half * 640 + s * 16 : half * 640 + s * 16 + 16, :] = rows if s == 36 else empty
+        span = pl.ds(half * 640 + 288, 352)
+        sends.append(
+            pltpu.make_async_copy(
+                out_ref.at[pl.ds(0, 8), span], grads_out.at[pl.ds(0, 8), span], out_sems.at[6 + half]
+            )
+        )
+        sends[-1].start()
+    for send in sends:
+        send.wait()
 
 
 def spread(out_ref, matrix, start):
@@ -242,21 +278,27 @@
 
 
 def hidden(normed, scaled, pack, layer):
+    free = pl.BlockSpec(memory_space=pl.ANY)
     return pl.pallas_call(
         hidden_kernel,
         grid=(1,),
         out_shape=(jax.ShapeDtypeStruct((PIX, CH), BF16),) * 4
         + (jax.ShapeDtypeStruct((8, 1280, LANES), BF16),)
         + (jax.ShapeDtypeStruct((8, CH), F32),),
-        in_specs=[pl.BlockSpec(memory_space=pl.ANY)] * 9 + [block(1, CH)],
-        out_specs=(block(PIX, CH),) * 4 + (block(8, 1280, LANES),) + (block(8, CH),),
+        in_specs=[free] * 9 + [block(1, CH)],
+        out_specs=(free,) * 5 + (block(8, CH),),
         scratch_shapes=[
             pltpu.VMEM((4 * PIX, CH), BF16),
             pltpu.VMEM((4 * PIX, CH), BF16),
-            pltpu.VMEM((8, PACK, CH), BF16),
+            pltpu.VMEM((8, 2, OWN, CH), BF16),
+            pltpu.VMEM((8, 2, OWN, CH), BF16),
+            pltpu.VMEM((2, 8, 16, CH), BF16),
             pltpu.VMEM((4 * PIX, CH), BF16),
             pltpu.VMEM((4 * PIX, CH), BF16),
-            pltpu.SemaphoreType.DMA((9,)),
+            pltpu.VMEM((4 * PIX, CH), BF16),
+            pltpu.VMEM((8, 1280, LANES), BF16),
+            pltpu.SemaphoreType.DMA((14,)),
+            pltpu.SemaphoreType.DMA((8,)),
         ],
         compiler_params=params(HIDDEN_MIB),
         interpret=INTERPRET,
@@ -497,7 +539,7 @@
     column = lax.axis_index("z")
     place = jnp.stack([half * 2 + core, column]).astype(jnp.int32)
     packed = pack_weights(place, first_weight, first_bias, second_weight)
-    packed = lax.all_gather(packed, "z", axis=0, tiled=True).reshape(8, PACK, CH)
+    packed = lax.all_gather(packed, "z", axis=0, tiled=True).reshape(8, 2, PACK, CH)
 
     kernel = conv_kernel.reshape(49, CH)
     gain = norm_gain.reshape(1, CH)
@@ -526,8 +568,8 @@
     small = join(jnp.sum(both[:, 80:128, :], axis=0), holds)
     small = jnp.concatenate([small, swap("xh", small)], axis=0)
     small = jnp.concatenate([small, swap("xl", small)], axis=0)
-    small, mine = lax.optimization_barrier((small, mine))
     pre = input_grad(conv_grad, kernel, scaled)
+    small, mine, pre = lax.optimization_barrier((small, mine, pre))
     images = float(lax.axis_size(REPLICA) * lax.axis_size(SHARD))
     grad_image, grad_first, grad_second, grad_bias, grad_kernel, grad_gain, grad_scale = finish(
         images,

time: 184 us -> 184 us (level)
    unnamed x26 -> x20, local copies, waits for them, and re-layouts: 3.19 us -> 0.77 us
  transfers between devices with their start and end apart: 19 -> 19, of which waited for: 14 -> 15; matrix products, arithmetic and copies ran while one was open for 2% -> 3% of each run, Pallas kernels for 6% -> 6%
where the time goes in v6:
time: 184 us; the launch traced here: 183 us
  starting transfers between devices  58.7 us (32%)
  waiting for transfers between devices  55.6 us (30%)
  Pallas kernels  27.7 us (15%)
  blocking collectives  17.4 us (9%)
  between operations  15.1 us (8%)
  other arithmetic  4.13 us (2%)
  local copies, waits for them, and re-layouts  4.02 us (2%)
    ppermute x9, waiting for transfers between devices, ring(): return lax.ppermute(value, RING, [(i, (i + shift) % 4) for i in range(4)])  30.4 us
    ppermute x9, starting transfers between devices, ring(): return lax.ppermute(value, RING, [(i, (i + shift) % 4) for i in range(4)])  28.4 us
    ppermute x5, starting transfers between devices, swap(): return lax.ppermute(value, axis, [(0, 1), (1, 0)])  17.5 us
    all_to_all x1, blocking collectives, per_device(): lax.all_to_all(jnp.concatenate([grads, both], axis=1), 'y', 0, 0, tiled=T...  17.4 us
    pallas_call x1, Pallas kernels, hidden(): pl.pallas_call(hidden_kernel, grid=(1,), out_shape=(jax.ShapeDtypeStruct(...  12.7 us
    all_to_all x2, waiting for transfers between devices, to_all(): lax.all_to_all(jnp.broadcast_to(value, (count, *value.shape)), axes, 0, 0...  8.3 us
    all_to_all x2, starting transfers between devices, to_all(): lax.all_to_all(jnp.broadcast_to(value, (count, *value.shape)), axes, 0, 0...  7.58 us
    all_to_all x1, waiting for transfers between devices, per_device(): small = lax.all_to_all(small.reshape(8, OWN, LANES), TEAM, 0, 0, tiled=True)  6.25 us
  transfers between devices with their start and end apart: 19, of which 15 were waited for; matrix products, arithmetic and copies ran while one was open for 3% of the time, Pallas kernels for 6%

profile of v6, /device:TPU:1, one launch (start us, length us, event | category | flops | bytes accessed | tf_op | source)
XLA Modules:
  0.0 182.7 jit_solution(18356509633572549521)
XLA Ops:
  7.2 0.0 all-gather.2.cloned.1.call-start
  7.3 0.6 pad_add_fusion.1.place_ref
  7.8 2.9 %pack.1 = bf16[2,112,768]{2,1,0:T(8,128)(2,1)} custom-call(s32[2]{0:T(128)} %pad_add_fusion.1.place_ref, bf16[192,768]{1,0:T(8,128)(2,1)} %bitcast.35, f32[1,192]{1,0:T(1,128)} %bitcast.39, bf16[192,768]{1,0:T(8,128)(2,1)} %second_in.1), custom_call_target="tpu_custom_call" | custom-call | tf_op jit(solution)/shard_map/pack/pallas_call | solution.py:83
  10.7 0.0 all-gather.2.cloned.1.call-update
  10.7 0.0 reduce-scatter.2.cloned.1.call-start
  11.4 1.3 fusion.4
  12.7 1.7 fusion
  14.4 0.0 copy-start
  14.4 5.2 %collective-permute-start.5 = (bf16[224,768]{1,0:T(8,128)(2,1)S(1)}, bf16[224,768]{1,0:T(8,128)(2,1)S(1)}, u32[]{:S(2)}, u32[]{:S(2)}) collective-permute-start(bf16[224,768]{1,0:T(8,128)(2,1)S(1)} %bitcast.24), channel_id=1, source_target_pairs={{0,40},{8,0},{32,8},{40,32},{1,41},{9,1},{33,9},{41,33},{2,42},{10... | collective-permute-start | bytes 1032200 | tf_op jit(solution)/shard_map/ppermute | solution.py:527
  19.7 2.4 %collective-permute-start.4 = (bf16[224,768]{1,0:T(8,128)(2,1)S(1)}, bf16[224,768]{1,0:T(8,128)(2,1)S(1)}, u32[]{:S(2)}, u32[]{:S(2)}) collective-permute-start(bf16[224,768]{1,0:T(8,128)(2,1)S(1)} %bitcast.25), channel_id=1, source_target_pairs={{0,32},{8,40},{32,0},{40,8},{1,33},{9,41},{33,1},{41,9},{2,34},{10... | collective-permute-start | bytes 1032200 | tf_op jit(solution)/shard_map/ppermute | solution.py:527
  22.1 2.5 %collective-permute-start.3 = (bf16[224,768]{1,0:T(8,128)(2,1)S(1)}, bf16[224,768]{1,0:T(8,128)(2,1)S(1)}, u32[]{:S(2)}, u32[]{:S(2)}) collective-permute-start(bf16[224,768]{1,0:T(8,128)(2,1)S(1)} %bitcast.26), channel_id=1, source_target_pairs={{0,8},{8,32},{32,40},{40,0},{1,9},{9,33},{33,41},{41,1},{2,10},{10... | collective-permute-start | bytes 1032200 | tf_op jit(solution)/shard_map/ppermute | solution.py:527
  24.6 0.7 reshape.56.gain_ref
  25.4 2.8 %conv_norm.1 = (bf16[224,768]{1,0:T(8,128)(2,1)S(1)}, f32[6,14,16,128]{3,2,1,0:T(8,128)S(1)}, f32[14,16,128]{2,1,0:T(8,128)S(1)}) custom-call(bf16[14,14,768]{2,1,0:T(8,128)(2,1)S(1)} %bitcast.29, bf16[49,768]{1,0:T(8,128)(2,1)S(1)} %reshape.55.kernel_ref, f32[1,768]{1,0:T(1,128)S(1)} %reshape.56.gain_ref), custom_call_target="tpu_custom_call" | custom-call | tf_op jit(solution)/shard_map/conv_norm/pallas_call | solution.py:152
  28.2 4.0 %collective-permute-start.2 = (bf16[224,768]{1,0:T(8,128)(2,1)S(1)}, bf16[224,768]{1,0:T(8,128)(2,1)S(1)}, u32[]{:S(2)}, u32[]{:S(2)}) collective-permute-start(bf16[224,768]{1,0:T(8,128)(2,1)S(1)} %get-tuple-element.28.refs_0_), channel_id=1, source_target_pairs={{0,40},{8,0},{32,8},{40,32},{1,41},{9,1},{33,9},{41,33},{2,42},{10... | collective-permute-start | bytes 1032200 | tf_op jit(solution)/shard_map/ppermute | solution.py:527
  32.2 3.1 %collective-permute-start.1 = (bf16[224,768]{1,0:T(8,128)(2,1)S(1)}, bf16[224,768]{1,0:T(8,128)(2,1)S(1)}, u32[]{:S(2)}, u32[]{:S(2)}) collective-permute-start(bf16[224,768]{1,0:T(8,128)(2,1)S(1)} %get-tuple-element.28.refs_0_), channel_id=1, source_target_pairs={{0,32},{8,40},{32,0},{40,8},{1,33},{9,41},{33,1},{41,9},{2,34},{10... | collective-permute-start | bytes 1032200 | tf_op jit(solution)/shard_map/ppermute | solution.py:527
  35.3 0.0 collective-permute-done.5.refs_7_
  35.4 1.9 %collective-permute-start = (bf16[224,768]{1,0:T(8,128)(2,1)S(1)}, bf16[224,768]{1,0:T(8,128)(2,1)}, u32[]{:S(2)}, u32[]{:S(2)}) collective-permute-start(bf16[224,768]{1,0:T(8,128)(2,1)S(1)} %get-tuple-element.28.refs_0_), channel_id=1, source_target_pairs={{0,8},{8,32},{32,40},{40,0},{1,9},{9,33},{33,41},{41,1},{2,10},{10... | collective-permute-start | bytes 1032200 | tf_op jit(solution)/shard_map/ppermute | solution.py:527
  37.3 0.0 copy-done.9
  37.3 0.0 collective-permute-done.4.refs_6_
  37.3 1.4 collective-permute-done.3.refs_5_
  38.8 1.0 collective-permute-done.2.refs_3_
  39.8 4.8 %collective-permute-done.1.refs_2_ = bf16[224,768]{1,0:T(8,128)(2,1)S(1)} collective-permute-done((bf16[224,768]{1,0:T(8,128)(2,1)S(1)}, bf16[224,768]{1,0:T(8,128)(2,1)S(1)}, u32[]{:S(2)}, u32[]{:S(2)}) %collective-permute-start.1) | collective-permute-done | bytes 344096 | tf_op jit(solution)/shard_map/ppermute | solution.py:527
  44.6 0.7 copy-done.7
  45.3 8.7 %collective-permute-done.refs_1_ = bf16[224,768]{1,0:T(8,128)(2,1)} collective-permute-done((bf16[224,768]{1,0:T(8,128)(2,1)S(1)}, bf16[224,768]{1,0:T(8,128)(2,1)}, u32[]{:S(2)}, u32[]{:S(2)}) %collective-permute-start) | collective-permute-done | bytes 344096 | tf_op jit(solution)/shard_map/ppermute | solution.py:527
  54.1 6.1 %all-gather.2.cloned.1.call-done = bf16[16,112,768]{2,1,0:T(8,128)(2,1)} async-done(((bf16[2,112,768]{2,1,0:T(8,128)(2,1)}), bf16[16,112,768]{2,1,0:T(8,128)(2,1)}) %all-gather.2.cloned.1.call-update) | async-done | bytes 2752528 | tf_op jit(solution)/shard_map/all_gather | solution.py:542
  60.2 0.0 copy-done.3
  60.2 0.0 copy-done.5
  60.2 12.7 %hidden.1 = (bf16[224,768]{1,0:T(8,128)(2,1)S(1)}, bf16[224,768]{1,0:T(8,128)(2,1)S(1)}, bf16[224,768]{1,0:T(8,128)(2,1)S(1)}, bf16[224,768]{1,0:T(8,128)(2,1)S(...) custom-call(bf16[224,768]{1,0:T(8,128)(2,1)S(1)} %get-tuple-element.28.refs_0_, ...), custom_call_target="tpu_custom_call" | custom-call | tf_op jit(solution)/shard_map/hidden/pallas_call | solution.py:282
  73.0 0.0 reduce-scatter.2.cloned.1.call-update
  73.0 4.2 %collective-permute-start.7 = (bf16[224,768]{1,0:T(8,128)(2,1)S(1)}, bf16[224,768]{1,0:T(8,128)(2,1)S(1)}, u32[]{:S(2)}, u32[]{:S(2)}) collective-permute-start(bf16[224,768]{1,0:T(8,128)(2,1)S(1)} %get-tuple-element.31), channel_id=1, source_target_pairs={{0,40},{8,0},{32,8},{40,32},{1,41},{9,1},{33,9},{41,33},{2,42},{10... | collective-permute-start | bytes 1032200 | tf_op jit(solution)/shard_map/ppermute | solution.py:527
  77.2 2.2 %collective-permute-start.8 = (bf16[224,768]{1,0:T(8,128)(2,1)S(1)}, bf16[224,768]{1,0:T(8,128)(2,1)S(1)}, u32[]{:S(2)}, u32[]{:S(2)}) collective-permute-start(bf16[224,768]{1,0:T(8,128)(2,1)S(1)} %get-tuple-element.32), channel_id=1, source_target_pairs={{0,32},{8,40},{32,0},{40,8},{1,33},{9,41},{33,1},{41,9},{2,34},{10... | collective-permute-start | bytes 1032200 | tf_op jit(solution)/shard_map/ppermute | solution.py:527
  79.5 2.7 %collective-permute-start.9 = (bf16[224,768]{1,0:T(8,128)(2,1)S(1)}, bf16[224,768]{1,0:T(8,128)(2,1)S(1)}, u32[]{:S(2)}, u32[]{:S(2)}) collective-permute-start(bf16[224,768]{1,0:T(8,128)(2,1)S(1)} %get-tuple-element.33), channel_id=1, source_target_pairs={{0,8},{8,32},{32,40},{40,0},{1,9},{9,33},{33,41},{41,1},{2,10},{10... | collective-permute-start | bytes 1032200 | tf_op jit(solution)/shard_map/ppermute | solution.py:527
  82.2 0.4 collective-permute-done.7.one_ref
  82.6 4.2 %collective-permute-done.8.two_ref = bf16[224,768]{1,0:T(8,128)(2,1)S(1)} collective-permute-done((bf16[224,768]{1,0:T(8,128)(2,1)S(1)}, bf16[224,768]{1,0:T(8,128)(2,1)S(1)}, u32[]{:S(2)}, u32[]{:S(2)}) %collective-permute-start.8) | collective-permute-done | bytes 344096 | tf_op jit(solution)/shard_map/ppermute | solution.py:527
  86.8 9.8 %collective-permute-done.9.three_ref = bf16[224,768]{1,0:T(8,128)(2,1)S(1)} collective-permute-done((bf16[224,768]{1,0:T(8,128)(2,1)S(1)}, bf16[224,768]{1,0:T(8,128)(2,1)S(1)}, u32[]{:S(2)}, u32[]{:S(2)}) %collective-permute-start.9) | collective-permute-done | bytes 344096 | tf_op jit(solution)/shard_map/ppermute | solution.py:527
  96.6 4.8 %norm_back.1 = (f32[6,64,128]{2,1,0:T(8,128)}, f32[6,14,16,128]{3,2,1,0:T(8,128)S(1)}) custom-call(f32[1]{0:T(128)} %bitcast.14.weight_ref, bf16[224,768]{1,0:T(8,128)(2,1)S(1)} %get-tuple-element.30.zero_ref, bf16[224,768]{1,0:T(8,128)(2,1)S(1)} %collective-permute-done.7.one_ref, bf16[224,768]{1,0:T(8,128)(2,1)S(1)} %collective-permute-done.8.two_ref, ...), custom_call_target="tpu_custom_call" | custom-call | tf_op jit(solution)/shard_map/norm_back/pallas_call | solution.py:366
  101.4 5.2 %all-to-all-start = ((f32[8,48,128]{2,1,0:T(8,128)}), f32[8,48,128]{2,1,0:T(8,128)S(1)}, u32[]{:S(2)}, u32[]{:S(2)}) async-start(f32[8,48,128]{2,1,0:T(8,128)} %bitcast.15), calls=%async_computation.1 | async-start | bytes 393216 | tf_op jit(solution)/shard_map/all_to_all | solution.py:562
  106.6 6.3 %all-to-all-done = f32[8,48,128]{2,1,0:T(8,128)S(1)} async-done(((f32[8,48,128]{2,1,0:T(8,128)}), f32[8,48,128]{2,1,0:T(8,128)S(1)}, u32[]{:S(2)}, u32[]{:S(2)}) %all-to-all-start) | async-done | bytes 196640 | tf_op jit(solution)/shard_map/all_to_all | solution.py:562
  112.9 0.1 fusion.2
  113.0 0.7 broadcast_in_dim.14
  113.6 4.0 %all-to-all-start.1 = ((bf16[8,48,128]{2,1,0:T(8,128)(2,1)}), bf16[8,48,128]{2,1,0:T(8,128)(2,1)S(1)}, u32[]{:S(2)}, u32[]{:S(2)}) async-start(bf16[8,48,128]{2,1,0:T(8,128)(2,1)} %broadcast_in_dim.14), calls=%async_computation.2 | async-start | bytes 196608 | tf_op jit(solution)/shard_map/all_to_all | solution.py:504
  117.7 7.8 %all-to-all-done.1 = bf16[8,48,128]{2,1,0:T(8,128)(2,1)S(1)} async-done(((bf16[8,48,128]{2,1,0:T(8,128)(2,1)}), bf16[8,48,128]{2,1,0:T(8,128)(2,1)S(1)}, u32[]{:S(2)}, u32[]{:S(2)}) %all-to-all-start.1) | async-done | bytes 98336 | tf_op jit(solution)/shard_map/all_to_all | solution.py:504
  125.5 0.1 convert_subtract_fusion
  125.6 0.0 reduce-scatter.2.cloned.1.call-done
  125.6 1.0 fusion.5
  126.6 3.4 %collective-permute-start.6 = (bf16[8,80,128]{2,1,0:T(8,128)(2,1)S(1)}, bf16[8,80,128]{2,1,0:T(8,128)(2,1)S(1)}, u32[]{:S(2)}, u32[]{:S(2)}) collective-permute-start(bf16[8,80,128]{2,1,0:T(8,128)(2,1)S(1)} %bitcast.36), channel_id=1, source_target_pairs={{0,16},{16,0},{1,17},{17,1},{2,18},{18,2},{3,19},{19,3},{4,20},{20... | collective-permute-start | bytes 491528 | tf_op jit(solution)/shard_map/ppermute | solution.py:508
  130.1 0.1 fusion.3
  130.2 0.9 collective-permute-done.6
  131.2 17.4 %all_to_all.20 = bf16[8,128,128]{2,1,0:T(8,128)(2,1)S(1)} all-to-all(bf16[8,128,128]{2,1,0:T(8,128)(2,1)S(1)} %pad_maximum_fusion), channel_id=1, replica_groups=mesh['y'=8,'xh'=2,'core'=2,'xl'=2,'z'=8] {'y'}, dimensions={0} | all-to-all | bytes 524288 | tf_op jit(solution)/shard_map/all_to_all | solution.py:566
  148.6 0.8 broadcast_in_dim.16
  149.4 3.5 %all-to-all-start.3 = ((bf16[16,80,128]{2,1,0:T(8,128)(2,1)}), bf16[16,80,128]{2,1,0:T(8,128)(2,1)S(1)}, u32[]{:S(2)}, u32[]{:S(2)}) async-start(bf16[16,80,128]{2,1,0:T(8,128)(2,1)} %broadcast_in_dim.16), calls=%async_computation.4 | async-start | bytes 655360 | tf_op jit(solution)/shard_map/all_to_all | solution.py:504
  153.0 0.1 add_select_fusion
  153.1 4.6 %collective-permute-start.10 = (f32[48,128]{1,0:T(8,128)S(1)}, f32[48,128]{1,0:T(8,128)S(1)}, u32[]{:S(2)}, u32[]{:S(2)}) collective-permute-start(f32[48,128]{1,0:T(8,128)S(1)} %add_select_fusion), channel_id=1, source_target_pairs={{0,32},{32,0},{1,33},{33,1},{2,34},{34,2},{3,35},{35,3},{4,36},{36... | collective-permute-start | bytes 73736 | tf_op jit(solution)/shard_map/ppermute | solution.py:508
  157.7 1.9 %collective-permute-done.10 = f32[48,128]{1,0:T(8,128)S(1)} collective-permute-done((f32[48,128]{1,0:T(8,128)S(1)}, f32[48,128]{1,0:T(8,128)S(1)}, u32[]{:S(2)}, u32[]{:S(2)}) %collective-permute-start.10) | collective-permute-done | bytes 24608 | tf_op jit(solution)/shard_map/ppermute | solution.py:508
  159.6 1.9 %collective-permute-start.11 = (f32[96,128]{1,0:T(8,128)S(1)}, f32[96,128]{1,0:T(8,128)S(1)}, u32[]{:S(2)}, u32[]{:S(2)}) collective-permute-start(f32[96,128]{1,0:T(8,128)S(1)} %pad_maximum_fusion.2), channel_id=1, source_target_pairs={{0,8},{8,0},{1,9},{9,1},{2,10},{10,2},{3,11},{11,3},{4,12},{12,4},... | collective-permute-start | bytes 147464 | tf_op jit(solution)/shard_map/ppermute | solution.py:508
  161.5 2.6 %input_grad.1.pre_ref = f32[1,14,14,768]{3,2,1,0:T(8,128)S(1)} custom-call(f32[6,14,16,128]{3,2,1,0:T(8,128)S(1)} %get-tuple-element.38.conv_ref, bf16[49,768]{1,0:T(8,128)(2,1)S(1)} %reshape.55.kernel_ref, bf16[224,768]{1,0:T(8,128)(2,1)S(1)} %bitcast.28), custom_call_target="tpu_custom_call" | custom-call | tf_op jit(solution)/shard_map/input_grad/pallas_call | solution.py:415
  164.1 0.5 collective-permute-done.11
  164.7 0.5 all-to-all-done.3
  165.2 5.6 %collective-permute-start.13 = (bf16[8,2,80,128]{3,2,1,0:T(8,128)(2,1)S(1)}, bf16[8,2,80,128]{3,2,1,0:T(8,128)(2,1)S(1)}, u32[]{:S(2)}, u32[]{:S(2)}) collective-permute-start(bf16[8,2,80,128]{3,2,1,0:T(8,128)(2,1)S(1)} %bitcast.31), channel_id=1, source_target_pairs={{0,16},{16,0},{1,17},{17,1},{2,18},{18,2},{3,19},{19,3},{4,20},{20... | collective-permute-start | bytes 983048 | tf_op jit(solution)/shard_map/ppermute | solution.py:508
  170.8 1.9 %collective-permute-start.12 = (f32[192,128]{1,0:T(8,128)S(1)}, f32[192,128]{1,0:T(8,128)S(1)}, u32[]{:S(2)}, u32[]{:S(2)}) collective-permute-start(f32[192,128]{1,0:T(8,128)S(1)} %pad_maximum_fusion.1.small_in), channel_id=1, source_target_pairs={{0,16},{16,0},{1,17},{17,1},{2,18},{18,2},{3,19},{19,3},{4,20},{20... | collective-permute-start | bytes 294920 | tf_op jit(solution)/shard_map/ppermute | solution.py:508
  172.7 0.1 pad_add_fusion.place_ref
  172.8 1.2 collective-permute-done.12.small_core_in
  174.0 0.0 collective-permute-done.13.other_ref
  174.0 1.8 %finish.1 = (bf16[1,14,14,768]{3,2,1,0:T(8,128)(2,1)}, f32[192,768]{1,0:T(8,128)}, f32[192,768]{1,0:T(8,128)}, f32[1,192]{1,0:T(1,128)}, f32[7,7,768]{2,1,0:T(8,128)}, /*index=5*/f32[768]{0:T(1024)}, f32[768]{0:T(1024)}) custom-call(s32[4]{0:T(128)S(1)} %pad_add_fusion.place_ref, f32[192,128]{1,0:T(8,128)S(1)} %pad_maximum_fusion.1.small_in, ...), custom_call_target="tpu_custom_call" | custom-call | tf_op jit(solution)/shard_map/finish/pallas_call | solution.py:472
  (37 shorter events, 0.4 us)
Async XLA Ops:
  7.2 18.2 %copy-start.8 = (bf16[7,7,768]{2,1,0:T(8,128)(2,1)S(1)}, bf16[7,7,768]{2,1,0:T(8,128)(2,1)}, u32[]{:S(2)}) copy-start(bf16[7,7,768]{2,1,0:T(8,128)(2,1)} %param.14) | copy-start | bytes 225796
  7.2 18.2 %copy-start.2 = (bf16[1,14,14,768]{3,2,1,0:T(8,128)(2,1)S(1)}, bf16[1,14,14,768]{3,2,1,0:T(8,128)(2,1)}, u32[]{:S(2)}) copy-start(bf16[1,14,14,768]{3,2,1,0:T(8,128)(2,1)} %param.10) | copy-start | bytes 903172
  7.2 30.1 %copy-start.9 = (f32[768]{0:T(1024)S(1)}, f32[768]{0:T(1024)}, u32[]{:S(2)}) copy-start(f32[768]{0:T(1024)} %param.19) | copy-start | bytes 9220
  7.2 53.0 %all-gather.2.cloned.1.call-start = ((), (), s32[]{:S(2)}) async-start(), calls=%async_computation.5 | async-start | bytes 3096576 | tf_op jit(solution)/shard_map/all_gather | solution.py:542
  10.7 114.9 %reduce-scatter.2.cloned.1.call-start = ((), (), s32[]{:S(2)}) async-start(), calls=%async_computation.6 | async-start | bytes 2949120 | tf_op jit(solution)/shard_map/reduce_scatter | solution.py:557
  14.4 45.8 %copy-start = (bf16[14,16,768]{2,1,0:T(8,128)(2,1)}, bf16[14,16,768]{2,1,0:T(8,128)(2,1)S(1)}, u32[]{:S(2)}) copy-start(bf16[14,16,768]{2,1,0:T(8,128)(2,1)S(1)} %pad.4) | copy-start | bytes 1032196
  14.4 20.9 %collective-permute-start.5 = (bf16[224,768]{1,0:T(8,128)(2,1)S(1)}, bf16[224,768]{1,0:T(8,128)(2,1)S(1)}, u32[]{:S(2)}, u32[]{:S(2)}) collective-permute-start(bf16[224,768]{1,0:T(8,128)(2,1)S(1)} %bitcast.24), channel_id=1, source_target_pairs={{0,40},{8,0},{32,8},{40,32},{1,41},{9,1},{33,9},{41,33},{2,42},{10... | collective-permute-start | bytes 1032200 | tf_op jit(solution)/shard_map/ppermute | solution.py:527
  19.7 17.7 %collective-permute-start.4 = (bf16[224,768]{1,0:T(8,128)(2,1)S(1)}, bf16[224,768]{1,0:T(8,128)(2,1)S(1)}, u32[]{:S(2)}, u32[]{:S(2)}) collective-permute-start(bf16[224,768]{1,0:T(8,128)(2,1)S(1)} %bitcast.25), channel_id=1, source_target_pairs={{0,32},{8,40},{32,0},{40,8},{1,33},{9,41},{33,1},{41,9},{2,34},{10... | collective-permute-start | bytes 1032200 | tf_op jit(solution)/shard_map/ppermute | solution.py:527
  22.1 16.7 %collective-permute-start.3 = (bf16[224,768]{1,0:T(8,128)(2,1)S(1)}, bf16[224,768]{1,0:T(8,128)(2,1)S(1)}, u32[]{:S(2)}, u32[]{:S(2)}) collective-permute-start(bf16[224,768]{1,0:T(8,128)(2,1)S(1)} %bitcast.26), channel_id=1, source_target_pairs={{0,8},{8,32},{32,40},{40,0},{1,9},{9,33},{33,41},{41,1},{2,10},{10... | collective-permute-start | bytes 1032200 | tf_op jit(solution)/shard_map/ppermute | solution.py:527
  28.2 11.6 %collective-permute-start.2 = (bf16[224,768]{1,0:T(8,128)(2,1)S(1)}, bf16[224,768]{1,0:T(8,128)(2,1)S(1)}, u32[]{:S(2)}, u32[]{:S(2)}) collective-permute-start(bf16[224,768]{1,0:T(8,128)(2,1)S(1)} %get-tuple-element.28.refs_0_), channel_id=1, source_target_pairs={{0,40},{8,0},{32,8},{40,32},{1,41},{9,1},{33,9},{41,33},{2,42},{10... | collective-permute-start | bytes 1032200 | tf_op jit(solution)/shard_map/ppermute | solution.py:527
  32.2 12.4 %collective-permute-start.1 = (bf16[224,768]{1,0:T(8,128)(2,1)S(1)}, bf16[224,768]{1,0:T(8,128)(2,1)S(1)}, u32[]{:S(2)}, u32[]{:S(2)}) collective-permute-start(bf16[224,768]{1,0:T(8,128)(2,1)S(1)} %get-tuple-element.28.refs_0_), channel_id=1, source_target_pairs={{0,32},{8,40},{32,0},{40,8},{1,33},{9,41},{33,1},{41,9},{2,34},{10... | collective-permute-start | bytes 1032200 | tf_op jit(solution)/shard_map/ppermute | solution.py:527
  35.4 24.9 %copy-start.3 = (bf16[224,768]{1,0:T(8,128)(2,1)}, bf16[224,768]{1,0:T(8,128)(2,1)S(1)}, u32[]{:S(2)}) copy-start(bf16[224,768]{1,0:T(8,128)(2,1)S(1)} %collective-permute-done.5.refs_7_) | copy-start | bytes 1032196
  35.4 18.7 %collective-permute-start = (bf16[224,768]{1,0:T(8,128)(2,1)S(1)}, bf16[224,768]{1,0:T(8,128)(2,1)}, u32[]{:S(2)}, u32[]{:S(2)}) collective-permute-start(bf16[224,768]{1,0:T(8,128)(2,1)S(1)} %get-tuple-element.28.refs_0_), channel_id=1, source_target_pairs={{0,8},{8,32},{32,40},{40,0},{1,9},{9,33},{33,41},{41,1},{2,10},{10... | collective-permute-start | bytes 1032200 | tf_op jit(solution)/shard_map/ppermute | solution.py:527
  37.3 22.9 %copy-start.4 = (bf16[224,768]{1,0:T(8,128)(2,1)}, bf16[224,768]{1,0:T(8,128)(2,1)S(1)}, u32[]{:S(2)}) copy-start(bf16[224,768]{1,0:T(8,128)(2,1)S(1)} %collective-permute-done.4.refs_6_) | copy-start | bytes 1032196
  38.8 21.4 %copy-start.5 = (bf16[224,768]{1,0:T(8,128)(2,1)}, bf16[224,768]{1,0:T(8,128)(2,1)S(1)}, u32[]{:S(2)}) copy-start(bf16[224,768]{1,0:T(8,128)(2,1)S(1)} %collective-permute-done.3.refs_5_) | copy-start | bytes 1032196
  39.8 4.8 %copy-start.6 = (bf16[224,768]{1,0:T(8,128)(2,1)}, bf16[224,768]{1,0:T(8,128)(2,1)S(1)}, u32[]{:S(2)}) copy-start(bf16[224,768]{1,0:T(8,128)(2,1)S(1)} %collective-permute-done.2.refs_3_) | copy-start | bytes 1032196
  44.6 0.7 copy-start.7
  73.0 9.6 %collective-permute-start.7 = (bf16[224,768]{1,0:T(8,128)(2,1)S(1)}, bf16[224,768]{1,0:T(8,128)(2,1)S(1)}, u32[]{:S(2)}, u32[]{:S(2)}) collective-permute-start(bf16[224,768]{1,0:T(8,128)(2,1)S(1)} %get-tuple-element.31), channel_id=1, source_target_pairs={{0,40},{8,0},{32,8},{40,32},{1,41},{9,1},{33,9},{41,33},{2,42},{10... | collective-permute-start | bytes 1032200 | tf_op jit(solution)/shard_map/ppermute | solution.py:527
  77.2 9.6 %collective-permute-start.8 = (bf16[224,768]{1,0:T(8,128)(2,1)S(1)}, bf16[224,768]{1,0:T(8,128)(2,1)S(1)}, u32[]{:S(2)}, u32[]{:S(2)}) collective-permute-start(bf16[224,768]{1,0:T(8,128)(2,1)S(1)} %get-tuple-element.32), channel_id=1, source_target_pairs={{0,32},{8,40},{32,0},{40,8},{1,33},{9,41},{33,1},{41,9},{2,34},{10... | collective-permute-start | bytes 1032200 | tf_op jit(solution)/shard_map/ppermute | solution.py:527
  79.5 17.1 %collective-permute-start.9 = (bf16[224,768]{1,0:T(8,128)(2,1)S(1)}, bf16[224,768]{1,0:T(8,128)(2,1)S(1)}, u32[]{:S(2)}, u32[]{:S(2)}) collective-permute-start(bf16[224,768]{1,0:T(8,128)(2,1)S(1)} %get-tuple-element.33), channel_id=1, source_target_pairs={{0,8},{8,32},{32,40},{40,0},{1,9},{9,33},{33,41},{41,1},{2,10},{10... | collective-permute-start | bytes 1032200 | tf_op jit(solution)/shard_map/ppermute | solution.py:527
  101.4 11.5 %all-to-all-start = ((f32[8,48,128]{2,1,0:T(8,128)}), f32[8,48,128]{2,1,0:T(8,128)S(1)}, u32[]{:S(2)}, u32[]{:S(2)}) async-start(f32[8,48,128]{2,1,0:T(8,128)} %bitcast.15), calls=%async_computation.1 | async-start | bytes 393216 | tf_op jit(solution)/shard_map/all_to_all | solution.py:562
  113.0 48.5 %copy-start.1 = (bf16[14,16,768]{2,1,0:T(8,128)(2,1)S(1)}, bf16[14,16,768]{2,1,0:T(8,128)(2,1)}, u32[]{:S(2)}) copy-start(bf16[14,16,768]{2,1,0:T(8,128)(2,1)} %copy-done) | copy-start | bytes 1032196
  113.6 11.8 %all-to-all-start.1 = ((bf16[8,48,128]{2,1,0:T(8,128)(2,1)}), bf16[8,48,128]{2,1,0:T(8,128)(2,1)S(1)}, u32[]{:S(2)}, u32[]{:S(2)}) async-start(bf16[8,48,128]{2,1,0:T(8,128)(2,1)} %broadcast_in_dim.14), calls=%async_computation.2 | async-start | bytes 196608 | tf_op jit(solution)/shard_map/all_to_all | solution.py:504
  126.6 4.4 %collective-permute-start.6 = (bf16[8,80,128]{2,1,0:T(8,128)(2,1)S(1)}, bf16[8,80,128]{2,1,0:T(8,128)(2,1)S(1)}, u32[]{:S(2)}, u32[]{:S(2)}) collective-permute-start(bf16[8,80,128]{2,1,0:T(8,128)(2,1)S(1)} %bitcast.36), channel_id=1, source_target_pairs={{0,16},{16,0},{1,17},{17,1},{2,18},{18,2},{3,19},{19,3},{4,20},{20... | collective-permute-start | bytes 491528 | tf_op jit(solution)/shard_map/ppermute | solution.py:508
  149.4 15.8 %all-to-all-start.3 = ((bf16[16,80,128]{2,1,0:T(8,128)(2,1)}), bf16[16,80,128]{2,1,0:T(8,128)(2,1)S(1)}, u32[]{:S(2)}, u32[]{:S(2)}) async-start(bf16[16,80,128]{2,1,0:T(8,128)(2,1)} %broadcast_in_dim.16), calls=%async_computation.4 | async-start | bytes 655360 | tf_op jit(solution)/shard_map/all_to_all | solution.py:504
  153.1 6.5 %collective-permute-start.10 = (f32[48,128]{1,0:T(8,128)S(1)}, f32[48,128]{1,0:T(8,128)S(1)}, u32[]{:S(2)}, u32[]{:S(2)}) collective-permute-start(f32[48,128]{1,0:T(8,128)S(1)} %add_select_fusion), channel_id=1, source_target_pairs={{0,32},{32,0},{1,33},{33,1},{2,34},{34,2},{3,35},{35,3},{4,36},{36... | collective-permute-start | bytes 73736 | tf_op jit(solution)/shard_map/ppermute | solution.py:508
  159.6 5.1 %collective-permute-start.11 = (f32[96,128]{1,0:T(8,128)S(1)}, f32[96,128]{1,0:T(8,128)S(1)}, u32[]{:S(2)}, u32[]{:S(2)}) collective-permute-start(f32[96,128]{1,0:T(8,128)S(1)} %pad_maximum_fusion.2), channel_id=1, source_target_pairs={{0,8},{8,0},{1,9},{9,1},{2,10},{10,2},{3,11},{11,3},{4,12},{12,4},... | collective-permute-start | bytes 147464 | tf_op jit(solution)/shard_map/ppermute | solution.py:508
  165.2 8.8 %collective-permute-start.13 = (bf16[8,2,80,128]{3,2,1,0:T(8,128)(2,1)S(1)}, bf16[8,2,80,128]{3,2,1,0:T(8,128)(2,1)S(1)}, u32[]{:S(2)}, u32[]{:S(2)}) collective-permute-start(bf16[8,2,80,128]{3,2,1,0:T(8,128)(2,1)S(1)} %bitcast.31), channel_id=1, source_target_pairs={{0,16},{16,0},{1,17},{17,1},{2,18},{18,2},{3,19},{19,3},{4,20},{20... | collective-permute-start | bytes 983048 | tf_op jit(solution)/shard_map/ppermute | solution.py:508
  170.8 3.2 %collective-permute-start.12 = (f32[192,128]{1,0:T(8,128)S(1)}, f32[192,128]{1,0:T(8,128)S(1)}, u32[]{:S(2)}, u32[]{:S(2)}) collective-permute-start(f32[192,128]{1,0:T(8,128)S(1)} %pad_maximum_fusion.1.small_in), channel_id=1, source_target_pairs={{0,16},{16,0},{1,17},{17,1},{2,18},{18,2},{3,19},{19,3},{4,20},{20... | collective-permute-start | bytes 294920 | tf_op jit(solution)/shard_map/ppermute | solution.py:508
Sparse Core Ops, SparseCore 0:
  10.9 49.2 all-gather.1
  73.1 44.3 reduce-scatter.1

commit v7 on v6

--- a/solution.py
+++ b/solution.py
@@ -52,31 +52,30 @@
     return pl.BlockSpec(shape, lambda i: (0,) * len(shape))
 
 
-def pack_kernel(place_ref, first_in, bias_in, second_in, out_ref, first_ref, bias_ref, second_ref, sems):
-    pairs = ((first_in, first_ref), (second_in, second_ref), (bias_in, bias_ref))
-    copies = [pltpu.make_async_copy(source, target, sems.at[i]) for i, (source, target) in enumerate(pairs)]
+def pack_kernel(place_ref, first_in, bias_in, second_in, out_ref, bias_ref, sems):
+    q = place_ref[0]
+    column = place_ref[1]
+    blocks = (q, q + 1 - 2 * lax.rem(q, 2))
+    copies = [pltpu.make_async_copy(bias_in, bias_ref, sems.at[4])]
+    for k in range(2):
+        rows = pl.ds(pl.multiple_of(blocks[k] * OWN, OWN), OWN)
+        copies.append(pltpu.make_async_copy(first_in.at[rows], out_ref.at[k, pl.ds(0, OWN)], sems.at[k]))
+        copies.append(pltpu.make_async_copy(second_in.at[rows], out_ref.at[k, pl.ds(OWN, OWN)], sems.at[2 + k]))
     for copy in copies:
         copy.start()
-    for copy in copies:
+    copies[0].wait()
+    bias = jnp.broadcast_to(bias_ref[...], (16, 192))
+    high = bias.astype(BF16)
+    low = (bias - high.astype(F32)).astype(BF16)
+    bias_row = lax.broadcasted_iota(jnp.int32, (16, 192), 0)
+    both = jnp.where(bias_row == 0, high.astype(F32), low.astype(F32)).astype(BF16)
+    unit = lax.broadcasted_iota(jnp.int32, (192, CH), 0)
+    spot = lax.broadcasted_iota(jnp.int32, (192, CH), 1) - column * UNITS
+    for k in range(2):
+        put = ((unit == spot + blocks[k] * OWN) & (spot >= 0) & (spot < OWN)).astype(BF16)
+        out_ref[k, UNITS:PACK, :] = jnp.dot(both, put, preferred_element_type=F32).astype(BF16)
+    for copy in copies[1:]:
         copy.wait()
-    q = place_ref[0]
-    column = place_ref[1]
-    for k in range(2):
-        at = q + k * (1 - 2 * lax.rem(q, 2))
-        row = lax.broadcasted_iota(jnp.int32, (OWN, 192), 0)
-        lane = lax.broadcasted_iota(jnp.int32, (OWN, 192), 1)
-        pick = (lane == row + at * OWN).astype(BF16)
-        out_ref[k, 0:OWN, :] = jnp.dot(pick, first_ref[...], preferred_element_type=F32).astype(BF16)
-        out_ref[k, OWN:UNITS, :] = jnp.dot(pick, second_ref[...], preferred_element_type=F32).astype(BF16)
-        unit = lax.broadcasted_iota(jnp.int32, (192, CH), 0)
-        spot = lax.broadcasted_iota(jnp.int32, (192, CH), 1) - column * UNITS
-        put = ((unit == spot + at * OWN) & (spot >= 0) & (spot < OWN)).astype(BF16)
-        bias = jnp.broadcast_to(bias_ref[...], (16, 192))
-        high = bias.astype(BF16)
-        low = (bias - high.astype(F32)).astype(BF16)
-        bias_row = lax.broadcasted_iota(jnp.int32, (16, 192), 0)
-        both = jnp.where(bias_row == 0, high.astype(F32), low.astype(F32)).astype(BF16)
-        out_ref[k, UNITS:PACK, :] = jnp.dot(both, put, preferred_element_type=F32).astype(BF16)
 
 
 def pack_weights(place, first_weight, first_bias, second_weight):
@@ -87,10 +86,8 @@
         in_specs=[scalars()] + [pl.BlockSpec(memory_space=pl.ANY)] * 3,
         out_specs=block(2, PACK, CH),
         scratch_shapes=[
-            pltpu.VMEM((192, CH), BF16),
             pltpu.VMEM((1, 192), F32),
-            pltpu.VMEM((192, CH), BF16),
-            pltpu.SemaphoreType.DMA((3,)),
+            pltpu.SemaphoreType.DMA((5,)),
         ],
         compiler_params=params(58),
         interpret=INTERPRET,
@@ -183,7 +180,7 @@
     pack_in, layer_ref = refs[8:10]
     part_outs = refs[10:14]
     grads_out, scale_ref = refs[14:16]
-    normed, scaled, firsts, seconds, biases, act, grad, parts, out_ref, sems, out_sems = refs[16:27]
+    normed, scaled, firsts, seconds, biases, act, grad, parts, out_ref, slopes, sems, out_sems = refs[16:28]
     first_copies, second_copies, normed_copies, scaled_copies, sends = [], [], [], [], []
     for k in range(2):
         whole_z = pl.ds(0, 8)
@@ -216,15 +213,16 @@
         normed_copies[i].wait()
         preact = nt(normed[rows, :], first) + bias
         cumulative = 0.5 * (1.0 + lax.erf(preact * 0.7071067811865476))
-        slope = cumulative + preact * jnp.exp(-0.5 * preact * preact) * 0.3989422804014327
+        slopes[rows, :] = cumulative + preact * jnp.exp(-0.5 * preact * preact) * 0.3989422804014327
         act[rows, :] = (preact * cumulative).astype(BF16)
-        if i == 0:
-            for copy in second_copies:
-                copy.wait()
-            second = seconds[...].reshape(CH, CH)
+    for copy in second_copies:
+        copy.wait()
+    second = seconds[...].reshape(CH, CH)
+    for i in range(4):
+        rows = slice(i * PIX, (i + 1) * PIX)
         scaled_copies[i].wait()
         branch_grad = (scaled[rows, :].astype(F32) * layer).astype(BF16)
-        preact_grad = (nt(branch_grad, second) * slope).astype(BF16)
+        preact_grad = (nt(branch_grad, second) * slopes[rows, :]).astype(BF16)
         grad[rows, :] = preact_grad
         parts[rows, :] = jnp.dot(preact_grad, first, preferred_element_type=F32).astype(BF16)
         sends.append(pltpu.make_async_copy(parts.at[pl.ds(i * PIX, PIX)], part_outs[i], out_sems.at[i]))
@@ -297,6 +295,7 @@
             pltpu.VMEM((4 * PIX, CH), BF16),
             pltpu.VMEM((4 * PIX, CH), BF16),
             pltpu.VMEM((8, 1280, LANES), BF16),
+            pltpu.VMEM((4 * PIX, CH), F32),
             pltpu.SemaphoreType.DMA((14,)),
             pltpu.SemaphoreType.DMA((8,)),
         ],

time: 184 us -> 183 us (level)
  no operation moved by 1% of the time
where the time goes in v7:
time: 183 us; the launch traced here: 182 us
  starting transfers between devices  58.9 us (32%)
  waiting for transfers between devices  55.4 us (30%)
  Pallas kernels  27.3 us (15%)
  blocking collectives  17.4 us (10%)
  between operations  15.1 us (8%)
  other arithmetic  4.13 us (2%)
  local copies, waits for them, and re-layouts  4.02 us (2%)
    ppermute x9, waiting for transfers between devices, ring(): return lax.ppermute(value, RING, [(i, (i + shift) % 4) for i in range(4)])  30.2 us
    ppermute x9, starting transfers between devices, ring(): return lax.ppermute(value, RING, [(i, (i + shift) % 4) for i in range(4)])  28.4 us
    ppermute x5, starting transfers between devices, swap(): return lax.ppermute(value, axis, [(0, 1), (1, 0)])  17.5 us
    all_to_all x1, blocking collectives, per_device(): lax.all_to_all(jnp.concatenate([grads, both], axis=1), 'y', 0, 0, tiled=T...  17.4 us
    pallas_call x1, Pallas kernels, hidden(): pl.pallas_call(hidden_kernel, grid=(1,), out_shape=(jax.ShapeDtypeStruct(...  12.8 us
    all_to_all x2, waiting for transfers between devices, to_all(): lax.all_to_all(jnp.broadcast_to(value, (count, *value.shape)), axes, 0, 0...  8.3 us
    all_to_all x2, starting transfers between devices, to_all(): lax.all_to_all(jnp.broadcast_to(value, (count, *value.shape)), axes, 0, 0...  7.62 us
    all_to_all x1, waiting for transfers between devices, per_device(): small = lax.all_to_all(small.reshape(8, OWN, LANES), TEAM, 0, 0, tiled=True)  6.25 us
  transfers between devices with their start and end apart: 19, of which 15 were waited for; matrix products, arithmetic and copies ran while one was open for 3% of the time, Pallas kernels for 6%

profile of v7, /device:TPU:1, one launch (start us, length us, event | category | flops | bytes accessed | tf_op | source)
XLA Modules:
  0.0 182.3 jit_solution(2113808594358017323)
XLA Ops:
  7.2 0.0 copy-start.8
  7.2 0.0 copy-start.2
  7.2 0.0 copy-start.9
  7.2 0.0 all-gather.2.cloned.1.call-start
  7.3 0.6 pad_add_fusion.1.place_ref
  7.8 2.4 %pack.1 = bf16[2,112,768]{2,1,0:T(8,128)(2,1)} custom-call(s32[2]{0:T(128)} %pad_add_fusion.1.place_ref, bf16[192,768]{1,0:T(8,128)(2,1)} %bitcast.35, f32[1,192]{1,0:T(1,128)} %bitcast.39, bf16[192,768]{1,0:T(8,128)(2,1)} %second_in.1), custom_call_target="tpu_custom_call" | custom-call | tf_op jit(solution)/shard_map/pack/pallas_call | solution.py:82
  10.3 0.0 all-gather.2.cloned.1.call-update
  10.3 0.0 reduce-scatter.2.cloned.1.call-start
  11.0 1.3 fusion.4
  12.3 1.7 fusion
  14.0 0.0 copy-start
  14.0 5.2 %collective-permute-start.5 = (bf16[224,768]{1,0:T(8,128)(2,1)S(1)}, bf16[224,768]{1,0:T(8,128)(2,1)S(1)}, u32[]{:S(2)}, u32[]{:S(2)}) collective-permute-start(bf16[224,768]{1,0:T(8,128)(2,1)S(1)} %bitcast.24), channel_id=1, source_target_pairs={{0,40},{8,0},{32,8},{40,32},{1,41},{9,1},{33,9},{41,33},{2,42},{10... | collective-permute-start | bytes 1032200 | tf_op jit(solution)/shard_map/ppermute | solution.py:526
  19.2 2.4 %collective-permute-start.4 = (bf16[224,768]{1,0:T(8,128)(2,1)S(1)}, bf16[224,768]{1,0:T(8,128)(2,1)S(1)}, u32[]{:S(2)}, u32[]{:S(2)}) collective-permute-start(bf16[224,768]{1,0:T(8,128)(2,1)S(1)} %bitcast.25), channel_id=1, source_target_pairs={{0,32},{8,40},{32,0},{40,8},{1,33},{9,41},{33,1},{41,9},{2,34},{10... | collective-permute-start | bytes 1032200 | tf_op jit(solution)/shard_map/ppermute | solution.py:526
  21.7 2.5 %collective-permute-start.3 = (bf16[224,768]{1,0:T(8,128)(2,1)S(1)}, bf16[224,768]{1,0:T(8,128)(2,1)S(1)}, u32[]{:S(2)}, u32[]{:S(2)}) collective-permute-start(bf16[224,768]{1,0:T(8,128)(2,1)S(1)} %bitcast.26), channel_id=1, source_target_pairs={{0,8},{8,32},{32,40},{40,0},{1,9},{9,33},{33,41},{41,1},{2,10},{10... | collective-permute-start | bytes 1032200 | tf_op jit(solution)/shard_map/ppermute | solution.py:526
  24.2 0.7 reshape.56.gain_ref
  24.9 2.8 %conv_norm.1 = (bf16[224,768]{1,0:T(8,128)(2,1)S(1)}, f32[6,14,16,128]{3,2,1,0:T(8,128)S(1)}, f32[14,16,128]{2,1,0:T(8,128)S(1)}) custom-call(bf16[14,14,768]{2,1,0:T(8,128)(2,1)S(1)} %bitcast.29, bf16[49,768]{1,0:T(8,128)(2,1)S(1)} %reshape.55.kernel_ref, f32[1,768]{1,0:T(1,128)S(1)} %reshape.56.gain_ref), custom_call_target="tpu_custom_call" | custom-call | tf_op jit(solution)/shard_map/conv_norm/pallas_call | solution.py:149
  27.8 4.0 %collective-permute-start.2 = (bf16[224,768]{1,0:T(8,128)(2,1)S(1)}, bf16[224,768]{1,0:T(8,128)(2,1)S(1)}, u32[]{:S(2)}, u32[]{:S(2)}) collective-permute-start(bf16[224,768]{1,0:T(8,128)(2,1)S(1)} %get-tuple-element.28.refs_0_), channel_id=1, source_target_pairs={{0,40},{8,0},{32,8},{40,32},{1,41},{9,1},{33,9},{41,33},{2,42},{10... | collective-permute-start | bytes 1032200 | tf_op jit(solution)/shard_map/ppermute | solution.py:526
  31.7 3.1 %collective-permute-start.1 = (bf16[224,768]{1,0:T(8,128)(2,1)S(1)}, bf16[224,768]{1,0:T(8,128)(2,1)S(1)}, u32[]{:S(2)}, u32[]{:S(2)}) collective-permute-start(bf16[224,768]{1,0:T(8,128)(2,1)S(1)} %get-tuple-element.28.refs_0_), channel_id=1, source_target_pairs={{0,32},{8,40},{32,0},{40,8},{1,33},{9,41},{33,1},{41,9},{2,34},{10... | collective-permute-start | bytes 1032200 | tf_op jit(solution)/shard_map/ppermute | solution.py:526
  34.9 0.0 collective-permute-done.5.refs_7_
  34.9 1.9 %collective-permute-start = (bf16[224,768]{1,0:T(8,128)(2,1)S(1)}, bf16[224,768]{1,0:T(8,128)(2,1)}, u32[]{:S(2)}, u32[]{:S(2)}) collective-permute-start(bf16[224,768]{1,0:T(8,128)(2,1)S(1)} %get-tuple-element.28.refs_0_), channel_id=1, source_target_pairs={{0,8},{8,32},{32,40},{40,0},{1,9},{9,33},{33,41},{41,1},{2,10},{10... | collective-permute-start | bytes 1032200 | tf_op jit(solution)/shard_map/ppermute | solution.py:526
  36.9 0.0 collective-permute-done.4.refs_6_
  36.9 1.4 collective-permute-done.3.refs_5_
  38.3 1.0 collective-permute-done.2.refs_3_
  39.4 4.8 %collective-permute-done.1.refs_2_ = bf16[224,768]{1,0:T(8,128)(2,1)S(1)} collective-permute-done((bf16[224,768]{1,0:T(8,128)(2,1)S(1)}, bf16[224,768]{1,0:T(8,128)(2,1)S(1)}, u32[]{:S(2)}, u32[]{:S(2)}) %collective-permute-start.1) | collective-permute-done | bytes 344096 | tf_op jit(solution)/shard_map/ppermute | solution.py:526
  44.2 0.7 copy-done.7
  44.9 8.7 %collective-permute-done.refs_1_ = bf16[224,768]{1,0:T(8,128)(2,1)} collective-permute-done((bf16[224,768]{1,0:T(8,128)(2,1)S(1)}, bf16[224,768]{1,0:T(8,128)(2,1)}, u32[]{:S(2)}, u32[]{:S(2)}) %collective-permute-start) | collective-permute-done | bytes 344096 | tf_op jit(solution)/shard_map/ppermute | solution.py:526
  53.6 6.1 %all-gather.2.cloned.1.call-done = bf16[16,112,768]{2,1,0:T(8,128)(2,1)} async-done(((bf16[2,112,768]{2,1,0:T(8,128)(2,1)}), bf16[16,112,768]{2,1,0:T(8,128)(2,1)}) %all-gather.2.cloned.1.call-update) | async-done | bytes 2752528 | tf_op jit(solution)/shard_map/all_gather | solution.py:541
  59.8 12.8 %hidden.1 = (bf16[224,768]{1,0:T(8,128)(2,1)S(1)}, bf16[224,768]{1,0:T(8,128)(2,1)S(1)}, bf16[224,768]{1,0:T(8,128)(2,1)S(1)}, bf16[224,768]{1,0:T(8,128)(2,1)S(...) custom-call(bf16[224,768]{1,0:T(8,128)(2,1)S(1)} %get-tuple-element.28.refs_0_, ...), custom_call_target="tpu_custom_call" | custom-call | tf_op jit(solution)/shard_map/hidden/pallas_call | solution.py:280
  72.6 0.0 reduce-scatter.2.cloned.1.call-update
  72.6 4.2 %collective-permute-start.7 = (bf16[224,768]{1,0:T(8,128)(2,1)S(1)}, bf16[224,768]{1,0:T(8,128)(2,1)S(1)}, u32[]{:S(2)}, u32[]{:S(2)}) collective-permute-start(bf16[224,768]{1,0:T(8,128)(2,1)S(1)} %get-tuple-element.31), channel_id=1, source_target_pairs={{0,40},{8,0},{32,8},{40,32},{1,41},{9,1},{33,9},{41,33},{2,42},{10... | collective-permute-start | bytes 1032200 | tf_op jit(solution)/shard_map/ppermute | solution.py:526
  76.8 2.6 %collective-permute-start.8 = (bf16[224,768]{1,0:T(8,128)(2,1)S(1)}, bf16[224,768]{1,0:T(8,128)(2,1)S(1)}, u32[]{:S(2)}, u32[]{:S(2)}) collective-permute-start(bf16[224,768]{1,0:T(8,128)(2,1)S(1)} %get-tuple-element.32), channel_id=1, source_target_pairs={{0,32},{8,40},{32,0},{40,8},{1,33},{9,41},{33,1},{41,9},{2,34},{10... | collective-permute-start | bytes 1032200 | tf_op jit(solution)/shard_map/ppermute | solution.py:526
  79.4 2.4 %collective-permute-start.9 = (bf16[224,768]{1,0:T(8,128)(2,1)S(1)}, bf16[224,768]{1,0:T(8,128)(2,1)S(1)}, u32[]{:S(2)}, u32[]{:S(2)}) collective-permute-start(bf16[224,768]{1,0:T(8,128)(2,1)S(1)} %get-tuple-element.33), channel_id=1, source_target_pairs={{0,8},{8,32},{32,40},{40,0},{1,9},{9,33},{33,41},{41,1},{2,10},{10... | collective-permute-start | bytes 1032200 | tf_op jit(solution)/shard_map/ppermute | solution.py:526
  81.8 0.3 collective-permute-done.7.one_ref
  82.1 4.3 %collective-permute-done.8.two_ref = bf16[224,768]{1,0:T(8,128)(2,1)S(1)} collective-permute-done((bf16[224,768]{1,0:T(8,128)(2,1)S(1)}, bf16[224,768]{1,0:T(8,128)(2,1)S(1)}, u32[]{:S(2)}, u32[]{:S(2)}) %collective-permute-start.8) | collective-permute-done | bytes 344096 | tf_op jit(solution)/shard_map/ppermute | solution.py:526
  86.4 9.6 %collective-permute-done.9.three_ref = bf16[224,768]{1,0:T(8,128)(2,1)S(1)} collective-permute-done((bf16[224,768]{1,0:T(8,128)(2,1)S(1)}, bf16[224,768]{1,0:T(8,128)(2,1)S(1)}, u32[]{:S(2)}, u32[]{:S(2)}) %collective-permute-start.9) | collective-permute-done | bytes 344096 | tf_op jit(solution)/shard_map/ppermute | solution.py:526
  96.0 4.8 %norm_back.1 = (f32[6,64,128]{2,1,0:T(8,128)}, f32[6,14,16,128]{3,2,1,0:T(8,128)S(1)}) custom-call(f32[1]{0:T(128)} %bitcast.14.weight_ref, bf16[224,768]{1,0:T(8,128)(2,1)S(1)} %get-tuple-element.30.zero_ref, bf16[224,768]{1,0:T(8,128)(2,1)S(1)} %collective-permute-done.7.one_ref, bf16[224,768]{1,0:T(8,128)(2,1)S(1)} %collective-permute-done.8.two_ref, ...), custom_call_target="tpu_custom_call" | custom-call | tf_op jit(solution)/shard_map/norm_back/pallas_call | solution.py:365
  100.8 5.3 %all-to-all-start = ((f32[8,48,128]{2,1,0:T(8,128)}), f32[8,48,128]{2,1,0:T(8,128)S(1)}, u32[]{:S(2)}, u32[]{:S(2)}) async-start(f32[8,48,128]{2,1,0:T(8,128)} %bitcast.15), calls=%async_computation.1 | async-start | bytes 393216 | tf_op jit(solution)/shard_map/all_to_all | solution.py:561
  106.2 6.3 %all-to-all-done = f32[8,48,128]{2,1,0:T(8,128)S(1)} async-done(((f32[8,48,128]{2,1,0:T(8,128)}), f32[8,48,128]{2,1,0:T(8,128)S(1)}, u32[]{:S(2)}, u32[]{:S(2)}) %all-to-all-start) | async-done | bytes 196640 | tf_op jit(solution)/shard_map/all_to_all | solution.py:561
  112.5 0.1 fusion.2
  112.5 0.7 broadcast_in_dim.14
  113.2 4.1 %all-to-all-start.1 = ((bf16[8,48,128]{2,1,0:T(8,128)(2,1)}), bf16[8,48,128]{2,1,0:T(8,128)(2,1)S(1)}, u32[]{:S(2)}, u32[]{:S(2)}) async-start(bf16[8,48,128]{2,1,0:T(8,128)(2,1)} %broadcast_in_dim.14), calls=%async_computation.2 | async-start | bytes 196608 | tf_op jit(solution)/shard_map/all_to_all | solution.py:503
  117.3 7.8 %all-to-all-done.1 = bf16[8,48,128]{2,1,0:T(8,128)(2,1)S(1)} async-done(((bf16[8,48,128]{2,1,0:T(8,128)(2,1)}), bf16[8,48,128]{2,1,0:T(8,128)(2,1)S(1)}, u32[]{:S(2)}, u32[]{:S(2)}) %all-to-all-start.1) | async-done | bytes 98336 | tf_op jit(solution)/shard_map/all_to_all | solution.py:503
  125.1 0.1 convert_subtract_fusion
  125.2 0.0 reduce-scatter.2.cloned.1.call-done
  125.2 1.0 fusion.5
  126.2 3.4 %collective-permute-start.6 = (bf16[8,80,128]{2,1,0:T(8,128)(2,1)S(1)}, bf16[8,80,128]{2,1,0:T(8,128)(2,1)S(1)}, u32[]{:S(2)}, u32[]{:S(2)}) collective-permute-start(bf16[8,80,128]{2,1,0:T(8,128)(2,1)S(1)} %bitcast.36), channel_id=1, source_target_pairs={{0,16},{16,0},{1,17},{17,1},{2,18},{18,2},{3,19},{19,3},{4,20},{20... | collective-permute-start | bytes 491528 | tf_op jit(solution)/shard_map/ppermute | solution.py:507
  129.7 0.1 fusion.3
  129.8 0.9 collective-permute-done.6
  130.8 17.4 %all_to_all.20 = bf16[8,128,128]{2,1,0:T(8,128)(2,1)S(1)} all-to-all(bf16[8,128,128]{2,1,0:T(8,128)(2,1)S(1)} %pad_maximum_fusion), channel_id=1, replica_groups=mesh['y'=8,'xh'=2,'core'=2,'xl'=2,'z'=8] {'y'}, dimensions={0} | all-to-all | bytes 524288 | tf_op jit(solution)/shard_map/all_to_all | solution.py:565
  148.2 0.8 broadcast_in_dim.16
  149.0 3.5 %all-to-all-start.3 = ((bf16[16,80,128]{2,1,0:T(8,128)(2,1)}), bf16[16,80,128]{2,1,0:T(8,128)(2,1)S(1)}, u32[]{:S(2)}, u32[]{:S(2)}) async-start(bf16[16,80,128]{2,1,0:T(8,128)(2,1)} %broadcast_in_dim.16), calls=%async_computation.4 | async-start | bytes 655360 | tf_op jit(solution)/shard_map/all_to_all | solution.py:503
  152.6 0.1 add_select_fusion
  152.7 4.6 %collective-permute-start.10 = (f32[48,128]{1,0:T(8,128)S(1)}, f32[48,128]{1,0:T(8,128)S(1)}, u32[]{:S(2)}, u32[]{:S(2)}) collective-permute-start(f32[48,128]{1,0:T(8,128)S(1)} %add_select_fusion), channel_id=1, source_target_pairs={{0,32},{32,0},{1,33},{33,1},{2,34},{34,2},{3,35},{35,3},{4,36},{36... | collective-permute-start | bytes 73736 | tf_op jit(solution)/shard_map/ppermute | solution.py:507
  157.3 1.9 %collective-permute-done.10 = f32[48,128]{1,0:T(8,128)S(1)} collective-permute-done((f32[48,128]{1,0:T(8,128)S(1)}, f32[48,128]{1,0:T(8,128)S(1)}, u32[]{:S(2)}, u32[]{:S(2)}) %collective-permute-start.10) | collective-permute-done | bytes 24608 | tf_op jit(solution)/shard_map/ppermute | solution.py:507
  159.2 1.9 %collective-permute-start.11 = (f32[96,128]{1,0:T(8,128)S(1)}, f32[96,128]{1,0:T(8,128)S(1)}, u32[]{:S(2)}, u32[]{:S(2)}) collective-permute-start(f32[96,128]{1,0:T(8,128)S(1)} %pad_maximum_fusion.2), channel_id=1, source_target_pairs={{0,8},{8,0},{1,9},{9,1},{2,10},{10,2},{3,11},{11,3},{4,12},{12,4},... | collective-permute-start | bytes 147464 | tf_op jit(solution)/shard_map/ppermute | solution.py:507
  161.1 2.6 %input_grad.1.pre_ref = f32[1,14,14,768]{3,2,1,0:T(8,128)S(1)} custom-call(f32[6,14,16,128]{3,2,1,0:T(8,128)S(1)} %get-tuple-element.38.conv_ref, bf16[49,768]{1,0:T(8,128)(2,1)S(1)} %reshape.55.kernel_ref, bf16[224,768]{1,0:T(8,128)(2,1)S(1)} %bitcast.28), custom_call_target="tpu_custom_call" | custom-call | tf_op jit(solution)/shard_map/input_grad/pallas_call | solution.py:414
  163.8 0.5 collective-permute-done.11
  164.3 0.5 all-to-all-done.3
  164.8 5.6 %collective-permute-start.13 = (bf16[8,2,80,128]{3,2,1,0:T(8,128)(2,1)S(1)}, bf16[8,2,80,128]{3,2,1,0:T(8,128)(2,1)S(1)}, u32[]{:S(2)}, u32[]{:S(2)}) collective-permute-start(bf16[8,2,80,128]{3,2,1,0:T(8,128)(2,1)S(1)} %bitcast.31), channel_id=1, source_target_pairs={{0,16},{16,0},{1,17},{17,1},{2,18},{18,2},{3,19},{19,3},{4,20},{20... | collective-permute-start | bytes 983048 | tf_op jit(solution)/shard_map/ppermute | solution.py:507
  170.4 1.9 %collective-permute-start.12 = (f32[192,128]{1,0:T(8,128)S(1)}, f32[192,128]{1,0:T(8,128)S(1)}, u32[]{:S(2)}, u32[]{:S(2)}) collective-permute-start(f32[192,128]{1,0:T(8,128)S(1)} %pad_maximum_fusion.1.small_in), channel_id=1, source_target_pairs={{0,16},{16,0},{1,17},{17,1},{2,18},{18,2},{3,19},{19,3},{4,20},{20... | collective-permute-start | bytes 294920 | tf_op jit(solution)/shard_map/ppermute | solution.py:507
  172.3 0.1 pad_add_fusion.place_ref
  172.4 1.2 collective-permute-done.12.small_core_in
  173.6 0.0 collective-permute-done.13.other_ref
  173.6 1.8 %finish.1 = (bf16[1,14,14,768]{3,2,1,0:T(8,128)(2,1)}, f32[192,768]{1,0:T(8,128)}, f32[192,768]{1,0:T(8,128)}, f32[1,192]{1,0:T(1,128)}, f32[7,7,768]{2,1,0:T(8,128)}, /*index=5*/f32[768]{0:T(1024)}, f32[768]{0:T(1024)}) custom-call(s32[4]{0:T(128)S(1)} %pad_add_fusion.place_ref, f32[192,128]{1,0:T(8,128)S(1)} %pad_maximum_fusion.1.small_in, ...), custom_call_target="tpu_custom_call" | custom-call | tf_op jit(solution)/shard_map/finish/pallas_call | solution.py:471
  (37 shorter events, 0.4 us)
Async XLA Ops:
  7.2 17.7 %copy-start.8 = (bf16[7,7,768]{2,1,0:T(8,128)(2,1)S(1)}, bf16[7,7,768]{2,1,0:T(8,128)(2,1)}, u32[]{:S(2)}) copy-start(bf16[7,7,768]{2,1,0:T(8,128)(2,1)} %param.14) | copy-start | bytes 225796
  7.2 17.7 %copy-start.2 = (bf16[1,14,14,768]{3,2,1,0:T(8,128)(2,1)S(1)}, bf16[1,14,14,768]{3,2,1,0:T(8,128)(2,1)}, u32[]{:S(2)}) copy-start(bf16[1,14,14,768]{3,2,1,0:T(8,128)(2,1)} %param.10) | copy-start | bytes 903172
  7.2 29.7 %copy-start.9 = (f32[768]{0:T(1024)S(1)}, f32[768]{0:T(1024)}, u32[]{:S(2)}) copy-start(f32[768]{0:T(1024)} %param.19) | copy-start | bytes 9220
  7.2 52.6 %all-gather.2.cloned.1.call-start = ((), (), s32[]{:S(2)}) async-start(), calls=%async_computation.5 | async-start | bytes 3096576 | tf_op jit(solution)/shard_map/all_gather | solution.py:541
  10.3 114.9 %reduce-scatter.2.cloned.1.call-start = ((), (), s32[]{:S(2)}) async-start(), calls=%async_computation.6 | async-start | bytes 2949120 | tf_op jit(solution)/shard_map/reduce_scatter | solution.py:556
  14.0 45.8 %copy-start = (bf16[14,16,768]{2,1,0:T(8,128)(2,1)}, bf16[14,16,768]{2,1,0:T(8,128)(2,1)S(1)}, u32[]{:S(2)}) copy-start(bf16[14,16,768]{2,1,0:T(8,128)(2,1)S(1)} %pad.4) | copy-start | bytes 1032196
  14.0 20.9 %collective-permute-start.5 = (bf16[224,768]{1,0:T(8,128)(2,1)S(1)}, bf16[224,768]{1,0:T(8,128)(2,1)S(1)}, u32[]{:S(2)}, u32[]{:S(2)}) collective-permute-start(bf16[224,768]{1,0:T(8,128)(2,1)S(1)} %bitcast.24), channel_id=1, source_target_pairs={{0,40},{8,0},{32,8},{40,32},{1,41},{9,1},{33,9},{41,33},{2,42},{10... | collective-permute-start | bytes 1032200 | tf_op jit(solution)/shard_map/ppermute | solution.py:526
  19.2 17.7 %collective-permute-start.4 = (bf16[224,768]{1,0:T(8,128)(2,1)S(1)}, bf16[224,768]{1,0:T(8,128)(2,1)S(1)}, u32[]{:S(2)}, u32[]{:S(2)}) collective-permute-start(bf16[224,768]{1,0:T(8,128)(2,1)S(1)} %bitcast.25), channel_id=1, source_target_pairs={{0,32},{8,40},{32,0},{40,8},{1,33},{9,41},{33,1},{41,9},{2,34},{10... | collective-permute-start | bytes 1032200 | tf_op jit(solution)/shard_map/ppermute | solution.py:526
  21.7 16.7 %collective-permute-start.3 = (bf16[224,768]{1,0:T(8,128)(2,1)S(1)}, bf16[224,768]{1,0:T(8,128)(2,1)S(1)}, u32[]{:S(2)}, u32[]{:S(2)}) collective-permute-start(bf16[224,768]{1,0:T(8,128)(2,1)S(1)} %bitcast.26), channel_id=1, source_target_pairs={{0,8},{8,32},{32,40},{40,0},{1,9},{9,33},{33,41},{41,1},{2,10},{10... | collective-permute-start | bytes 1032200 | tf_op jit(solution)/shard_map/ppermute | solution.py:526
  27.8 11.6 %collective-permute-start.2 = (bf16[224,768]{1,0:T(8,128)(2,1)S(1)}, bf16[224,768]{1,0:T(8,128)(2,1)S(1)}, u32[]{:S(2)}, u32[]{:S(2)}) collective-permute-start(bf16[224,768]{1,0:T(8,128)(2,1)S(1)} %get-tuple-element.28.refs_0_), channel_id=1, source_target_pairs={{0,40},{8,0},{32,8},{40,32},{1,41},{9,1},{33,9},{41,33},{2,42},{10... | collective-permute-start | bytes 1032200 | tf_op jit(solution)/shard_map/ppermute | solution.py:526
  31.7 12.4 %collective-permute-start.1 = (bf16[224,768]{1,0:T(8,128)(2,1)S(1)}, bf16[224,768]{1,0:T(8,128)(2,1)S(1)}, u32[]{:S(2)}, u32[]{:S(2)}) collective-permute-start(bf16[224,768]{1,0:T(8,128)(2,1)S(1)} %get-tuple-element.28.refs_0_), channel_id=1, source_target_pairs={{0,32},{8,40},{32,0},{40,8},{1,33},{9,41},{33,1},{41,9},{2,34},{10... | collective-permute-start | bytes 1032200 | tf_op jit(solution)/shard_map/ppermute | solution.py:526
  34.9 24.9 %copy-start.3 = (bf16[224,768]{1,0:T(8,128)(2,1)}, bf16[224,768]{1,0:T(8,128)(2,1)S(1)}, u32[]{:S(2)}) copy-start(bf16[224,768]{1,0:T(8,128)(2,1)S(1)} %collective-permute-done.5.refs_7_) | copy-start | bytes 1032196
  34.9 18.7 %collective-permute-start = (bf16[224,768]{1,0:T(8,128)(2,1)S(1)}, bf16[224,768]{1,0:T(8,128)(2,1)}, u32[]{:S(2)}, u32[]{:S(2)}) collective-permute-start(bf16[224,768]{1,0:T(8,128)(2,1)S(1)} %get-tuple-element.28.refs_0_), channel_id=1, source_target_pairs={{0,8},{8,32},{32,40},{40,0},{1,9},{9,33},{33,41},{41,1},{2,10},{10... | collective-permute-start | bytes 1032200 | tf_op jit(solution)/shard_map/ppermute | solution.py:526
  36.9 22.9 %copy-start.4 = (bf16[224,768]{1,0:T(8,128)(2,1)}, bf16[224,768]{1,0:T(8,128)(2,1)S(1)}, u32[]{:S(2)}) copy-start(bf16[224,768]{1,0:T(8,128)(2,1)S(1)} %collective-permute-done.4.refs_6_) | copy-start | bytes 1032196
  38.3 21.4 %copy-start.5 = (bf16[224,768]{1,0:T(8,128)(2,1)}, bf16[224,768]{1,0:T(8,128)(2,1)S(1)}, u32[]{:S(2)}) copy-start(bf16[224,768]{1,0:T(8,128)(2,1)S(1)} %collective-permute-done.3.refs_5_) | copy-start | bytes 1032196
  39.4 4.8 %copy-start.6 = (bf16[224,768]{1,0:T(8,128)(2,1)}, bf16[224,768]{1,0:T(8,128)(2,1)S(1)}, u32[]{:S(2)}) copy-start(bf16[224,768]{1,0:T(8,128)(2,1)S(1)} %collective-permute-done.2.refs_3_) | copy-start | bytes 1032196
  44.2 0.7 copy-start.7
  72.6 9.5 %collective-permute-start.7 = (bf16[224,768]{1,0:T(8,128)(2,1)S(1)}, bf16[224,768]{1,0:T(8,128)(2,1)S(1)}, u32[]{:S(2)}, u32[]{:S(2)}) collective-permute-start(bf16[224,768]{1,0:T(8,128)(2,1)S(1)} %get-tuple-element.31), channel_id=1, source_target_pairs={{0,40},{8,0},{32,8},{40,32},{1,41},{9,1},{33,9},{41,33},{2,42},{10... | collective-permute-start | bytes 1032200 | tf_op jit(solution)/shard_map/ppermute | solution.py:526
  76.8 9.6 %collective-permute-start.8 = (bf16[224,768]{1,0:T(8,128)(2,1)S(1)}, bf16[224,768]{1,0:T(8,128)(2,1)S(1)}, u32[]{:S(2)}, u32[]{:S(2)}) collective-permute-start(bf16[224,768]{1,0:T(8,128)(2,1)S(1)} %get-tuple-element.32), channel_id=1, source_target_pairs={{0,32},{8,40},{32,0},{40,8},{1,33},{9,41},{33,1},{41,9},{2,34},{10... | collective-permute-start | bytes 1032200 | tf_op jit(solution)/shard_map/ppermute | solution.py:526
  79.4 16.6 %collective-permute-start.9 = (bf16[224,768]{1,0:T(8,128)(2,1)S(1)}, bf16[224,768]{1,0:T(8,128)(2,1)S(1)}, u32[]{:S(2)}, u32[]{:S(2)}) collective-permute-start(bf16[224,768]{1,0:T(8,128)(2,1)S(1)} %get-tuple-element.33), channel_id=1, source_target_pairs={{0,8},{8,32},{32,40},{40,0},{1,9},{9,33},{33,41},{41,1},{2,10},{10... | collective-permute-start | bytes 1032200 | tf_op jit(solution)/shard_map/ppermute | solution.py:526
  100.8 11.6 %all-to-all-start = ((f32[8,48,128]{2,1,0:T(8,128)}), f32[8,48,128]{2,1,0:T(8,128)S(1)}, u32[]{:S(2)}, u32[]{:S(2)}) async-start(f32[8,48,128]{2,1,0:T(8,128)} %bitcast.15), calls=%async_computation.1 | async-start | bytes 393216 | tf_op jit(solution)/shard_map/all_to_all | solution.py:561
  112.5 48.6 %copy-start.1 = (bf16[14,16,768]{2,1,0:T(8,128)(2,1)S(1)}, bf16[14,16,768]{2,1,0:T(8,128)(2,1)}, u32[]{:S(2)}) copy-start(bf16[14,16,768]{2,1,0:T(8,128)(2,1)} %copy-done) | copy-start | bytes 1032196
  113.2 11.9 %all-to-all-start.1 = ((bf16[8,48,128]{2,1,0:T(8,128)(2,1)}), bf16[8,48,128]{2,1,0:T(8,128)(2,1)S(1)}, u32[]{:S(2)}, u32[]{:S(2)}) async-start(bf16[8,48,128]{2,1,0:T(8,128)(2,1)} %broadcast_in_dim.14), calls=%async_computation.2 | async-start | bytes 196608 | tf_op jit(solution)/shard_map/all_to_all | solution.py:503
  126.2 4.4 %collective-permute-start.6 = (bf16[8,80,128]{2,1,0:T(8,128)(2,1)S(1)}, bf16[8,80,128]{2,1,0:T(8,128)(2,1)S(1)}, u32[]{:S(2)}, u32[]{:S(2)}) collective-permute-start(bf16[8,80,128]{2,1,0:T(8,128)(2,1)S(1)} %bitcast.36), channel_id=1, source_target_pairs={{0,16},{16,0},{1,17},{17,1},{2,18},{18,2},{3,19},{19,3},{4,20},{20... | collective-permute-start | bytes 491528 | tf_op jit(solution)/shard_map/ppermute | solution.py:507
  149.0 15.8 %all-to-all-start.3 = ((bf16[16,80,128]{2,1,0:T(8,128)(2,1)}), bf16[16,80,128]{2,1,0:T(8,128)(2,1)S(1)}, u32[]{:S(2)}, u32[]{:S(2)}) async-start(bf16[16,80,128]{2,1,0:T(8,128)(2,1)} %broadcast_in_dim.16), calls=%async_computation.4 | async-start | bytes 655360 | tf_op jit(solution)/shard_map/all_to_all | solution.py:503
  152.7 6.5 %collective-permute-start.10 = (f32[48,128]{1,0:T(8,128)S(1)}, f32[48,128]{1,0:T(8,128)S(1)}, u32[]{:S(2)}, u32[]{:S(2)}) collective-permute-start(f32[48,128]{1,0:T(8,128)S(1)} %add_select_fusion), channel_id=1, source_target_pairs={{0,32},{32,0},{1,33},{33,1},{2,34},{34,2},{3,35},{35,3},{4,36},{36... | collective-permute-start | bytes 73736 | tf_op jit(solution)/shard_map/ppermute | solution.py:507
  159.2 5.1 %collective-permute-start.11 = (f32[96,128]{1,0:T(8,128)S(1)}, f32[96,128]{1,0:T(8,128)S(1)}, u32[]{:S(2)}, u32[]{:S(2)}) collective-permute-start(f32[96,128]{1,0:T(8,128)S(1)} %pad_maximum_fusion.2), channel_id=1, source_target_pairs={{0,8},{8,0},{1,9},{9,1},{2,10},{10,2},{3,11},{11,3},{4,12},{12,4},... | collective-permute-start | bytes 147464 | tf_op jit(solution)/shard_map/ppermute | solution.py:507
  164.8 8.8 %collective-permute-start.13 = (bf16[8,2,80,128]{3,2,1,0:T(8,128)(2,1)S(1)}, bf16[8,2,80,128]{3,2,1,0:T(8,128)(2,1)S(1)}, u32[]{:S(2)}, u32[]{:S(2)}) collective-permute-start(bf16[8,2,80,128]{3,2,1,0:T(8,128)(2,1)S(1)} %bitcast.31), channel_id=1, source_target_pairs={{0,16},{16,0},{1,17},{17,1},{2,18},{18,2},{3,19},{19,3},{4,20},{20... | collective-permute-start | bytes 983048 | tf_op jit(solution)/shard_map/ppermute | solution.py:507
  170.4 3.2 %collective-permute-start.12 = (f32[192,128]{1,0:T(8,128)S(1)}, f32[192,128]{1,0:T(8,128)S(1)}, u32[]{:S(2)}, u32[]{:S(2)}) collective-permute-start(f32[192,128]{1,0:T(8,128)S(1)} %pad_maximum_fusion.1.small_in), channel_id=1, source_target_pairs={{0,16},{16,0},{1,17},{17,1},{2,18},{18,2},{3,19},{19,3},{4,20},{20... | collective-permute-start | bytes 294920 | tf_op jit(solution)/shard_map/ppermute | solution.py:507
Sparse Core Ops, SparseCore 0:
  10.4 49.2 all-gather.1
  72.7 44.3 reduce-scatter.1
